TPU v7x, 32 devices: a whole 2x2x4 slice. The times are simulated.
32 devices in a mesh: rep: 2 (over x), grp: 8 (over z, y), loc: 2 (over core).
Axes of the slice: x: 2, y: 2, z: 4, core: 2. Of those that a mesh axis runs over, the one named last changes fastest.
Arguments:
- tokens: bfloat16 [4096, 2048], P(('rep', 'grp', 'loc')), parts along dimension 0, may hold values from -6 to 6
- cotangent: bfloat16 [4096, 2048], P(('rep', 'grp', 'loc')), parts along dimension 0, may hold values from -4 to 4
- expert_ids: int32 [4096, 8], P(('rep', 'grp', 'loc')), parts along dimension 0, may hold values from 0 to 31, as said below
- route_weights: bfloat16 [4096, 8], P(('rep', 'grp', 'loc')), parts along dimension 0, may hold values from 0.049804688 to 0.5
- gate_weight: bfloat16 [32, 2048, 384], P(('grp', 'loc')), may hold values from -0.125 to 0.125
- up_weight: bfloat16 [32, 2048, 384], P(('grp', 'loc')), may hold values from -0.125 to 0.125
- down_weight: bfloat16 [32, 384, 2048], P(('grp', 'loc')), may hold values from -0.3125 to 0.3125
Outputs:
- grad_tokens: bfloat16 [4096, 2048], P(('rep', 'grp', 'loc')), parts along dimension 0
- grad_weights: bfloat16 [4096, 8], P(('rep', 'grp', 'loc')), parts along dimension 0
There are 2 independent parts, one for each index of `rep`. A program takes and returns all parts, laid end to end along the dimension named above; an argument that names none is the same for every part. Nothing has to cross between parts.
Inputs may be any that keep to these rules, and one draw needn't show every extreme that they name: `expert_ids`: each row names 8 distinct experts, two in each of exactly 4 groups (group = id // 4). In each device's aligned block of 128 rows at most 96 rows name any one group, and some groups reach 96 in every block; every expert of a group is named by exactly half of the block's rows that name the group. In all, at most 768 rows name any one expert, and some experts reach it.
All inputs are finite; a program needn't handle non-finite values.
Results may differ from a plain program's by a relative error of at most 0.009.
Values may be sent and summed in bfloat16 or wider, within the bound.
No kernel may reach another device: no remote copies, remote signals or barrier semaphores. Data moves between devices by JAX's collectives and lax.ppermute only.
A program may use at most 128 MiB of HBM per device.

v0:
```python
import functools

import jax
import jax.numpy as jnp
from jax import lax
from jax.experimental import pallas as pl
from jax.experimental.pallas import tpu as pltpu
from jax.sharding import PartitionSpec as P

TOP = 8
TOP_GROUPS = 4


def shortened(shard):
    return jax.tree.map(lambda a: a.astype(jnp.bfloat16) if a.dtype == jnp.float32 else a, shard)


def take_rows(values, indices, filler):
    return jnp.take(values, indices, axis=0, mode="fill", fill_value=filler)


def route_table(targets, dest_total, capacity):
    token_total = targets.shape[0]
    dest_iota = jnp.arange(dest_total, dtype=jnp.int32)
    reached = jnp.any(targets[:, :, None] == dest_iota[None, None, :], axis=1)
    ranked = jnp.cumsum(reached.astype(jnp.int32), axis=0) - 1
    slot_of = jnp.where(reached, ranked, capacity)
    dest_grid = jnp.broadcast_to(dest_iota[None, :], slot_of.shape)
    token_grid = jnp.broadcast_to(jnp.arange(token_total, dtype=jnp.int32)[:, None], slot_of.shape)
    sources = jnp.full((dest_total, capacity), token_total, jnp.int32)
    sources = sources.at[dest_grid, slot_of].set(token_grid, mode="drop")
    return (slot_of, sources)


def token_groups(group_ids, group_total):
    token_total = group_ids.shape[0]
    group_iota = jnp.arange(group_total, dtype=jnp.int32)
    reached = jnp.any(group_ids[:, :, None] == group_iota[None, None, :], axis=1)
    ranked = jnp.cumsum(reached.astype(jnp.int32), axis=1) - 1
    column = jnp.where(reached, ranked, TOP_GROUPS)
    token_grid = jnp.broadcast_to(jnp.arange(token_total, dtype=jnp.int32)[:, None], column.shape)
    listed = jnp.full((token_total, TOP_GROUPS), group_total, jnp.int32)
    return listed.at[token_grid, column].set(
        jnp.broadcast_to(group_iota[None, :], column.shape), mode="drop"
    )


def expert_pass(
    token_rows,
    grad_rows,
    id_rows,
    weight_rows,
    gate_weight,
    up_weight,
    down_weight,
    first_expert,
    capacity,
):
    row_total = token_rows.shape[0]
    local_total = gate_weight.shape[0]
    model_width = token_rows.shape[1]
    experts_here = first_expert + jnp.arange(local_total, dtype=jnp.int32)
    matched = id_rows[None, :, :] == experts_here[:, None, None]
    chosen = jnp.any(matched, axis=2)
    weight_of = jnp.sum(
        jnp.where(matched, weight_rows.astype(jnp.float32)[None, :, :], 0.0), axis=2
    )
    ranked = jnp.cumsum(chosen.astype(jnp.int32), axis=1) - 1
    slot_of = jnp.where(chosen, ranked, capacity)
    expert_grid = jnp.broadcast_to(jnp.arange(local_total, dtype=jnp.int32)[:, None], slot_of.shape)
    row_grid = jnp.broadcast_to(jnp.arange(row_total, dtype=jnp.int32)[None, :], slot_of.shape)
    picks = (
        jnp.full((local_total, capacity), row_total, jnp.int32)
        .at[expert_grid, slot_of]
        .set(row_grid, mode="drop")
    )
    buffer_x = take_rows(token_rows, picks, 0)
    buffer_g = take_rows(grad_rows, picks, 0)
    buffer_w = jnp.take_along_axis(weight_of, picks, axis=1, mode="fill", fill_value=0.0)
    gate_act = jnp.einsum("ecd,edf->ecf", buffer_x, gate_weight, preferred_element_type=jnp.float32)
    up_act = jnp.einsum("ecd,edf->ecf", buffer_x, up_weight, preferred_element_type=jnp.float32)
    back_grad = jnp.einsum(
        "ecd,efd->ecf", buffer_g, down_weight, preferred_element_type=jnp.float32
    )
    sigmoid_val = jax.nn.sigmoid(gate_act)
    silu_val = gate_act * sigmoid_val
    route_grad = jnp.sum(back_grad * silu_val * up_act, axis=2)
    hidden_grad = buffer_w[:, :, None] * back_grad
    gate_grad = (
        hidden_grad * up_act * sigmoid_val * (1.0 + gate_act * (1.0 - sigmoid_val))
    ).astype(jnp.bfloat16)
    up_grad = (hidden_grad * silu_val).astype(jnp.bfloat16)
    input_grad = jnp.einsum(
        "ecf,edf->ecd", gate_grad, gate_weight, preferred_element_type=jnp.float32
    )
    input_grad = input_grad + jnp.einsum(
        "ecf,edf->ecd", up_grad, up_weight, preferred_element_type=jnp.float32
    )
    partial_value = jnp.zeros((row_total, model_width), jnp.float32)
    partial_value = partial_value.at[picks.reshape(-1)].add(
        input_grad.reshape(-1, model_width), mode="drop"
    )
    cap_grid = jnp.broadcast_to(jnp.arange(local_total, dtype=jnp.int32)[:, None], picks.shape)
    route_per = (
        jnp.zeros((local_total, row_total), jnp.float32)
        .at[cap_grid, picks]
        .add(route_grad, mode="drop")
    )
    route_rows = jnp.sum(jnp.where(matched, route_per[:, :, None], 0.0), axis=0)
    return (partial_value, route_rows)


def routed_body(tokens, cotangent, expert_ids, route_weights, gate_weight, up_weight, down_weight):
    group_total = lax.axis_size("grp")
    loc_total = lax.axis_size("loc")
    token_total = tokens.shape[0]
    model_width = tokens.shape[1]
    per_device = gate_weight.shape[0]
    per_group = per_device * loc_total
    group_cap = 6 * token_total // group_total
    expert_cap = 3 * token_total * loc_total
    device_rank = lax.axis_index("grp") * loc_total + lax.axis_index("loc")
    first_expert = device_rank * per_device
    group_ids = expert_ids // per_group
    listed = token_groups(group_ids, group_total)
    slot_range = jnp.arange(TOP, dtype=jnp.int32)[None, :]
    slot_of, sources = route_table(group_ids, group_total, group_cap)
    send_x = take_rows(tokens, sources, 0)
    send_g = take_rows(cotangent, sources, 0)
    send_ids = take_rows(expert_ids, sources, -1)
    send_w = take_rows(route_weights, sources, 0)
    recv_x, recv_g, recv_ids, recv_w = (
        lax.all_to_all(send_x, "grp", split_axis=0, concat_axis=0, tiled=True),
        lax.all_to_all(send_g, "grp", split_axis=0, concat_axis=0, tiled=True),
        lax.all_to_all(send_ids, "grp", split_axis=0, concat_axis=0, tiled=True),
        lax.all_to_all(send_w, "grp", split_axis=0, concat_axis=0, tiled=True),
    )
    row_total = group_total * group_cap
    shared_x, shared_g, shared_ids, shared_w = (
        lax.all_gather(recv_x.reshape(row_total, model_width), "loc", axis=0, tiled=True),
        lax.all_gather(recv_g.reshape(row_total, model_width), "loc", axis=0, tiled=True),
        lax.all_gather(shortened(recv_ids.reshape(row_total, TOP)), "loc", axis=0, tiled=True),
        lax.all_gather(recv_w.reshape(row_total, TOP), "loc", axis=0, tiled=True),
    )
    partial_value, route_rows = expert_pass(
        shared_x,
        shared_g,
        shared_ids,
        shared_w,
        gate_weight,
        up_weight,
        down_weight,
        first_expert,
        expert_cap,
    )
    summed, route_sum = (
        lax.psum_scatter(partial_value, "loc", scatter_dimension=0, tiled=True),
        lax.psum_scatter(route_rows, "loc", scatter_dimension=0, tiled=True),
    )
    group_part = summed.astype(jnp.bfloat16).reshape(group_total, group_cap, model_width)
    route_part = route_sum.astype(jnp.bfloat16).reshape(group_total, group_cap, TOP)
    back_terms, back_route = (
        lax.all_to_all(group_part, "grp", split_axis=0, concat_axis=0, tiled=True),
        lax.all_to_all(route_part, "grp", split_axis=0, concat_axis=0, tiled=True),
    )
    slot_pad = jnp.concatenate([slot_of, jnp.full((token_total, 1), group_cap, jnp.int32)], axis=1)
    found = jnp.take_along_axis(slot_pad, listed, axis=1)
    position = jnp.where(found < group_cap, listed * group_cap + found, row_total)
    pieces = take_rows(back_terms.reshape(row_total, model_width), position, 0)
    grad_tokens = jnp.sum(pieces.astype(jnp.float32), axis=1).astype(jnp.bfloat16)
    slot_found = jnp.take_along_axis(slot_of, group_ids, axis=1)
    route_index = (group_ids * group_cap + slot_found) * TOP + slot_range
    grad_weights = back_route.reshape(row_total * TOP)[route_index]
    return (grad_tokens, grad_weights)


LANES = 128
NT = (((1,), (1,)), ((), ()))
ANYWHERE = pl.BlockSpec(memory_space=pl.ANY)
IN_VMEM = pl.BlockSpec(memory_space=pltpu.VMEM)
IN_SMEM = pl.BlockSpec(memory_space=pltpu.SMEM)
MIB = 1024 * 1024
TOKEN = jax.ShapeDtypeStruct((8, LANES), jnp.float32)


def pack_kernel(tokens, cotangent, ids, weights, block, ids_here, weights_here, sems):
    rows, width = tokens.shape
    small = (
        pltpu.make_async_copy(ids, ids_here, sems.at[0]),
        pltpu.make_async_copy(weights, weights_here, sems.at[1]),
    )
    large = (
        pltpu.make_async_copy(tokens, block.at[:, pl.ds(0, width)], sems.at[2]),
        pltpu.make_async_copy(cotangent, block.at[:, pl.ds(width, width)], sems.at[3]),
    )
    for copy in small + large:
        copy.start()
    for copy in small:
        copy.wait()
    expert = lax.broadcasted_iota(jnp.int32, (LANES, rows), 0)
    table = jnp.zeros((LANES, rows), jnp.float32)
    for k in range(ids.shape[0]):
        chosen = expert == ids_here[k : k + 1, :]
        table += jnp.where(chosen, weights_here[k : k + 1, :].astype(jnp.float32), 0.0)
    block[:, 2 * width :] = table.T.astype(jnp.bfloat16)
    for copy in large:
        copy.wait()


def pack(tokens, cotangent, ids, weights):
    rows, width = tokens.shape
    return pl.pallas_call(
        pack_kernel,
        out_shape=pltpu.VMEM((rows, 2 * width + LANES), jnp.bfloat16),
        in_specs=[ANYWHERE] * 4,
        out_specs=IN_VMEM,
        scratch_shapes=[
            pltpu.VMEM((ids.shape[1], rows), jnp.int32),
            pltpu.VMEM((ids.shape[1], rows), jnp.bfloat16),
            pltpu.SemaphoreType.DMA((4,)),
        ],
        compiler_params=pltpu.CompilerParams(vmem_limit_bytes=8 * MIB),
    )(*(in_hbm(a) for a in (tokens, cotangent, ids.T, weights.T)))


def in_hbm(a):
    return pltpu.with_memory_space_constraint(a, pltpu.HBM)


def in_vmem(a):
    return pltpu.with_memory_space_constraint(a, pltpu.VMEM)


def load_kernel(after_this, gate, up, down, gate_up, back, down_back, token, down_here, sems):
    del after_this
    token[...] = jnp.zeros_like(token)
    per_device, hidden = gate.shape[0], gate.shape[2]
    copies = []
    for e in range(per_device):
        copies.append(
            (
                pltpu.make_async_copy(down.at[e], down_here.at[e], sems.at[2, e]),
                pltpu.make_async_copy(gate.at[e], gate_up.at[e, :, pl.ds(0, hidden)], sems.at[0, e]),
                pltpu.make_async_copy(up.at[e], gate_up.at[e, :, pl.ds(hidden, hidden)], sems.at[1, e]),
            )
        )
    for three in copies:
        for copy in three:
            copy.start()
    for e, (first, second, third) in enumerate(copies):
        first.wait()
        down_back[:, e * hidden : (e + 1) * hidden] = down_here[e].T
        second.wait()
        third.wait()
        back[2 * e * hidden : 2 * (e + 1) * hidden, :] = gate_up[e].T


def load(after_this, gate, up, down):
    per_device, width, hidden = gate.shape
    return pl.pallas_call(
        load_kernel,
        out_shape=(
            pltpu.VMEM((per_device, width, 2 * hidden), jnp.bfloat16),
            pltpu.VMEM((2 * per_device * hidden, width), jnp.bfloat16),
            pltpu.VMEM((width, per_device * hidden), jnp.bfloat16),
            TOKEN,
        ),
        in_specs=[ANYWHERE] * 4,
        out_specs=(IN_VMEM,) * 4,
        scratch_shapes=[pltpu.VMEM(down.shape, jnp.bfloat16), pltpu.SemaphoreType.DMA((3, per_device))],
        compiler_params=pltpu.CompilerParams(vmem_limit_bytes=8 * MIB),
        cost_estimate=pl.CostEstimate(flops=1, bytes_accessed=24 * MIB, transcendentals=0),
    )(after_this, gate, up, down)


def experts_kernel(pieces, place, after_this, *refs):
    del after_this
    packed, refs = refs[:pieces], refs[pieces:]
    loaded, refs = (refs[:3], refs[3:6]), refs[6:]
    outs, token = refs[:pieces], refs[pieces]
    token[...] = jnp.zeros_like(token)
    per_device, width, both_hidden = loaded[0][0].shape
    hidden = both_hidden // 2
    x = jnp.concatenate([a[:, :width] for a in packed], axis=0)
    g = jnp.concatenate([a[:, width : 2 * width] for a in packed], axis=0)
    table = jnp.concatenate([a[:, 2 * width :] for a in packed], axis=0).astype(jnp.float32)
    lane = lax.broadcasted_iota(jnp.int32, table.shape, 1)
    route = jnp.zeros(table.shape, jnp.float32)
    grads = []
    for pair, (gate_up, _, down_back) in enumerate(loaded):
        backs = jnp.dot(g, down_back[...], preferred_element_type=jnp.float32)
        mine = []
        for at in range(per_device):
            back = backs[:, at * hidden : (at + 1) * hidden]
            column = place[0] + lax.rem(place[1] + pair * per_device + at, 2 * per_device)
            weight = jnp.sum(jnp.where(lane == column, table, 0.0), axis=1, keepdims=True)
            both = jnp.dot(x, gate_up[at], preferred_element_type=jnp.float32)
            gate_act, up_act = both[:, :hidden], both[:, hidden:]
            sig = jax.nn.sigmoid(gate_act)
            silu = gate_act * sig
            back_up = back * up_act
            route_grad = jnp.sum(back_up * silu, axis=1, keepdims=True)
            mine.append((weight * back_up * sig * (1.0 + gate_act * (1.0 - sig))).astype(jnp.bfloat16))
            mine.append((weight * back * silu).astype(jnp.bfloat16))
            route += jnp.where(lane == column, route_grad, 0.0)
        grads.append(jnp.concatenate(mine, axis=1))
    step = 4 * LANES

    def chunk(i, carry):
        part = pl.ds(pl.multiple_of(i * step, step), step)
        total = sum(
            jnp.dot(a, back[:, part], preferred_element_type=jnp.float32) for a, (_, back, _) in zip(grads, loaded)
        ).astype(jnp.bfloat16)
        start = 0
        for out in outs:
            out[:, part] = total[start : start + out.shape[0]]
            start += out.shape[0]
        return carry

    lax.fori_loop(0, width // step, chunk, 0)
    start = 0
    for out in outs:
        out[:, width:] = route[start : start + out.shape[0]].astype(out.dtype)
        start += out.shape[0]


def experts_call(place, after_this, packed, loaded):
    width = loaded[0].shape[1]
    return pl.pallas_call(
        functools.partial(experts_kernel, len(packed)),
        out_shape=[jax.ShapeDtypeStruct((a.shape[0], width + LANES), jnp.bfloat16) for a in packed] + [TOKEN],
        in_specs=[IN_SMEM, ANYWHERE] + [IN_VMEM] * (len(packed) + 6),
        out_specs=[IN_VMEM] * (len(packed) + 1),
        compiler_params=pltpu.CompilerParams(vmem_limit_bytes=12 * MIB),
        cost_estimate=pl.CostEstimate(flops=1, bytes_accessed=1, transcendentals=0),
    )(place, after_this, *(in_vmem(a) for a in packed), *loaded)


def finish_kernel(ids, mine, top0, top1, low0, low1, grad_tokens, grad_weights):
    rows, width = grad_tokens.shape
    cut = rows // 2
    routes = []
    for start, terms in ((0, (top0, top1)), (cut, (low0, low1))):
        summed = mine[start : start + cut, :].astype(jnp.float32)
        for term in terms:
            summed += term[...].astype(jnp.float32)
        grad_tokens[start : start + cut, :] = summed[:, :width].astype(grad_tokens.dtype)
        routes.append(summed[:, width:])
    route = jnp.concatenate(routes, axis=0).T
    expert = lax.broadcasted_iota(jnp.int32, route.shape, 0)
    found = [
        jnp.sum(jnp.where(expert == ids[k : k + 1, :], route, 0.0), axis=0, keepdims=True) for k in range(ids.shape[0])
    ]
    grad_weights[...] = jnp.concatenate(found, axis=0).astype(grad_weights.dtype)


def finish(ids, terms, width):
    rows, top = ids.shape
    grad_tokens, grad_weights = pl.pallas_call(
        finish_kernel,
        out_shape=(
            jax.ShapeDtypeStruct((rows, width), jnp.bfloat16),
            jax.ShapeDtypeStruct((top, rows), jnp.bfloat16),
        ),
        in_specs=[IN_VMEM] * 6,
        out_specs=(IN_VMEM, IN_VMEM),
        compiler_params=pltpu.CompilerParams(vmem_limit_bytes=12 * MIB),
    )(ids.T, *terms)
    return grad_tokens, grad_weights.T


def add_kernel(a, b, out):
    out[...] = (a[...].astype(jnp.float32) + b[...].astype(jnp.float32)).astype(out.dtype)


def added(a, b):
    return pl.pallas_call(
        add_kernel,
        out_shape=jax.ShapeDtypeStruct(a.shape, a.dtype),
        in_specs=[IN_VMEM] * 2,
        out_specs=IN_VMEM,
        compiler_params=pltpu.CompilerParams(vmem_limit_bytes=8 * MIB),
        cost_estimate=pl.CostEstimate(flops=1, bytes_accessed=1, transcendentals=0),
    )(a, b)


def ring_body(tokens, cotangent, expert_ids, route_weights, gate_weight, up_weight, down_weight):
    ring_total = lax.axis_size("grp")
    loc_total = lax.axis_size("loc")
    width = tokens.shape[1]
    per_device = gate_weight.shape[0]
    order = list(range(0, ring_total, 2)) + list(range(ring_total - 1, 0, -2))
    ahead = [(order[i], order[(i + 1) % ring_total]) for i in range(ring_total)]
    behind = [(b, a) for a, b in ahead]
    rank, loc = lax.axis_index("grp"), lax.axis_index("loc")

    def send(pair):
        return lax.ppermute(pair[0], "grp", ahead), lax.ppermute(pair[1], "grp", behind)

    def send_back(pair):
        return lax.ppermute(pair[0], "grp", behind), lax.ppermute(pair[1], "grp", ahead)

    def tie(pair, *others):
        return tuple(lax.optimization_barrier((a, *others))[0] for a in pair)

    own = (gate_weight, up_weight, down_weight)
    other = [lax.ppermute(a, "loc", [(i, loc_total - 1 - i) for i in range(loc_total)]) for a in own]
    block = pack(tokens, cotangent, expert_ids, route_weights)
    came = send((block, block))
    place = jnp.stack([rank * (loc_total * per_device), loc * per_device]).astype(jnp.int32)
    *loaded, loaded_own = load(place, *(in_hbm(a) for a in own))
    *others, last = load(loaded_own, *tie(other[:2], *came), other[2])
    loaded += others

    def call(after_this, *packed):
        *parts, token = experts_call(place, after_this, packed, loaded)
        return parts, token

    half, cut = ring_total // 2, block.shape[0] // 2

    def split(pair):
        return (pair[0][:cut], pair[1][cut:]), (pair[0][cut:], pair[1][:cut])

    long, short = split(came)
    long_next, short_next = send(tie(long, loaded_own, *other)), send(tie(short, loaded_own, *other))
    (mine,), last = call(last, block)
    filler = last
    parts, last = call(last, *came)
    ahead_terms, behind_terms = split(parts)
    long_terms, short_terms = [None, ahead_terms], [None, behind_terms]
    for s in range(2, half - 1):
        long, short = long_next, short_next
        long_next = send(tie(long, filler))
        short_next = send(tie(short, last))
        parts, last = call(last, long[0], short[0], long[1], short[1])
        long_terms.append((parts[0], parts[2]))
        short_terms.append((parts[1], parts[3]))
    long, short = long_next, short_next
    long_last = send(tie(long, last))
    parts, last = call(last, *long)
    long_terms.append(tuple(parts))
    parts, last = call(last, *short)
    short_back = send_back(parts)
    parts, last = call(last, *long_last)
    long_back = send_back(tie(parts, *short_back))
    for s in range(half - 1, 0, -1):
        if s < half - 1:
            short_back = send_back([added(a, b) for a, b in zip(short_terms[s], short_back)])
        long_back = send_back([added(a, b) for a, b in zip(long_terms[s], long_back)])
    return finish(expert_ids, (mine, long_back[0], short_back[1], short_back[0], long_back[1]), width)


def body(tokens, cotangent, expert_ids, route_weights, gate_weight, up_weight, down_weight):
    args = (tokens, cotangent, expert_ids, route_weights, gate_weight, up_weight, down_weight)
    ring_total, loc_total = lax.axis_size("grp"), lax.axis_size("loc")
    experts = ring_total * loc_total * gate_weight.shape[0]
    if loc_total == 2 and ring_total in (6, 8) and experts <= LANES and tokens.shape[0] % 32 == 0:
        return ring_body(*args)
    return routed_body(*args)


def solution(mesh):
    placed = (
        P(("rep", "grp", "loc"), None),
        P(("rep", "grp", "loc"), None),
        P(("rep", "grp", "loc"), None),
        P(("rep", "grp", "loc"), None),
        P(("grp", "loc"), None, None),
        P(("grp", "loc"), None, None),
        P(("grp", "loc"), None, None),
    )
    return jax.shard_map(
        body,
        mesh=mesh,
        in_specs=placed,
        out_specs=(P(("rep", "grp", "loc"), None), P(("rep", "grp", "loc"), None)),
        check_vma=False,
    )
```

profile of v0, /device:TPU:0, one launch (start us, length us, event | category | flops | bytes accessed | tf_op | source)
XLA Modules:
  0.0 137.6 jit_solution(6080322466764853962)
XLA Ops:
  0.6 0.5 collective-permute-start
  1.1 0.1 collective-permute-start.3
  1.2 0.4 collective-permute-start.4
  1.7 1.3 shard_map.87.refs_0_
  2.9 2.7 %collective-permute-start.1 = (bf16[128,4224]{1,0:T(8,128)(2,1)S(1)}, bf16[128,4224]{1,0:T(8,128)(2,1)S(1)}, u32[]{:S(2)}, u32[]{:S(2)}) collective-permute-start(bf16[128,4224]{1,0:T(8,128)(2,1)S(1)} %shard_map.87.refs_0_), channel_id=1, source_target_pairs={{0,4},{4,8},{8,12},{12,14},{14,10},{10,6},{6,2},{2,0},{1,5},{5,9},... | collective-permute-start | bytes 3244040 | tf_op jit(solution)/shard_map/ppermute | solution.py:398
  5.7 4.7 %shard_map.86 = (bf16[2,2048,768]{2,1,0:T(8,128)(2,1)S(1)}, bf16[1536,2048]{1,0:T(8,128)(2,1)S(1)}, bf16[2048,768]{1,0:T(8,128)(2,1)S(1)}, f32[8,128]{1,0:T(8,128)S(1)}) custom-call(s32[2]{0:T(128)S(1)} %pad_add_fusion.after_this.place, bf16[2,2048,384]{2,1,0:T(8,128)(2,1)} %gate.1, bf16[2,2048,384]{2,1,0:T(8,128)(2,1)} %up.1, bf16[2,384,2048]{2,1,0:T(8,128)(2,1)} %down.1), custom_call_target="tpu_custom_call" | custom-call | flops 1 | bytes 25165824 | tf_op jit(solution)/shard_map/pallas_call | solution.py:260
  10.5 19.6 %collective-permute-done.1.refs_0_ = bf16[128,4224]{1,0:T(8,128)(2,1)S(1)} collective-permute-done((bf16[128,4224]{1,0:T(8,128)(2,1)S(1)}, bf16[128,4224]{1,0:T(8,128)(2,1)S(1)}, u32[]{:S(2)}, u32[]{:S(2)}) %collective-permute-start.1) | collective-permute-done | bytes 1081376 | tf_op jit(solution)/shard_map/ppermute | solution.py:398
  30.2 1.9 %collective-permute-start.5 = (bf16[64,4224]{1,0:T(8,128)(2,1)S(1)}, bf16[64,4224]{1,0:T(8,128)(2,1)S(1)}, u32[]{:S(2)}, u32[]{:S(2)}) collective-permute-start(bf16[64,4224]{1,0:T(8,128)(2,1)S(1)} %get-tuple-element.58), channel_id=1, source_target_pairs={{0,4},{4,8},{8,12},{12,14},{14,10},{10,6},{6,2},{2,0},{1,5},{5,9},... | collective-permute-start | bytes 1622024 | tf_op jit(solution)/shard_map/ppermute | solution.py:398
  32.1 0.3 collective-permute-start.7
  32.4 1.8 %collective-permute-start.6 = (bf16[64,4224]{1,0:T(8,128)(2,1)S(1)}, bf16[64,4224]{1,0:T(8,128)(2,1)S(1)}, u32[]{:S(2)}, u32[]{:S(2)}) collective-permute-start(bf16[64,4224]{1,0:T(8,128)(2,1)S(1)} %get-tuple-element.59), channel_id=1, source_target_pairs={{0,4},{4,8},{8,12},{12,14},{14,10},{10,6},{6,2},{2,0},{1,5},{5,9},... | collective-permute-start | bytes 1622024 | tf_op jit(solution)/shard_map/ppermute | solution.py:398
  34.2 0.2 collective-permute-start.8
  34.4 4.9 %shard_map.88 = (bf16[2,2048,768]{2,1,0:T(8,128)(2,1)S(1)}, bf16[1536,2048]{1,0:T(8,128)(2,1)S(1)}, bf16[2048,768]{1,0:T(8,128)(2,1)S(1)}, f32[8,128]{1,0:T(8,128)S(1)}) custom-call(f32[8,128]{1,0:T(8,128)S(1)} %get-tuple-element.44.after_this, bf16[2,2048,384]{2,1,0:T(8,128)(2,1)} %collective-permute-done.gate, ...), custom_call_target="tpu_custom_call" | custom-call | flops 1 | bytes 25165824 | tf_op jit(solution)/shard_map/pallas_call | solution.py:260
  39.3 6.0 %shard_map.89 = (bf16[128,2176]{1,0:T(8,128)(2,1)S(1)}, f32[8,128]{1,0:T(8,128)S(1)}) custom-call(s32[2]{0:T(128)S(1)} %pad_add_fusion.after_this.place, f32[8,128]{1,0:T(8,128)S(1)} %get-tuple-element.47.after_this, bf16[128,4224]{1,0:T(8,128)(2,1)S(1)} %copy-done.3, bf16[2,2048,768]{2,1,0:T(8,128)(2,1)S(1)} %get-tuple-element.48.refs_1_.refs_2_.refs_4_, ...), custom_call_target="tpu_custom_call" | custom-call | flops 1 | bytes 1 | tf_op jit(solution)/shard_map/pallas_call | solution.py:329
  45.3 0.1 collective-permute-done.5.refs_0_
  45.4 1.8 %collective-permute-start.9 = (bf16[64,4224]{1,0:T(8,128)(2,1)S(1)}, bf16[64,4224]{1,0:T(8,128)(2,1)S(1)}, u32[]{:S(2)}, u32[]{:S(2)}) collective-permute-start(bf16[64,4224]{1,0:T(8,128)(2,1)S(1)} %collective-permute-done.5.refs_0_), channel_id=1, source_target_pairs={{0,4},{4,8},{8,12},{12,14},{14,10},{10,6},{6,2},{2,0},{1,5},{5,9},... | collective-permute-start | bytes 1622024 | tf_op jit(solution)/shard_map/ppermute | solution.py:398
  47.2 0.2 collective-permute-done.7.refs_2_
  47.4 0.2 collective-permute-start.10
  47.6 10.2 %shard_map.90 = (bf16[128,2176]{1,0:T(8,128)(2,1)S(1)}, bf16[128,2176]{1,0:T(8,128)(2,1)S(1)}, f32[8,128]{1,0:T(8,128)S(1)}) custom-call(s32[2]{0:T(128)S(1)} %pad_add_fusion.after_this.place, f32[8,128]{1,0:T(8,128)S(1)} %get-tuple-element.55.after_this, bf16[128,4224]{1,0:T(8,128)(2,1)S(1)} %copy-done.1, ...), custom_call_target="tpu_custom_call" | custom-call | flops 1 | bytes 1 | tf_op jit(solution)/shard_map/pallas_call | solution.py:329
  57.8 1.9 %collective-permute-start.11 = (bf16[64,4224]{1,0:T(8,128)(2,1)S(1)}, bf16[64,4224]{1,0:T(8,128)(2,1)S(1)}, u32[]{:S(2)}, u32[]{:S(2)}) collective-permute-start(bf16[64,4224]{1,0:T(8,128)(2,1)S(1)} %collective-permute-done.6.refs_1_), channel_id=1, source_target_pairs={{0,4},{4,8},{8,12},{12,14},{14,10},{10,6},{6,2},{2,0},{1,5},{5,9},... | collective-permute-start | bytes 1622024 | tf_op jit(solution)/shard_map/ppermute | solution.py:398
  59.6 0.2 collective-permute-start.12
  59.8 10.2 %shard_map.91 = (bf16[64,2176]{1,0:T(8,128)(2,1)S(1)}, bf16[64,2176]{1,0:T(8,128)(2,1)S(1)}, bf16[64,2176]{1,0:T(8,128)(2,1)S(1)}, bf16[64,2176]{1,0:T(8,128)(2,1)S(1)}, f32[8,128]{1,0:T(8,128)S(1)}) custom-call(s32[2]{0:T(128)S(1)} %pad_add_fusion.after_this.place, f32[8,128]{1,0:T(8,128)S(1)} %get-tuple-element.57.after_this, ...), custom_call_target="tpu_custom_call" | custom-call | flops 1 | bytes 1 | tf_op jit(solution)/shard_map/pallas_call | solution.py:329
  70.0 1.9 %collective-permute-start.13 = (bf16[64,4224]{1,0:T(8,128)(2,1)S(1)}, bf16[64,4224]{1,0:T(8,128)(2,1)S(1)}, u32[]{:S(2)}, u32[]{:S(2)}) collective-permute-start(bf16[64,4224]{1,0:T(8,128)(2,1)S(1)} %collective-permute-done.9.refs_0_), channel_id=1, source_target_pairs={{0,4},{4,8},{8,12},{12,14},{14,10},{10,6},{6,2},{2,0},{1,5},{5,9},... | collective-permute-start | bytes 1622024 | tf_op jit(solution)/shard_map/ppermute | solution.py:398
  71.9 0.2 collective-permute-start.14
  72.2 6.0 %shard_map.92 = (bf16[64,2176]{1,0:T(8,128)(2,1)S(1)}, bf16[64,2176]{1,0:T(8,128)(2,1)S(1)}, f32[8,128]{1,0:T(8,128)S(1)}) custom-call(s32[2]{0:T(128)S(1)} %pad_add_fusion.after_this.place, f32[8,128]{1,0:T(8,128)S(1)} %get-tuple-element.63.after_this, bf16[64,4224]{1,0:T(8,128)(2,1)S(1)} %collective-permute-done.9.refs_0_, ...), custom_call_target="tpu_custom_call" | custom-call | flops 1 | bytes 1 | tf_op jit(solution)/shard_map/pallas_call | solution.py:329
  78.2 1.9 %collective-permute-done.11.refs_0_ = bf16[64,4224]{1,0:T(8,128)(2,1)S(1)} collective-permute-done((bf16[64,4224]{1,0:T(8,128)(2,1)S(1)}, bf16[64,4224]{1,0:T(8,128)(2,1)S(1)}, u32[]{:S(2)}, u32[]{:S(2)}) %collective-permute-start.11) | collective-permute-done | bytes 540704 | tf_op jit(solution)/shard_map/ppermute | solution.py:398
  80.1 2.0 %collective-permute-done.12.refs_1_ = bf16[64,4224]{1,0:T(8,128)(2,1)S(1)} collective-permute-done((bf16[64,4224]{1,0:T(8,128)(2,1)S(1)}, bf16[64,4224]{1,0:T(8,128)(2,1)S(1)}, u32[]{:S(2)}, u32[]{:S(2)}) %collective-permute-start.12) | collective-permute-done | bytes 540704 | tf_op jit(solution)/shard_map/ppermute | solution.py:398
  82.1 6.0 %shard_map.93 = (bf16[64,2176]{1,0:T(8,128)(2,1)S(1)}, bf16[64,2176]{1,0:T(8,128)(2,1)S(1)}, f32[8,128]{1,0:T(8,128)S(1)}) custom-call(s32[2]{0:T(128)S(1)} %pad_add_fusion.after_this.place, f32[8,128]{1,0:T(8,128)S(1)} %get-tuple-element.67.after_this, bf16[64,4224]{1,0:T(8,128)(2,1)S(1)} %collective-permute-done.11.refs_0_, ...), custom_call_target="tpu_custom_call" | custom-call | flops 1 | bytes 1 | tf_op jit(solution)/shard_map/pallas_call | solution.py:329
  88.1 0.3 collective-permute-start.15
  88.4 1.8 %collective-permute-start.16 = (bf16[64,2176]{1,0:T(8,128)(2,1)S(1)}, bf16[64,2176]{1,0:T(8,128)(2,1)S(1)}, u32[]{:S(2)}, u32[]{:S(2)}) collective-permute-start(bf16[64,2176]{1,0:T(8,128)(2,1)S(1)} %get-tuple-element.75), channel_id=1, source_target_pairs={{0,4},{4,8},{8,12},{12,14},{14,10},{10,6},{6,2},{2,0},{1,5},{5,9},... | collective-permute-start | bytes 835592 | tf_op jit(solution)/shard_map/ppermute | solution.py:401
  90.2 1.5 %collective-permute-done.13.refs_0_ = bf16[64,4224]{1,0:T(8,128)(2,1)S(1)} collective-permute-done((bf16[64,4224]{1,0:T(8,128)(2,1)S(1)}, bf16[64,4224]{1,0:T(8,128)(2,1)S(1)}, u32[]{:S(2)}, u32[]{:S(2)}) %collective-permute-start.13) | collective-permute-done | bytes 540704 | tf_op jit(solution)/shard_map/ppermute | solution.py:398
  91.7 2.0 %collective-permute-done.14.refs_1_ = bf16[64,4224]{1,0:T(8,128)(2,1)S(1)} collective-permute-done((bf16[64,4224]{1,0:T(8,128)(2,1)S(1)}, bf16[64,4224]{1,0:T(8,128)(2,1)S(1)}, u32[]{:S(2)}, u32[]{:S(2)}) %collective-permute-start.14) | collective-permute-done | bytes 540704 | tf_op jit(solution)/shard_map/ppermute | solution.py:398
  93.7 6.1 %shard_map.94 = (bf16[64,2176]{1,0:T(8,128)(2,1)S(1)}, bf16[64,2176]{1,0:T(8,128)(2,1)S(1)}, f32[8,128]{1,0:T(8,128)}) custom-call(s32[2]{0:T(128)S(1)} %pad_add_fusion.after_this.place, f32[8,128]{1,0:T(8,128)S(1)} %get-tuple-element.70.after_this, bf16[64,4224]{1,0:T(8,128)(2,1)S(1)} %collective-permute-done.13.refs_0_, ...), custom_call_target="tpu_custom_call" | custom-call | flops 1 | bytes 1 | tf_op jit(solution)/shard_map/pallas_call | solution.py:329
  99.8 0.3 collective-permute-start.17
  100.1 1.8 %collective-permute-start.25 = (bf16[64,2176]{1,0:T(8,128)(2,1)S(1)}, bf16[64,2176]{1,0:T(8,128)(2,1)S(1)}, u32[]{:S(2)}, u32[]{:S(2)}) collective-permute-start(bf16[64,2176]{1,0:T(8,128)(2,1)S(1)} %get-tuple-element.83), channel_id=1, source_target_pairs={{0,4},{4,8},{8,12},{12,14},{14,10},{10,6},{6,2},{2,0},{1,5},{5,9},... | collective-permute-start | bytes 835592 | tf_op jit(solution)/shard_map/ppermute | solution.py:401
  101.9 6.1 %collective-permute-done.17.b = bf16[64,2176]{1,0:T(8,128)(2,1)S(1)} collective-permute-done((bf16[64,2176]{1,0:T(8,128)(2,1)S(1)}, bf16[64,2176]{1,0:T(8,128)(2,1)S(1)}, u32[]{:S(2)}, u32[]{:S(2)}) %collective-permute-start.17) | collective-permute-done | bytes 278560 | tf_op jit(solution)/shard_map/ppermute | solution.py:401
  108.2 2.1 %collective-permute-start.26 = (bf16[64,2176]{1,0:T(8,128)(2,1)S(1)}, bf16[64,2176]{1,0:T(8,128)(2,1)S(1)}, u32[]{:S(2)}, u32[]{:S(2)}) collective-permute-start(bf16[64,2176]{1,0:T(8,128)(2,1)S(1)} %shard_map.102), channel_id=1, source_target_pairs={{0,4},{4,8},{8,12},{12,14},{14,10},{10,6},{6,2},{2,0},{1,5},{5,9},... | collective-permute-start | bytes 835592 | tf_op jit(solution)/shard_map/ppermute | solution.py:401
  110.5 1.6 %collective-permute-start.21 = (bf16[64,2176]{1,0:T(8,128)(2,1)S(1)}, bf16[64,2176]{1,0:T(8,128)(2,1)S(1)}, u32[]{:S(2)}, u32[]{:S(2)}) collective-permute-start(bf16[64,2176]{1,0:T(8,128)(2,1)S(1)} %shard_map.98), channel_id=1, source_target_pairs={{0,4},{4,8},{8,12},{12,14},{14,10},{10,6},{6,2},{2,0},{1,5},{5,9},... | collective-permute-start | bytes 835592 | tf_op jit(solution)/shard_map/ppermute | solution.py:401
  112.2 0.5 collective-permute-start.23
  112.7 5.1 %collective-permute-done.18.b = bf16[64,2176]{1,0:T(8,128)(2,1)S(1)} collective-permute-done((bf16[64,2176]{1,0:T(8,128)(2,1)S(1)}, bf16[64,2176]{1,0:T(8,128)(2,1)S(1)}, u32[]{:S(2)}, u32[]{:S(2)}) %collective-permute-start.18) | collective-permute-done | bytes 278560 | tf_op jit(solution)/shard_map/ppermute | solution.py:401
  118.0 2.1 %collective-permute-start.27 = (bf16[64,2176]{1,0:T(8,128)(2,1)S(1)}, bf16[64,2176]{1,0:T(8,128)(2,1)S(1)}, u32[]{:S(2)}, u32[]{:S(2)}) collective-permute-start(bf16[64,2176]{1,0:T(8,128)(2,1)S(1)} %shard_map.103), channel_id=1, source_target_pairs={{0,4},{4,8},{8,12},{12,14},{14,10},{10,6},{6,2},{2,0},{1,5},{5,9},... | collective-permute-start | bytes 835592 | tf_op jit(solution)/shard_map/ppermute | solution.py:401
  120.1 3.8 %collective-permute-done.21.b = bf16[64,2176]{1,0:T(8,128)(2,1)S(1)} collective-permute-done((bf16[64,2176]{1,0:T(8,128)(2,1)S(1)}, bf16[64,2176]{1,0:T(8,128)(2,1)S(1)}, u32[]{:S(2)}, u32[]{:S(2)}) %collective-permute-start.21) | collective-permute-done | bytes 278560 | tf_op jit(solution)/shard_map/ppermute | solution.py:401
  123.9 2.1 %collective-permute-start.22 = (bf16[64,2176]{1,0:T(8,128)(2,1)S(1)}, bf16[64,2176]{1,0:T(8,128)(2,1)S(1)}, u32[]{:S(2)}, u32[]{:S(2)}) collective-permute-start(bf16[64,2176]{1,0:T(8,128)(2,1)S(1)} %shard_map.99), channel_id=1, source_target_pairs={{0,4},{4,8},{8,12},{12,14},{14,10},{10,6},{6,2},{2,0},{1,5},{5,9},... | collective-permute-start | bytes 835592 | tf_op jit(solution)/shard_map/ppermute | solution.py:401
  126.2 3.5 %collective-permute-done.19.b = bf16[64,2176]{1,0:T(8,128)(2,1)S(1)} collective-permute-done((bf16[64,2176]{1,0:T(8,128)(2,1)S(1)}, bf16[64,2176]{1,0:T(8,128)(2,1)S(1)}, u32[]{:S(2)}, u32[]{:S(2)}) %collective-permute-start.19) | collective-permute-done | bytes 278560 | tf_op jit(solution)/shard_map/ppermute | solution.py:401
  129.9 2.1 %collective-permute-start.28 = (bf16[64,2176]{1,0:T(8,128)(2,1)S(1)}, bf16[64,2176]{1,0:T(8,128)(2,1)S(1)}, u32[]{:S(2)}, u32[]{:S(2)}) collective-permute-start(bf16[64,2176]{1,0:T(8,128)(2,1)S(1)} %shard_map.104), channel_id=1, source_target_pairs={{0,4},{4,8},{8,12},{12,14},{14,10},{10,6},{6,2},{2,0},{1,5},{5,9},... | collective-permute-start | bytes 835592 | tf_op jit(solution)/shard_map/ppermute | solution.py:401
  132.0 1.5 %collective-permute-done.22.top1 = bf16[64,2176]{1,0:T(8,128)(2,1)S(1)} collective-permute-done((bf16[64,2176]{1,0:T(8,128)(2,1)S(1)}, bf16[64,2176]{1,0:T(8,128)(2,1)S(1)}, u32[]{:S(2)}, u32[]{:S(2)}) %collective-permute-start.22) | collective-permute-done | bytes 278560 | tf_op jit(solution)/shard_map/ppermute | solution.py:401
  133.5 2.9 %collective-permute-done.20.top0 = bf16[64,2176]{1,0:T(8,128)(2,1)S(1)} collective-permute-done((bf16[64,2176]{1,0:T(8,128)(2,1)S(1)}, bf16[64,2176]{1,0:T(8,128)(2,1)S(1)}, u32[]{:S(2)}, u32[]{:S(2)}) %collective-permute-start.20) | collective-permute-done | bytes 278560 | tf_op jit(solution)/shard_map/ppermute | solution.py:401
  136.3 0.2 collective-permute-done.28.low1
  136.5 1.1 shard_map.105
  (45 shorter events, 1.3 us)
Async XLA Ops:
  0.6 29.5 %collective-permute-start = (bf16[2,2048,384]{2,1,0:T(8,128)(2,1)}, bf16[2,2048,384]{2,1,0:T(8,128)(2,1)}, u32[]{:S(2)}, u32[]{:S(2)}) collective-permute-start(bf16[2,2048,384]{2,1,0:T(8,128)(2,1)} %gate.1), channel_id=1, source_target_pairs={{0,1},{1,0},{2,3},{3,2},{4,5},{5,4},{6,7},{7,6},{8,9},{9,8},{10,11... | collective-permute-start | bytes 9437192 | tf_op jit(solution)/shard_map/ppermute | solution.py:407
  1.1 29.0 %collective-permute-start.3 = (bf16[2,2048,384]{2,1,0:T(8,128)(2,1)}, bf16[2,2048,384]{2,1,0:T(8,128)(2,1)}, u32[]{:S(2)}, u32[]{:S(2)}) collective-permute-start(bf16[2,2048,384]{2,1,0:T(8,128)(2,1)} %up.1), channel_id=1, source_target_pairs={{0,1},{1,0},{2,3},{3,2},{4,5},{5,4},{6,7},{7,6},{8,9},{9,8},{10,11... | collective-permute-start | bytes 9437192 | tf_op jit(solution)/shard_map/ppermute | solution.py:407
  1.2 28.9 %collective-permute-start.4 = (bf16[2,384,2048]{2,1,0:T(8,128)(2,1)}, bf16[2,384,2048]{2,1,0:T(8,128)(2,1)}, u32[]{:S(2)}, u32[]{:S(2)}) collective-permute-start(bf16[2,384,2048]{2,1,0:T(8,128)(2,1)} %down.1), channel_id=1, source_target_pairs={{0,1},{1,0},{2,3},{3,2},{4,5},{5,4},{6,7},{7,6},{8,9},{9,8},{10,11... | collective-permute-start | bytes 9437192 | tf_op jit(solution)/shard_map/ppermute | solution.py:407
  2.9 7.6 %copy-start.2 = (bf16[128,4224]{1,0:T(8,128)(2,1)}, bf16[128,4224]{1,0:T(8,128)(2,1)S(1)}, u32[]{:S(2)}) copy-start(bf16[128,4224]{1,0:T(8,128)(2,1)S(1)} %shard_map.87.refs_0_) | copy-start | bytes 3244036
  2.9 27.1 %collective-permute-start.1 = (bf16[128,4224]{1,0:T(8,128)(2,1)S(1)}, bf16[128,4224]{1,0:T(8,128)(2,1)S(1)}, u32[]{:S(2)}, u32[]{:S(2)}) collective-permute-start(bf16[128,4224]{1,0:T(8,128)(2,1)S(1)} %shard_map.87.refs_0_), channel_id=1, source_target_pairs={{0,4},{4,8},{8,12},{12,14},{14,10},{10,6},{6,2},{2,0},{1,5},{5,9},... | collective-permute-start | bytes 3244040 | tf_op jit(solution)/shard_map/ppermute | solution.py:398
  5.7 26.3 %collective-permute-start.2 = (bf16[128,4224]{1,0:T(8,128)(2,1)S(1)}, bf16[128,4224]{1,0:T(8,128)(2,1)S(1)}, u32[]{:S(2)}, u32[]{:S(2)}) collective-permute-start(bf16[128,4224]{1,0:T(8,128)(2,1)S(1)} %shard_map.87.refs_0_), channel_id=1, source_target_pairs={{4,0},{8,4},{12,8},{14,12},{10,14},{6,10},{2,6},{0,2},{5,1},{9,5},... | collective-permute-start | bytes 3244040 | tf_op jit(solution)/shard_map/ppermute | solution.py:398
  30.0 4.1 %copy-start = (bf16[128,4224]{1,0:T(8,128)(2,1)}, bf16[128,4224]{1,0:T(8,128)(2,1)S(1)}, u32[]{:S(2)}) copy-start(bf16[128,4224]{1,0:T(8,128)(2,1)S(1)} %collective-permute-done.1.refs_0_) | copy-start | bytes 3244036
  30.2 15.2 %collective-permute-start.5 = (bf16[64,4224]{1,0:T(8,128)(2,1)S(1)}, bf16[64,4224]{1,0:T(8,128)(2,1)S(1)}, u32[]{:S(2)}, u32[]{:S(2)}) collective-permute-start(bf16[64,4224]{1,0:T(8,128)(2,1)S(1)} %get-tuple-element.58), channel_id=1, source_target_pairs={{0,4},{4,8},{8,12},{12,14},{14,10},{10,6},{6,2},{2,0},{1,5},{5,9},... | collective-permute-start | bytes 1622024 | tf_op jit(solution)/shard_map/ppermute | solution.py:398
  32.1 15.3 %collective-permute-start.7 = (bf16[64,4224]{1,0:T(8,128)(2,1)S(1)}, bf16[64,4224]{1,0:T(8,128)(2,1)S(1)}, u32[]{:S(2)}, u32[]{:S(2)}) collective-permute-start(bf16[64,4224]{1,0:T(8,128)(2,1)S(1)} %get-tuple-element.60), channel_id=1, source_target_pairs={{4,0},{8,4},{12,8},{14,12},{10,14},{6,10},{2,6},{0,2},{5,1},{9,5},... | collective-permute-start | bytes 1622024 | tf_op jit(solution)/shard_map/ppermute | solution.py:398
  32.4 25.4 %collective-permute-start.6 = (bf16[64,4224]{1,0:T(8,128)(2,1)S(1)}, bf16[64,4224]{1,0:T(8,128)(2,1)S(1)}, u32[]{:S(2)}, u32[]{:S(2)}) collective-permute-start(bf16[64,4224]{1,0:T(8,128)(2,1)S(1)} %get-tuple-element.59), channel_id=1, source_target_pairs={{0,4},{4,8},{8,12},{12,14},{14,10},{10,6},{6,2},{2,0},{1,5},{5,9},... | collective-permute-start | bytes 1622024 | tf_op jit(solution)/shard_map/ppermute | solution.py:398
  34.2 5.1 %copy-start.3 = (bf16[128,4224]{1,0:T(8,128)(2,1)S(1)}, bf16[128,4224]{1,0:T(8,128)(2,1)}, u32[]{:S(2)}) copy-start(bf16[128,4224]{1,0:T(8,128)(2,1)} %copy-done.2) | copy-start | bytes 3244036
  34.2 25.4 %collective-permute-start.8 = (bf16[64,4224]{1,0:T(8,128)(2,1)S(1)}, bf16[64,4224]{1,0:T(8,128)(2,1)S(1)}, u32[]{:S(2)}, u32[]{:S(2)}) collective-permute-start(bf16[64,4224]{1,0:T(8,128)(2,1)S(1)} %get-tuple-element.61), channel_id=1, source_target_pairs={{4,0},{8,4},{12,8},{14,12},{10,14},{6,10},{2,6},{0,2},{5,1},{9,5},... | collective-permute-start | bytes 1622024 | tf_op jit(solution)/shard_map/ppermute | solution.py:398
  39.3 8.3 %copy-start.1 = (bf16[128,4224]{1,0:T(8,128)(2,1)S(1)}, bf16[128,4224]{1,0:T(8,128)(2,1)}, u32[]{:S(2)}) copy-start(bf16[128,4224]{1,0:T(8,128)(2,1)} %copy-done) | copy-start | bytes 3244036
  45.4 24.7 %collective-permute-start.9 = (bf16[64,4224]{1,0:T(8,128)(2,1)S(1)}, bf16[64,4224]{1,0:T(8,128)(2,1)S(1)}, u32[]{:S(2)}, u32[]{:S(2)}) collective-permute-start(bf16[64,4224]{1,0:T(8,128)(2,1)S(1)} %collective-permute-done.5.refs_0_), channel_id=1, source_target_pairs={{0,4},{4,8},{8,12},{12,14},{14,10},{10,6},{6,2},{2,0},{1,5},{5,9},... | collective-permute-start | bytes 1622024 | tf_op jit(solution)/shard_map/ppermute | solution.py:398
  47.4 24.6 %collective-permute-start.10 = (bf16[64,4224]{1,0:T(8,128)(2,1)S(1)}, bf16[64,4224]{1,0:T(8,128)(2,1)S(1)}, u32[]{:S(2)}, u32[]{:S(2)}) collective-permute-start(bf16[64,4224]{1,0:T(8,128)(2,1)S(1)} %collective-permute-done.7.refs_2_), channel_id=1, source_target_pairs={{4,0},{8,4},{12,8},{14,12},{10,14},{6,10},{2,6},{0,2},{5,1},{9,5},... | collective-permute-start | bytes 1622024 | tf_op jit(solution)/shard_map/ppermute | solution.py:398
  57.8 22.4 %collective-permute-start.11 = (bf16[64,4224]{1,0:T(8,128)(2,1)S(1)}, bf16[64,4224]{1,0:T(8,128)(2,1)S(1)}, u32[]{:S(2)}, u32[]{:S(2)}) collective-permute-start(bf16[64,4224]{1,0:T(8,128)(2,1)S(1)} %collective-permute-done.6.refs_1_), channel_id=1, source_target_pairs={{0,4},{4,8},{8,12},{12,14},{14,10},{10,6},{6,2},{2,0},{1,5},{5,9},... | collective-permute-start | bytes 1622024 | tf_op jit(solution)/shard_map/ppermute | solution.py:398
  59.6 22.5 %collective-permute-start.12 = (bf16[64,4224]{1,0:T(8,128)(2,1)S(1)}, bf16[64,4224]{1,0:T(8,128)(2,1)S(1)}, u32[]{:S(2)}, u32[]{:S(2)}) collective-permute-start(bf16[64,4224]{1,0:T(8,128)(2,1)S(1)} %collective-permute-done.8.refs_3_), channel_id=1, source_target_pairs={{4,0},{8,4},{12,8},{14,12},{10,14},{6,10},{2,6},{0,2},{5,1},{9,5},... | collective-permute-start | bytes 1622024 | tf_op jit(solution)/shard_map/ppermute | solution.py:398
  70.0 21.7 %collective-permute-start.13 = (bf16[64,4224]{1,0:T(8,128)(2,1)S(1)}, bf16[64,4224]{1,0:T(8,128)(2,1)S(1)}, u32[]{:S(2)}, u32[]{:S(2)}) collective-permute-start(bf16[64,4224]{1,0:T(8,128)(2,1)S(1)} %collective-permute-done.9.refs_0_), channel_id=1, source_target_pairs={{0,4},{4,8},{8,12},{12,14},{14,10},{10,6},{6,2},{2,0},{1,5},{5,9},... | collective-permute-start | bytes 1622024 | tf_op jit(solution)/shard_map/ppermute | solution.py:398
  71.9 21.8 %collective-permute-start.14 = (bf16[64,4224]{1,0:T(8,128)(2,1)S(1)}, bf16[64,4224]{1,0:T(8,128)(2,1)S(1)}, u32[]{:S(2)}, u32[]{:S(2)}) collective-permute-start(bf16[64,4224]{1,0:T(8,128)(2,1)S(1)} %collective-permute-done.10.refs_1_), channel_id=1, source_target_pairs={{4,0},{8,4},{12,8},{14,12},{10,14},{6,10},{2,6},{0,2},{5,1},{9,5},... | collective-permute-start | bytes 1622024 | tf_op jit(solution)/shard_map/ppermute | solution.py:398
  88.1 11.7 %collective-permute-start.15 = (bf16[64,2176]{1,0:T(8,128)(2,1)S(1)}, bf16[64,2176]{1,0:T(8,128)(2,1)S(1)}, u32[]{:S(2)}, u32[]{:S(2)}) collective-permute-start(bf16[64,2176]{1,0:T(8,128)(2,1)S(1)} %get-tuple-element.74), channel_id=1, source_target_pairs={{4,0},{8,4},{12,8},{14,12},{10,14},{6,10},{2,6},{0,2},{5,1},{9,5},... | collective-permute-start | bytes 835592 | tf_op jit(solution)/shard_map/ppermute | solution.py:401
  88.4 11.4 %collective-permute-start.16 = (bf16[64,2176]{1,0:T(8,128)(2,1)S(1)}, bf16[64,2176]{1,0:T(8,128)(2,1)S(1)}, u32[]{:S(2)}, u32[]{:S(2)}) collective-permute-start(bf16[64,2176]{1,0:T(8,128)(2,1)S(1)} %get-tuple-element.75), channel_id=1, source_target_pairs={{0,4},{4,8},{8,12},{12,14},{14,10},{10,6},{6,2},{2,0},{1,5},{5,9},... | collective-permute-start | bytes 835592 | tf_op jit(solution)/shard_map/ppermute | solution.py:401
  99.8 8.2 %collective-permute-start.17 = (bf16[64,2176]{1,0:T(8,128)(2,1)S(1)}, bf16[64,2176]{1,0:T(8,128)(2,1)S(1)}, u32[]{:S(2)}, u32[]{:S(2)}) collective-permute-start(bf16[64,2176]{1,0:T(8,128)(2,1)S(1)} %get-tuple-element.76), channel_id=1, source_target_pairs={{4,0},{8,4},{12,8},{14,12},{10,14},{6,10},{2,6},{0,2},{5,1},{9,5},... | collective-permute-start | bytes 835592 | tf_op jit(solution)/shard_map/ppermute | solution.py:401
  100.1 8.1 %collective-permute-start.25 = (bf16[64,2176]{1,0:T(8,128)(2,1)S(1)}, bf16[64,2176]{1,0:T(8,128)(2,1)S(1)}, u32[]{:S(2)}, u32[]{:S(2)}) collective-permute-start(bf16[64,2176]{1,0:T(8,128)(2,1)S(1)} %get-tuple-element.83), channel_id=1, source_target_pairs={{0,4},{4,8},{8,12},{12,14},{14,10},{10,6},{6,2},{2,0},{1,5},{5,9},... | collective-permute-start | bytes 835592 | tf_op jit(solution)/shard_map/ppermute | solution.py:401
  108.1 9.6 %collective-permute-start.18 = (bf16[64,2176]{1,0:T(8,128)(2,1)S(1)}, bf16[64,2176]{1,0:T(8,128)(2,1)S(1)}, u32[]{:S(2)}, u32[]{:S(2)}) collective-permute-start(bf16[64,2176]{1,0:T(8,128)(2,1)S(1)} %shard_map.95), channel_id=1, source_target_pairs={{4,0},{8,4},{12,8},{14,12},{10,14},{6,10},{2,6},{0,2},{5,1},{9,5},... | collective-permute-start | bytes 835592 | tf_op jit(solution)/shard_map/ppermute | solution.py:401
  108.2 9.6 %collective-permute-start.26 = (bf16[64,2176]{1,0:T(8,128)(2,1)S(1)}, bf16[64,2176]{1,0:T(8,128)(2,1)S(1)}, u32[]{:S(2)}, u32[]{:S(2)}) collective-permute-start(bf16[64,2176]{1,0:T(8,128)(2,1)S(1)} %shard_map.102), channel_id=1, source_target_pairs={{0,4},{4,8},{8,12},{12,14},{14,10},{10,6},{6,2},{2,0},{1,5},{5,9},... | collective-permute-start | bytes 835592 | tf_op jit(solution)/shard_map/ppermute | solution.py:401
  110.5 13.4 %collective-permute-start.21 = (bf16[64,2176]{1,0:T(8,128)(2,1)S(1)}, bf16[64,2176]{1,0:T(8,128)(2,1)S(1)}, u32[]{:S(2)}, u32[]{:S(2)}) collective-permute-start(bf16[64,2176]{1,0:T(8,128)(2,1)S(1)} %shard_map.98), channel_id=1, source_target_pairs={{0,4},{4,8},{8,12},{12,14},{14,10},{10,6},{6,2},{2,0},{1,5},{5,9},... | collective-permute-start | bytes 835592 | tf_op jit(solution)/shard_map/ppermute | solution.py:401
  112.2 24.3 %copy-start.4 = (s32[128,8]{0,1:T(8,128)S(1)}, s32[128,8]{0,1:T(8,128)}, u32[]{:S(2)}) copy-start(s32[128,8]{0,1:T(8,128)} %param.9) | copy-start | bytes 12292
  112.2 13.9 %collective-permute-start.23 = (bf16[64,2176]{1,0:T(8,128)(2,1)S(1)}, bf16[64,2176]{1,0:T(8,128)(2,1)S(1)}, u32[]{:S(2)}, u32[]{:S(2)}) collective-permute-start(bf16[64,2176]{1,0:T(8,128)(2,1)S(1)} %shard_map.100), channel_id=1, source_target_pairs={{4,0},{8,4},{12,8},{14,12},{10,14},{6,10},{2,6},{0,2},{5,1},{9,5},... | collective-permute-start | bytes 835592 | tf_op jit(solution)/shard_map/ppermute | solution.py:401
  117.8 11.9 %collective-permute-start.19 = (bf16[64,2176]{1,0:T(8,128)(2,1)S(1)}, bf16[64,2176]{1,0:T(8,128)(2,1)S(1)}, u32[]{:S(2)}, u32[]{:S(2)}) collective-permute-start(bf16[64,2176]{1,0:T(8,128)(2,1)S(1)} %shard_map.96), channel_id=1, source_target_pairs={{4,0},{8,4},{12,8},{14,12},{10,14},{6,10},{2,6},{0,2},{5,1},{9,5},... | collective-permute-start | bytes 835592 | tf_op jit(solution)/shard_map/ppermute | solution.py:401
  118.0 11.9 %collective-permute-start.27 = (bf16[64,2176]{1,0:T(8,128)(2,1)S(1)}, bf16[64,2176]{1,0:T(8,128)(2,1)S(1)}, u32[]{:S(2)}, u32[]{:S(2)}) collective-permute-start(bf16[64,2176]{1,0:T(8,128)(2,1)S(1)} %shard_map.103), channel_id=1, source_target_pairs={{0,4},{4,8},{8,12},{12,14},{14,10},{10,6},{6,2},{2,0},{1,5},{5,9},... | collective-permute-start | bytes 835592 | tf_op jit(solution)/shard_map/ppermute | solution.py:401
  123.9 9.6 %collective-permute-start.22 = (bf16[64,2176]{1,0:T(8,128)(2,1)S(1)}, bf16[64,2176]{1,0:T(8,128)(2,1)S(1)}, u32[]{:S(2)}, u32[]{:S(2)}) collective-permute-start(bf16[64,2176]{1,0:T(8,128)(2,1)S(1)} %shard_map.99), channel_id=1, source_target_pairs={{0,4},{4,8},{8,12},{12,14},{14,10},{10,6},{6,2},{2,0},{1,5},{5,9},... | collective-permute-start | bytes 835592 | tf_op jit(solution)/shard_map/ppermute | solution.py:401
  126.1 7.4 %collective-permute-start.24 = (bf16[64,2176]{1,0:T(8,128)(2,1)S(1)}, bf16[64,2176]{1,0:T(8,128)(2,1)S(1)}, u32[]{:S(2)}, u32[]{:S(2)}) collective-permute-start(bf16[64,2176]{1,0:T(8,128)(2,1)S(1)} %shard_map.101), channel_id=1, source_target_pairs={{4,0},{8,4},{12,8},{14,12},{10,14},{6,10},{2,6},{0,2},{5,1},{9,5},... | collective-permute-start | bytes 835592 | tf_op jit(solution)/shard_map/ppermute | solution.py:401
  129.7 6.6 %collective-permute-start.20 = (bf16[64,2176]{1,0:T(8,128)(2,1)S(1)}, bf16[64,2176]{1,0:T(8,128)(2,1)S(1)}, u32[]{:S(2)}, u32[]{:S(2)}) collective-permute-start(bf16[64,2176]{1,0:T(8,128)(2,1)S(1)} %shard_map.97), channel_id=1, source_target_pairs={{4,0},{8,4},{12,8},{14,12},{10,14},{6,10},{2,6},{0,2},{5,1},{9,5},... | collective-permute-start | bytes 835592 | tf_op jit(solution)/shard_map/ppermute | solution.py:401
  129.9 6.6 %collective-permute-start.28 = (bf16[64,2176]{1,0:T(8,128)(2,1)S(1)}, bf16[64,2176]{1,0:T(8,128)(2,1)S(1)}, u32[]{:S(2)}, u32[]{:S(2)}) collective-permute-start(bf16[64,2176]{1,0:T(8,128)(2,1)S(1)} %shard_map.104), channel_id=1, source_target_pairs={{0,4},{4,8},{8,12},{12,14},{14,10},{10,6},{6,2},{2,0},{1,5},{5,9},... | collective-permute-start | bytes 835592 | tf_op jit(solution)/shard_map/ppermute | solution.py:401
where the time goes:
time: 138 us
  Pallas kernels  57.1 us (41%)
  waiting for transfers between devices  50.2 us (36%)
  starting transfers between devices  29.1 us (21%)
    pallas_call x6, Pallas kernels, experts_call(): pl.pallas_call(functools.partial(experts_kernel, len(packed)), out_shape=...  44.4 us
    ppermute x6, waiting for transfers between devices, send(): lax.ppermute(pair[0], 'grp', ahead)  23.1 us
    ppermute x7, waiting for transfers between devices, send_back(): lax.ppermute(pair[0], 'grp', behind)  17.5 us
    ppermute x7, starting transfers between devices, send_back(): lax.ppermute(pair[1], 'grp', ahead)  13.7 us
    ppermute x6, starting transfers between devices, send(): lax.ppermute(pair[0], 'grp', ahead)  12 us
    pallas_call x2, Pallas kernels, load(): pl.pallas_call(load_kernel, out_shape=(pltpu.VMEM((per_device, width, 2 *...  9.6 us
    ppermute x7, waiting for transfers between devices, send_back(): lax.ppermute(pair[1], 'grp', ahead)  5.43 us
    ppermute x6, waiting for transfers between devices, send(): lax.ppermute(pair[1], 'grp', behind)  4.15 us
  transfers between devices with their start and end apart: 29, of which 14 were waited for; matrix products, arithmetic and copies ran while one was open for 0% of the time, Pallas kernels for 41%

commit v1 on v0

--- a/solution.py
+++ b/solution.py
@@ -183,43 +183,68 @@
 TOKEN = jax.ShapeDtypeStruct((8, LANES), jnp.float32)
 
 
-def pack_kernel(tokens, cotangent, ids, weights, block, ids_here, weights_here, sems):
+def pack_kernel(per_group, tokens, cotangent, ids, weights, block, order, ids_here, weights_here, rows_here, sems):
     rows, width = tokens.shape
+    first_expert = (lax.axis_size("grp") - 1 - lax.axis_index("grp")) * per_group
     small = (
         pltpu.make_async_copy(ids, ids_here, sems.at[0]),
         pltpu.make_async_copy(weights, weights_here, sems.at[1]),
     )
     large = (
-        pltpu.make_async_copy(tokens, block.at[:, pl.ds(0, width)], sems.at[2]),
-        pltpu.make_async_copy(cotangent, block.at[:, pl.ds(width, width)], sems.at[3]),
+        pltpu.make_async_copy(tokens, rows_here.at[:, pl.ds(0, width)], sems.at[2]),
+        pltpu.make_async_copy(cotangent, rows_here.at[:, pl.ds(width, width)], sems.at[3]),
     )
     for copy in small + large:
         copy.start()
     for copy in small:
         copy.wait()
-    expert = lax.broadcasted_iota(jnp.int32, (LANES, rows), 0)
+    sublane = lax.broadcasted_iota(jnp.int32, (LANES, rows), 0)
     table = jnp.zeros((LANES, rows), jnp.float32)
+    named = jnp.zeros((1, rows), jnp.float32)
     for k in range(ids.shape[0]):
-        chosen = expert == ids_here[k : k + 1, :]
-        table += jnp.where(chosen, weights_here[k : k + 1, :].astype(jnp.float32), 0.0)
-    block[:, 2 * width :] = table.T.astype(jnp.bfloat16)
-    for copy in large:
+        chosen = ids_here[k : k + 1, :]
+        table += jnp.where(sublane == chosen, weights_here[k : k + 1, :].astype(jnp.float32), 0.0)
+        inside = (chosen >= first_expert) & (chosen < first_expert + per_group)
+        named = jnp.maximum(named, jnp.where(inside, 1.0, 0.0))
+    from_row = lax.broadcasted_iota(jnp.int32, (rows, rows), 0)
+    to_row = lax.broadcasted_iota(jnp.int32, (rows, rows), 1)
+    upper = jnp.where(from_row <= to_row, 1.0, 0.0).astype(jnp.bfloat16)
+    spread = jnp.broadcast_to(named, (16, rows)).astype(jnp.bfloat16)
+    count = jnp.dot(spread, upper, preferred_element_type=jnp.float32)[:1].astype(jnp.int32)
+    total = jnp.max(count, axis=1, keepdims=True)
+    first = lax.shift_right_logical(total + 1, 1)
+    at = lax.broadcasted_iota(jnp.int32, (1, rows), 1)
+    rank = count - 1
+    named_to = jnp.where(rank < first, rank, rows - total + rank)
+    target = jnp.where(named > 0.0, named_to, first + at - count)
+    order_here = jnp.where(from_row == target, 1.0, 0.0).astype(jnp.bfloat16)
+    order[...] = order_here
+    block[:, 2 * width :] = lax.dot_general(
+        order_here, table.astype(jnp.bfloat16), NT, preferred_element_type=jnp.float32
+    ).astype(jnp.bfloat16)
+    for part, copy in enumerate(large):
         copy.wait()
-
-
-def pack(tokens, cotangent, ids, weights):
+        lanes = slice(part * width, (part + 1) * width)
+        block[:, lanes] = jnp.dot(order_here, rows_here[:, lanes], preferred_element_type=jnp.float32).astype(jnp.bfloat16)
+
+
+def pack(per_group, tokens, cotangent, ids, weights):
     rows, width = tokens.shape
     return pl.pallas_call(
-        pack_kernel,
-        out_shape=pltpu.VMEM((rows, 2 * width + LANES), jnp.bfloat16),
+        functools.partial(pack_kernel, per_group),
+        out_shape=(
+            pltpu.VMEM((rows, 2 * width + LANES), jnp.bfloat16),
+            jax.ShapeDtypeStruct((rows, rows), jnp.bfloat16),
+        ),
         in_specs=[ANYWHERE] * 4,
-        out_specs=IN_VMEM,
+        out_specs=(IN_VMEM, IN_VMEM),
         scratch_shapes=[
             pltpu.VMEM((ids.shape[1], rows), jnp.int32),
             pltpu.VMEM((ids.shape[1], rows), jnp.bfloat16),
+            pltpu.VMEM((rows, 2 * width), jnp.bfloat16),
             pltpu.SemaphoreType.DMA((4,)),
         ],
-        compiler_params=pltpu.CompilerParams(vmem_limit_bytes=8 * MIB),
+        compiler_params=pltpu.CompilerParams(vmem_limit_bytes=12 * MIB),
     )(*(in_hbm(a) for a in (tokens, cotangent, ids.T, weights.T)))
 
 
@@ -336,17 +361,19 @@
     )(place, after_this, *(in_vmem(a) for a in packed), *loaded)
 
 
-def finish_kernel(ids, mine, top0, top1, low0, low1, grad_tokens, grad_weights):
+def finish_kernel(ids, order, mine, top0, top1, low0, low1, grad_tokens, grad_weights):
     rows, width = grad_tokens.shape
     cut = rows // 2
-    routes = []
+    halves = []
     for start, terms in ((0, (top0, top1)), (cut, (low0, low1))):
         summed = mine[start : start + cut, :].astype(jnp.float32)
         for term in terms:
             summed += term[...].astype(jnp.float32)
-        grad_tokens[start : start + cut, :] = summed[:, :width].astype(grad_tokens.dtype)
-        routes.append(summed[:, width:])
-    route = jnp.concatenate(routes, axis=0).T
+        halves.append(summed.astype(jnp.bfloat16))
+    summed = jnp.concatenate(halves, axis=0)
+    back = order[...].T
+    grad_tokens[...] = jnp.dot(back, summed[:, :width], preferred_element_type=jnp.float32).astype(grad_tokens.dtype)
+    route = jnp.dot(back, summed[:, width:], preferred_element_type=jnp.float32).T
     expert = lax.broadcasted_iota(jnp.int32, route.shape, 0)
     found = [
         jnp.sum(jnp.where(expert == ids[k : k + 1, :], route, 0.0), axis=0, keepdims=True) for k in range(ids.shape[0])
@@ -362,20 +389,26 @@
             jax.ShapeDtypeStruct((rows, width), jnp.bfloat16),
             jax.ShapeDtypeStruct((top, rows), jnp.bfloat16),
         ),
-        in_specs=[IN_VMEM] * 6,
+        in_specs=[IN_VMEM] * 7,
         out_specs=(IN_VMEM, IN_VMEM),
         compiler_params=pltpu.CompilerParams(vmem_limit_bytes=12 * MIB),
     )(ids.T, *terms)
     return grad_tokens, grad_weights.T
 
 
-def add_kernel(a, b, out):
-    out[...] = (a[...].astype(jnp.float32) + b[...].astype(jnp.float32)).astype(out.dtype)
-
-
-def added(a, b):
+def add_kernel(start, a, b, out):
+    rows = b.shape[0]
+    if start:
+        out[:start, :] = a[:start, :]
+    if start + rows < a.shape[0]:
+        out[start + rows :, :] = a[start + rows :, :]
+    part = slice(start, start + rows)
+    out[part, :] = (a[part, :].astype(jnp.float32) + b[...].astype(jnp.float32)).astype(out.dtype)
+
+
+def added(a, b, start=0):
     return pl.pallas_call(
-        add_kernel,
+        functools.partial(add_kernel, start),
         out_shape=jax.ShapeDtypeStruct(a.shape, a.dtype),
         in_specs=[IN_VMEM] * 2,
         out_specs=IN_VMEM,
@@ -405,9 +438,10 @@
 
     own = (gate_weight, up_weight, down_weight)
     other = [lax.ppermute(a, "loc", [(i, loc_total - 1 - i) for i in range(loc_total)]) for a in own]
-    block = pack(tokens, cotangent, expert_ids, route_weights)
+    per_group = loc_total * per_device
+    place = jnp.stack([rank * per_group, loc * per_device]).astype(jnp.int32)
+    block, rows_order = pack(per_group, tokens, cotangent, expert_ids, route_weights)
     came = send((block, block))
-    place = jnp.stack([rank * (loc_total * per_device), loc * per_device]).astype(jnp.int32)
     *loaded, loaded_own = load(place, *(in_hbm(a) for a in own))
     *others, last = load(loaded_own, *tie(other[:2], *came), other[2])
     loaded += others
@@ -417,6 +451,7 @@
         return parts, token
 
     half, cut = ring_total // 2, block.shape[0] // 2
+    most = 3 * block.shape[0] // ring_total
 
     def split(pair):
         return (pair[0][:cut], pair[1][cut:]), (pair[0][cut:], pair[1][:cut])
@@ -436,7 +471,7 @@
         long_terms.append((parts[0], parts[2]))
         short_terms.append((parts[1], parts[3]))
     long, short = long_next, short_next
-    long_last = send(tie(long, last))
+    long_last = send(tie((long[0][:most], long[1][cut - most :]), last))
     parts, last = call(last, *long)
     long_terms.append(tuple(parts))
     parts, last = call(last, *short)
@@ -446,8 +481,9 @@
     for s in range(half - 1, 0, -1):
         if s < half - 1:
             short_back = send_back([added(a, b) for a, b in zip(short_terms[s], short_back)])
-        long_back = send_back([added(a, b) for a, b in zip(long_terms[s], long_back)])
-    return finish(expert_ids, (mine, long_back[0], short_back[1], short_back[0], long_back[1]), width)
+        starts = (0, cut - most) if s == half - 1 else (0, 0)
+        long_back = send_back([added(a, b, at) for a, b, at in zip(long_terms[s], long_back, starts)])
+    return finish(expert_ids, (rows_order, mine, long_back[0], short_back[1], short_back[0], long_back[1]), width)
 
 
 def body(tokens, cotangent, expert_ids, route_weights, gate_weight, up_weight, down_weight):

time: 138 us -> 135 us (0.978)
  waiting for transfers between devices: 50.2 us -> 46 us
    ppermute x6, waiting for transfers between devices: 23.1 us -> 21.2 us  [send(): lax.ppermute(pair[0], 'grp', ahead)]
    ppermute x6, waiting for transfers between devices: 4.15 us -> 2.61 us  [send(): lax.ppermute(pair[1], 'grp', behind)]
  transfers between devices with their start and end apart: 29 -> 29, of which waited for: 14 -> 13; matrix products, arithmetic and copies ran while one was open for 0% -> 0% of each run, Pallas kernels for 41% -> 42%
where the time goes in v1:
time: 135 us
  Pallas kernels  58.2 us (43%)
  waiting for transfers between devices  46 us (34%)
  starting transfers between devices  29.3 us (22%)
    pallas_call x6, Pallas kernels, experts_call(): pl.pallas_call(functools.partial(experts_kernel, len(packed)), out_shape=...  45 us
    ppermute x6, waiting for transfers between devices, send(): lax.ppermute(pair[0], 'grp', ahead)  21.2 us
    ppermute x7, waiting for transfers between devices, send_back(): lax.ppermute(pair[0], 'grp', behind)  16.7 us
    ppermute x7, starting transfers between devices, send_back(): lax.ppermute(pair[1], 'grp', ahead)  13.7 us
    ppermute x6, starting transfers between devices, send(): lax.ppermute(pair[0], 'grp', ahead)  12 us
    pallas_call x2, Pallas kernels, load(): pl.pallas_call(load_kernel, out_shape=(pltpu.VMEM((per_device, width, 2 *...  9.6 us
    ppermute x7, waiting for transfers between devices, send_back(): lax.ppermute(pair[1], 'grp', ahead)  5.48 us
  transfers between devices with their start and end apart: 29, of which 13 were waited for; matrix products, arithmetic and copies ran while one was open for 0% of the time, Pallas kernels for 42%

profile of v1, /device:TPU:0, one launch (start us, length us, event | category | flops | bytes accessed | tf_op | source)
XLA Modules:
  0.0 134.8 jit_solution(7745802829619917377)
XLA Ops:
  0.6 0.5 collective-permute-start
  1.1 0.1 collective-permute-start.3
  1.2 0.4 collective-permute-start.4
  1.7 1.7 %shard_map.86 = (bf16[128,4224]{1,0:T(8,128)(2,1)S(1)}, bf16[128,128]{1,0:T(8,128)(2,1)S(1)}) custom-call(bf16[128,2048]{1,0:T(8,128)(2,1)} %tokens.1, bf16[128,2048]{1,0:T(8,128)(2,1)} %cotangent.1, s32[8,128]{1,0:T(8,128)} %bitcast.5, bf16[8,128]{1,0:T(8,128)(2,1)} %bitcast.7), custom_call_target="tpu_custom_call" | custom-call | tf_op jit(solution)/shard_map/pallas_call | solution.py:233
  3.4 2.7 %collective-permute-start.1 = (bf16[128,4224]{1,0:T(8,128)(2,1)S(1)}, bf16[128,4224]{1,0:T(8,128)(2,1)S(1)}, u32[]{:S(2)}, u32[]{:S(2)}) collective-permute-start(bf16[128,4224]{1,0:T(8,128)(2,1)S(1)} %get-tuple-element.48.refs_0_), channel_id=1, source_target_pairs={{0,4},{4,8},{8,12},{12,14},{14,10},{10,6},{6,2},{2,0},{1,5},{5,9},... | collective-permute-start | bytes 3244040 | tf_op jit(solution)/shard_map/ppermute | solution.py:431
  6.1 0.1 pad_add_fusion.after_this.place
  6.2 4.7 %shard_map.87 = (bf16[2,2048,768]{2,1,0:T(8,128)(2,1)S(1)}, bf16[1536,2048]{1,0:T(8,128)(2,1)S(1)}, bf16[2048,768]{1,0:T(8,128)(2,1)S(1)}, f32[8,128]{1,0:T(8,128)S(1)}) custom-call(s32[2]{0:T(128)S(1)} %pad_add_fusion.after_this.place, bf16[2,2048,384]{2,1,0:T(8,128)(2,1)} %gate.1, bf16[2,2048,384]{2,1,0:T(8,128)(2,1)} %up.1, bf16[2,384,2048]{2,1,0:T(8,128)(2,1)} %down.1), custom_call_target="tpu_custom_call" | custom-call | flops 1 | bytes 25165824 | tf_op jit(solution)/shard_map/pallas_call | solution.py:285
  11.0 19.5 %collective-permute-done.1.refs_0_ = bf16[128,4224]{1,0:T(8,128)(2,1)S(1)} collective-permute-done((bf16[128,4224]{1,0:T(8,128)(2,1)S(1)}, bf16[128,4224]{1,0:T(8,128)(2,1)S(1)}, u32[]{:S(2)}, u32[]{:S(2)}) %collective-permute-start.1) | collective-permute-done | bytes 1081376 | tf_op jit(solution)/shard_map/ppermute | solution.py:431
  30.5 0.1 fusion.1
  30.6 1.9 %collective-permute-start.5 = (bf16[64,4224]{1,0:T(8,128)(2,1)S(1)}, bf16[64,4224]{1,0:T(8,128)(2,1)S(1)}, u32[]{:S(2)}, u32[]{:S(2)}) collective-permute-start(bf16[64,4224]{1,0:T(8,128)(2,1)S(1)} %get-tuple-element.62), channel_id=1, source_target_pairs={{0,4},{4,8},{8,12},{12,14},{14,10},{10,6},{6,2},{2,0},{1,5},{5,9},... | collective-permute-start | bytes 1622024 | tf_op jit(solution)/shard_map/ppermute | solution.py:431
  32.6 0.3 collective-permute-start.7
  32.8 1.8 %collective-permute-start.6 = (bf16[64,4224]{1,0:T(8,128)(2,1)S(1)}, bf16[64,4224]{1,0:T(8,128)(2,1)S(1)}, u32[]{:S(2)}, u32[]{:S(2)}) collective-permute-start(bf16[64,4224]{1,0:T(8,128)(2,1)S(1)} %get-tuple-element.63), channel_id=1, source_target_pairs={{0,4},{4,8},{8,12},{12,14},{14,10},{10,6},{6,2},{2,0},{1,5},{5,9},... | collective-permute-start | bytes 1622024 | tf_op jit(solution)/shard_map/ppermute | solution.py:431
  34.7 0.2 collective-permute-start.8
  34.9 4.9 %shard_map.88 = (bf16[2,2048,768]{2,1,0:T(8,128)(2,1)S(1)}, bf16[1536,2048]{1,0:T(8,128)(2,1)S(1)}, bf16[2048,768]{1,0:T(8,128)(2,1)S(1)}, f32[8,128]{1,0:T(8,128)S(1)}) custom-call(f32[8,128]{1,0:T(8,128)S(1)} %get-tuple-element.47.after_this, bf16[2,2048,384]{2,1,0:T(8,128)(2,1)} %collective-permute-done.gate, ...), custom_call_target="tpu_custom_call" | custom-call | flops 1 | bytes 25165824 | tf_op jit(solution)/shard_map/pallas_call | solution.py:285
  39.8 6.0 %shard_map.89 = (bf16[128,2176]{1,0:T(8,128)(2,1)S(1)}, f32[8,128]{1,0:T(8,128)S(1)}) custom-call(s32[2]{0:T(128)S(1)} %pad_add_fusion.after_this.place, f32[8,128]{1,0:T(8,128)S(1)} %get-tuple-element.51.after_this, bf16[128,4224]{1,0:T(8,128)(2,1)S(1)} %copy-done.3, bf16[2,2048,768]{2,1,0:T(8,128)(2,1)S(1)} %get-tuple-element.52.refs_1_.refs_2_.refs_4_, ...), custom_call_target="tpu_custom_call" | custom-call | flops 1 | bytes 1 | tf_op jit(solution)/shard_map/pallas_call | solution.py:354
  45.8 1.8 %collective-permute-start.9 = (bf16[64,4224]{1,0:T(8,128)(2,1)S(1)}, bf16[64,4224]{1,0:T(8,128)(2,1)S(1)}, u32[]{:S(2)}, u32[]{:S(2)}) collective-permute-start(bf16[64,4224]{1,0:T(8,128)(2,1)S(1)} %collective-permute-done.5.refs_0_), channel_id=1, source_target_pairs={{0,4},{4,8},{8,12},{12,14},{14,10},{10,6},{6,2},{2,0},{1,5},{5,9},... | collective-permute-start | bytes 1622024 | tf_op jit(solution)/shard_map/ppermute | solution.py:431
  47.7 0.2 collective-permute-done.7.refs_2_
  47.8 0.2 collective-permute-start.10
  48.0 10.2 %shard_map.90 = (bf16[128,2176]{1,0:T(8,128)(2,1)S(1)}, bf16[128,2176]{1,0:T(8,128)(2,1)S(1)}, f32[8,128]{1,0:T(8,128)S(1)}) custom-call(s32[2]{0:T(128)S(1)} %pad_add_fusion.after_this.place, f32[8,128]{1,0:T(8,128)S(1)} %get-tuple-element.59.after_this, bf16[128,4224]{1,0:T(8,128)(2,1)S(1)} %copy-done.1, ...), custom_call_target="tpu_custom_call" | custom-call | flops 1 | bytes 1 | tf_op jit(solution)/shard_map/pallas_call | solution.py:354
  58.3 1.9 %collective-permute-start.11 = (bf16[64,4224]{1,0:T(8,128)(2,1)S(1)}, bf16[64,4224]{1,0:T(8,128)(2,1)S(1)}, u32[]{:S(2)}, u32[]{:S(2)}) collective-permute-start(bf16[64,4224]{1,0:T(8,128)(2,1)S(1)} %collective-permute-done.6.refs_1_), channel_id=1, source_target_pairs={{0,4},{4,8},{8,12},{12,14},{14,10},{10,6},{6,2},{2,0},{1,5},{5,9},... | collective-permute-start | bytes 1622024 | tf_op jit(solution)/shard_map/ppermute | solution.py:431
  60.1 0.2 collective-permute-start.12
  60.4 10.2 %shard_map.91 = (bf16[64,2176]{1,0:T(8,128)(2,1)S(1)}, bf16[64,2176]{1,0:T(8,128)(2,1)S(1)}, bf16[64,2176]{1,0:T(8,128)(2,1)S(1)}, bf16[64,2176]{1,0:T(8,128)(2,1)S(1)}, f32[8,128]{1,0:T(8,128)S(1)}) custom-call(s32[2]{0:T(128)S(1)} %pad_add_fusion.after_this.place, f32[8,128]{1,0:T(8,128)S(1)} %get-tuple-element.61.after_this, ...), custom_call_target="tpu_custom_call" | custom-call | flops 1 | bytes 1 | tf_op jit(solution)/shard_map/pallas_call | solution.py:354
  70.6 1.9 %collective-permute-start.13 = (bf16[48,4224]{1,0:T(8,128)(2,1)S(1)}, bf16[48,4224]{1,0:T(8,128)(2,1)S(1)}, u32[]{:S(2)}, u32[]{:S(2)}) collective-permute-start(bf16[48,4224]{1,0:T(8,128)(2,1)S(1)} %slice.44), channel_id=1, source_target_pairs={{0,4},{4,8},{8,12},{12,14},{14,10},{10,6},{6,2},{2,0},{1,5},{5,9},... | collective-permute-start | bytes 1216520 | tf_op jit(solution)/shard_map/ppermute | solution.py:431
  72.5 0.5 collective-permute-start.14
  73.0 6.0 %shard_map.92 = (bf16[64,2176]{1,0:T(8,128)(2,1)S(1)}, bf16[64,2176]{1,0:T(8,128)(2,1)S(1)}, f32[8,128]{1,0:T(8,128)S(1)}) custom-call(s32[2]{0:T(128)S(1)} %pad_add_fusion.after_this.place, f32[8,128]{1,0:T(8,128)S(1)} %get-tuple-element.67.after_this, bf16[64,4224]{1,0:T(8,128)(2,1)S(1)} %collective-permute-done.9.refs_0_, ...), custom_call_target="tpu_custom_call" | custom-call | flops 1 | bytes 1 | tf_op jit(solution)/shard_map/pallas_call | solution.py:354
  79.0 1.6 %collective-permute-done.11.refs_0_ = bf16[64,4224]{1,0:T(8,128)(2,1)S(1)} collective-permute-done((bf16[64,4224]{1,0:T(8,128)(2,1)S(1)}, bf16[64,4224]{1,0:T(8,128)(2,1)S(1)}, u32[]{:S(2)}, u32[]{:S(2)}) %collective-permute-start.11) | collective-permute-done | bytes 540704 | tf_op jit(solution)/shard_map/ppermute | solution.py:431
  80.6 2.0 %collective-permute-done.12.refs_1_ = bf16[64,4224]{1,0:T(8,128)(2,1)S(1)} collective-permute-done((bf16[64,4224]{1,0:T(8,128)(2,1)S(1)}, bf16[64,4224]{1,0:T(8,128)(2,1)S(1)}, u32[]{:S(2)}, u32[]{:S(2)}) %collective-permute-start.12) | collective-permute-done | bytes 540704 | tf_op jit(solution)/shard_map/ppermute | solution.py:431
  82.6 6.0 %shard_map.93 = (bf16[64,2176]{1,0:T(8,128)(2,1)S(1)}, bf16[64,2176]{1,0:T(8,128)(2,1)S(1)}, f32[8,128]{1,0:T(8,128)S(1)}) custom-call(s32[2]{0:T(128)S(1)} %pad_add_fusion.after_this.place, f32[8,128]{1,0:T(8,128)S(1)} %get-tuple-element.71.after_this, bf16[64,4224]{1,0:T(8,128)(2,1)S(1)} %collective-permute-done.11.refs_0_, ...), custom_call_target="tpu_custom_call" | custom-call | flops 1 | bytes 1 | tf_op jit(solution)/shard_map/pallas_call | solution.py:354
  88.6 0.3 collective-permute-start.15
  88.9 1.8 %collective-permute-start.16 = (bf16[64,2176]{1,0:T(8,128)(2,1)S(1)}, bf16[64,2176]{1,0:T(8,128)(2,1)S(1)}, u32[]{:S(2)}, u32[]{:S(2)}) collective-permute-start(bf16[64,2176]{1,0:T(8,128)(2,1)S(1)} %get-tuple-element.79), channel_id=1, source_target_pairs={{0,4},{4,8},{8,12},{12,14},{14,10},{10,6},{6,2},{2,0},{1,5},{5,9},... | collective-permute-start | bytes 835592 | tf_op jit(solution)/shard_map/ppermute | solution.py:434
  90.7 0.4 collective-permute-done.14.refs_1_
  91.1 6.6 %shard_map.94 = (bf16[48,2176]{1,0:T(8,128)(2,1)S(1)}, bf16[48,2176]{1,0:T(8,128)(2,1)S(1)}, f32[8,128]{1,0:T(8,128)}) custom-call(s32[2]{0:T(128)S(1)} %pad_add_fusion.after_this.place, f32[8,128]{1,0:T(8,128)S(1)} %get-tuple-element.74.after_this, bf16[48,4224]{1,0:T(8,128)(2,1)S(1)} %collective-permute-done.13.refs_0_, ...), custom_call_target="tpu_custom_call" | custom-call | flops 1 | bytes 1 | tf_op jit(solution)/shard_map/pallas_call | solution.py:354
  97.7 0.2 collective-permute-start.17
  98.0 1.8 %collective-permute-start.25 = (bf16[48,2176]{1,0:T(8,128)(2,1)S(1)}, bf16[48,2176]{1,0:T(8,128)(2,1)S(1)}, u32[]{:S(2)}, u32[]{:S(2)}) collective-permute-start(bf16[48,2176]{1,0:T(8,128)(2,1)S(1)} %get-tuple-element.87), channel_id=1, source_target_pairs={{0,4},{4,8},{8,12},{12,14},{14,10},{10,6},{6,2},{2,0},{1,5},{5,9},... | collective-permute-start | bytes 626696 | tf_op jit(solution)/shard_map/ppermute | solution.py:434
  99.8 5.3 %collective-permute-done.17.b = bf16[48,2176]{1,0:T(8,128)(2,1)S(1)} collective-permute-done((bf16[48,2176]{1,0:T(8,128)(2,1)S(1)}, bf16[48,2176]{1,0:T(8,128)(2,1)S(1)}, u32[]{:S(2)}, u32[]{:S(2)}) %collective-permute-start.17) | collective-permute-done | bytes 208928 | tf_op jit(solution)/shard_map/ppermute | solution.py:434
  105.3 2.1 %collective-permute-start.26 = (bf16[64,2176]{1,0:T(8,128)(2,1)S(1)}, bf16[64,2176]{1,0:T(8,128)(2,1)S(1)}, u32[]{:S(2)}, u32[]{:S(2)}) collective-permute-start(bf16[64,2176]{1,0:T(8,128)(2,1)S(1)} %shard_map.102), channel_id=1, source_target_pairs={{0,4},{4,8},{8,12},{12,14},{14,10},{10,6},{6,2},{2,0},{1,5},{5,9},... | collective-permute-start | bytes 835592 | tf_op jit(solution)/shard_map/ppermute | solution.py:434
  107.6 1.7 %collective-permute-start.21 = (bf16[64,2176]{1,0:T(8,128)(2,1)S(1)}, bf16[64,2176]{1,0:T(8,128)(2,1)S(1)}, u32[]{:S(2)}, u32[]{:S(2)}) collective-permute-start(bf16[64,2176]{1,0:T(8,128)(2,1)S(1)} %shard_map.98), channel_id=1, source_target_pairs={{0,4},{4,8},{8,12},{12,14},{14,10},{10,6},{6,2},{2,0},{1,5},{5,9},... | collective-permute-start | bytes 835592 | tf_op jit(solution)/shard_map/ppermute | solution.py:434
  109.3 0.5 collective-permute-start.23
  109.8 5.1 %collective-permute-done.18.b = bf16[64,2176]{1,0:T(8,128)(2,1)S(1)} collective-permute-done((bf16[64,2176]{1,0:T(8,128)(2,1)S(1)}, bf16[64,2176]{1,0:T(8,128)(2,1)S(1)}, u32[]{:S(2)}, u32[]{:S(2)}) %collective-permute-start.18) | collective-permute-done | bytes 278560 | tf_op jit(solution)/shard_map/ppermute | solution.py:434
  115.0 2.1 %collective-permute-start.27 = (bf16[64,2176]{1,0:T(8,128)(2,1)S(1)}, bf16[64,2176]{1,0:T(8,128)(2,1)S(1)}, u32[]{:S(2)}, u32[]{:S(2)}) collective-permute-start(bf16[64,2176]{1,0:T(8,128)(2,1)S(1)} %shard_map.103), channel_id=1, source_target_pairs={{0,4},{4,8},{8,12},{12,14},{14,10},{10,6},{6,2},{2,0},{1,5},{5,9},... | collective-permute-start | bytes 835592 | tf_op jit(solution)/shard_map/ppermute | solution.py:434
  117.2 3.7 %collective-permute-done.21.b = bf16[64,2176]{1,0:T(8,128)(2,1)S(1)} collective-permute-done((bf16[64,2176]{1,0:T(8,128)(2,1)S(1)}, bf16[64,2176]{1,0:T(8,128)(2,1)S(1)}, u32[]{:S(2)}, u32[]{:S(2)}) %collective-permute-start.21) | collective-permute-done | bytes 278560 | tf_op jit(solution)/shard_map/ppermute | solution.py:434
  121.0 2.1 %collective-permute-start.22 = (bf16[64,2176]{1,0:T(8,128)(2,1)S(1)}, bf16[64,2176]{1,0:T(8,128)(2,1)S(1)}, u32[]{:S(2)}, u32[]{:S(2)}) collective-permute-start(bf16[64,2176]{1,0:T(8,128)(2,1)S(1)} %shard_map.99), channel_id=1, source_target_pairs={{0,4},{4,8},{8,12},{12,14},{14,10},{10,6},{6,2},{2,0},{1,5},{5,9},... | collective-permute-start | bytes 835592 | tf_op jit(solution)/shard_map/ppermute | solution.py:434
  123.3 3.5 %collective-permute-done.19.b = bf16[64,2176]{1,0:T(8,128)(2,1)S(1)} collective-permute-done((bf16[64,2176]{1,0:T(8,128)(2,1)S(1)}, bf16[64,2176]{1,0:T(8,128)(2,1)S(1)}, u32[]{:S(2)}, u32[]{:S(2)}) %collective-permute-start.19) | collective-permute-done | bytes 278560 | tf_op jit(solution)/shard_map/ppermute | solution.py:434
  127.0 2.1 %collective-permute-start.28 = (bf16[64,2176]{1,0:T(8,128)(2,1)S(1)}, bf16[64,2176]{1,0:T(8,128)(2,1)S(1)}, u32[]{:S(2)}, u32[]{:S(2)}) collective-permute-start(bf16[64,2176]{1,0:T(8,128)(2,1)S(1)} %shard_map.104), channel_id=1, source_target_pairs={{0,4},{4,8},{8,12},{12,14},{14,10},{10,6},{6,2},{2,0},{1,5},{5,9},... | collective-permute-start | bytes 835592 | tf_op jit(solution)/shard_map/ppermute | solution.py:434
  129.1 1.5 %collective-permute-done.22.top1 = bf16[64,2176]{1,0:T(8,128)(2,1)S(1)} collective-permute-done((bf16[64,2176]{1,0:T(8,128)(2,1)S(1)}, bf16[64,2176]{1,0:T(8,128)(2,1)S(1)}, u32[]{:S(2)}, u32[]{:S(2)}) %collective-permute-start.22) | collective-permute-done | bytes 278560 | tf_op jit(solution)/shard_map/ppermute | solution.py:434
  130.6 2.8 %collective-permute-done.20.top0 = bf16[64,2176]{1,0:T(8,128)(2,1)S(1)} collective-permute-done((bf16[64,2176]{1,0:T(8,128)(2,1)S(1)}, bf16[64,2176]{1,0:T(8,128)(2,1)S(1)}, u32[]{:S(2)}, u32[]{:S(2)}) %collective-permute-start.20) | collective-permute-done | bytes 278560 | tf_op jit(solution)/shard_map/ppermute | solution.py:434
  133.4 0.2 collective-permute-done.28.low1
  133.6 1.2 shard_map.105
  (47 shorter events, 1.3 us)
Async XLA Ops:
  0.6 30.0 %collective-permute-start = (bf16[2,2048,384]{2,1,0:T(8,128)(2,1)}, bf16[2,2048,384]{2,1,0:T(8,128)(2,1)}, u32[]{:S(2)}, u32[]{:S(2)}) collective-permute-start(bf16[2,2048,384]{2,1,0:T(8,128)(2,1)} %gate.1), channel_id=1, source_target_pairs={{0,1},{1,0},{2,3},{3,2},{4,5},{5,4},{6,7},{7,6},{8,9},{9,8},{10,11... | collective-permute-start | bytes 9437192 | tf_op jit(solution)/shard_map/ppermute | solution.py:440
  1.1 29.5 %collective-permute-start.3 = (bf16[2,2048,384]{2,1,0:T(8,128)(2,1)}, bf16[2,2048,384]{2,1,0:T(8,128)(2,1)}, u32[]{:S(2)}, u32[]{:S(2)}) collective-permute-start(bf16[2,2048,384]{2,1,0:T(8,128)(2,1)} %up.1), channel_id=1, source_target_pairs={{0,1},{1,0},{2,3},{3,2},{4,5},{5,4},{6,7},{7,6},{8,9},{9,8},{10,11... | collective-permute-start | bytes 9437192 | tf_op jit(solution)/shard_map/ppermute | solution.py:440
  1.2 29.4 %collective-permute-start.4 = (bf16[2,384,2048]{2,1,0:T(8,128)(2,1)}, bf16[2,384,2048]{2,1,0:T(8,128)(2,1)}, u32[]{:S(2)}, u32[]{:S(2)}) collective-permute-start(bf16[2,384,2048]{2,1,0:T(8,128)(2,1)} %down.1), channel_id=1, source_target_pairs={{0,1},{1,0},{2,3},{3,2},{4,5},{5,4},{6,7},{7,6},{8,9},{9,8},{10,11... | collective-permute-start | bytes 9437192 | tf_op jit(solution)/shard_map/ppermute | solution.py:440
  3.4 7.6 %copy-start.2 = (bf16[128,4224]{1,0:T(8,128)(2,1)}, bf16[128,4224]{1,0:T(8,128)(2,1)S(1)}, u32[]{:S(2)}) copy-start(bf16[128,4224]{1,0:T(8,128)(2,1)S(1)} %get-tuple-element.48.refs_0_) | copy-start | bytes 3244036
  3.4 27.1 %collective-permute-start.1 = (bf16[128,4224]{1,0:T(8,128)(2,1)S(1)}, bf16[128,4224]{1,0:T(8,128)(2,1)S(1)}, u32[]{:S(2)}, u32[]{:S(2)}) collective-permute-start(bf16[128,4224]{1,0:T(8,128)(2,1)S(1)} %get-tuple-element.48.refs_0_), channel_id=1, source_target_pairs={{0,4},{4,8},{8,12},{12,14},{14,10},{10,6},{6,2},{2,0},{1,5},{5,9},... | collective-permute-start | bytes 3244040 | tf_op jit(solution)/shard_map/ppermute | solution.py:431
  6.2 26.3 %collective-permute-start.2 = (bf16[128,4224]{1,0:T(8,128)(2,1)S(1)}, bf16[128,4224]{1,0:T(8,128)(2,1)S(1)}, u32[]{:S(2)}, u32[]{:S(2)}) collective-permute-start(bf16[128,4224]{1,0:T(8,128)(2,1)S(1)} %get-tuple-element.48.refs_0_), channel_id=1, source_target_pairs={{4,0},{8,4},{12,8},{14,12},{10,14},{6,10},{2,6},{0,2},{5,1},{9,5},... | collective-permute-start | bytes 3244040 | tf_op jit(solution)/shard_map/ppermute | solution.py:431
  30.5 4.1 %copy-start = (bf16[128,4224]{1,0:T(8,128)(2,1)}, bf16[128,4224]{1,0:T(8,128)(2,1)S(1)}, u32[]{:S(2)}) copy-start(bf16[128,4224]{1,0:T(8,128)(2,1)S(1)} %collective-permute-done.1.refs_0_) | copy-start | bytes 3244036
  30.6 15.2 %collective-permute-start.5 = (bf16[64,4224]{1,0:T(8,128)(2,1)S(1)}, bf16[64,4224]{1,0:T(8,128)(2,1)S(1)}, u32[]{:S(2)}, u32[]{:S(2)}) collective-permute-start(bf16[64,4224]{1,0:T(8,128)(2,1)S(1)} %get-tuple-element.62), channel_id=1, source_target_pairs={{0,4},{4,8},{8,12},{12,14},{14,10},{10,6},{6,2},{2,0},{1,5},{5,9},... | collective-permute-start | bytes 1622024 | tf_op jit(solution)/shard_map/ppermute | solution.py:431
  32.6 15.3 %collective-permute-start.7 = (bf16[64,4224]{1,0:T(8,128)(2,1)S(1)}, bf16[64,4224]{1,0:T(8,128)(2,1)S(1)}, u32[]{:S(2)}, u32[]{:S(2)}) collective-permute-start(bf16[64,4224]{1,0:T(8,128)(2,1)S(1)} %get-tuple-element.64), channel_id=1, source_target_pairs={{4,0},{8,4},{12,8},{14,12},{10,14},{6,10},{2,6},{0,2},{5,1},{9,5},... | collective-permute-start | bytes 1622024 | tf_op jit(solution)/shard_map/ppermute | solution.py:431
  32.8 25.4 %collective-permute-start.6 = (bf16[64,4224]{1,0:T(8,128)(2,1)S(1)}, bf16[64,4224]{1,0:T(8,128)(2,1)S(1)}, u32[]{:S(2)}, u32[]{:S(2)}) collective-permute-start(bf16[64,4224]{1,0:T(8,128)(2,1)S(1)} %get-tuple-element.63), channel_id=1, source_target_pairs={{0,4},{4,8},{8,12},{12,14},{14,10},{10,6},{6,2},{2,0},{1,5},{5,9},... | collective-permute-start | bytes 1622024 | tf_op jit(solution)/shard_map/ppermute | solution.py:431
  34.7 5.1 %copy-start.3 = (bf16[128,4224]{1,0:T(8,128)(2,1)S(1)}, bf16[128,4224]{1,0:T(8,128)(2,1)}, u32[]{:S(2)}) copy-start(bf16[128,4224]{1,0:T(8,128)(2,1)} %copy-done.2) | copy-start | bytes 3244036
  34.7 25.5 %collective-permute-start.8 = (bf16[64,4224]{1,0:T(8,128)(2,1)S(1)}, bf16[64,4224]{1,0:T(8,128)(2,1)S(1)}, u32[]{:S(2)}, u32[]{:S(2)}) collective-permute-start(bf16[64,4224]{1,0:T(8,128)(2,1)S(1)} %get-tuple-element.65), channel_id=1, source_target_pairs={{4,0},{8,4},{12,8},{14,12},{10,14},{6,10},{2,6},{0,2},{5,1},{9,5},... | collective-permute-start | bytes 1622024 | tf_op jit(solution)/shard_map/ppermute | solution.py:431
  39.7 8.3 %copy-start.1 = (bf16[128,4224]{1,0:T(8,128)(2,1)S(1)}, bf16[128,4224]{1,0:T(8,128)(2,1)}, u32[]{:S(2)}) copy-start(bf16[128,4224]{1,0:T(8,128)(2,1)} %copy-done) | copy-start | bytes 3244036
  45.8 24.7 %collective-permute-start.9 = (bf16[64,4224]{1,0:T(8,128)(2,1)S(1)}, bf16[64,4224]{1,0:T(8,128)(2,1)S(1)}, u32[]{:S(2)}, u32[]{:S(2)}) collective-permute-start(bf16[64,4224]{1,0:T(8,128)(2,1)S(1)} %collective-permute-done.5.refs_0_), channel_id=1, source_target_pairs={{0,4},{4,8},{8,12},{12,14},{14,10},{10,6},{6,2},{2,0},{1,5},{5,9},... | collective-permute-start | bytes 1622024 | tf_op jit(solution)/shard_map/ppermute | solution.py:431
  47.8 24.6 %collective-permute-start.10 = (bf16[64,4224]{1,0:T(8,128)(2,1)S(1)}, bf16[64,4224]{1,0:T(8,128)(2,1)S(1)}, u32[]{:S(2)}, u32[]{:S(2)}) collective-permute-start(bf16[64,4224]{1,0:T(8,128)(2,1)S(1)} %collective-permute-done.7.refs_2_), channel_id=1, source_target_pairs={{4,0},{8,4},{12,8},{14,12},{10,14},{6,10},{2,6},{0,2},{5,1},{9,5},... | collective-permute-start | bytes 1622024 | tf_op jit(solution)/shard_map/ppermute | solution.py:431
  58.3 22.3 %collective-permute-start.11 = (bf16[64,4224]{1,0:T(8,128)(2,1)S(1)}, bf16[64,4224]{1,0:T(8,128)(2,1)S(1)}, u32[]{:S(2)}, u32[]{:S(2)}) collective-permute-start(bf16[64,4224]{1,0:T(8,128)(2,1)S(1)} %collective-permute-done.6.refs_1_), channel_id=1, source_target_pairs={{0,4},{4,8},{8,12},{12,14},{14,10},{10,6},{6,2},{2,0},{1,5},{5,9},... | collective-permute-start | bytes 1622024 | tf_op jit(solution)/shard_map/ppermute | solution.py:431
  60.1 22.5 %collective-permute-start.12 = (bf16[64,4224]{1,0:T(8,128)(2,1)S(1)}, bf16[64,4224]{1,0:T(8,128)(2,1)S(1)}, u32[]{:S(2)}, u32[]{:S(2)}) collective-permute-start(bf16[64,4224]{1,0:T(8,128)(2,1)S(1)} %collective-permute-done.8.refs_3_), channel_id=1, source_target_pairs={{4,0},{8,4},{12,8},{14,12},{10,14},{6,10},{2,6},{0,2},{5,1},{9,5},... | collective-permute-start | bytes 1622024 | tf_op jit(solution)/shard_map/ppermute | solution.py:431
  70.6 20.1 %collective-permute-start.13 = (bf16[48,4224]{1,0:T(8,128)(2,1)S(1)}, bf16[48,4224]{1,0:T(8,128)(2,1)S(1)}, u32[]{:S(2)}, u32[]{:S(2)}) collective-permute-start(bf16[48,4224]{1,0:T(8,128)(2,1)S(1)} %slice.44), channel_id=1, source_target_pairs={{0,4},{4,8},{8,12},{12,14},{14,10},{10,6},{6,2},{2,0},{1,5},{5,9},... | collective-permute-start | bytes 1216520 | tf_op jit(solution)/shard_map/ppermute | solution.py:431
  72.5 18.7 %collective-permute-start.14 = (bf16[48,4224]{1,0:T(8,128)(2,1)S(1)}, bf16[48,4224]{1,0:T(8,128)(2,1)S(1)}, u32[]{:S(2)}, u32[]{:S(2)}) collective-permute-start(bf16[48,4224]{1,0:T(8,128)(2,1)S(1)} %slice.45), channel_id=1, source_target_pairs={{4,0},{8,4},{12,8},{14,12},{10,14},{6,10},{2,6},{0,2},{5,1},{9,5},... | collective-permute-start | bytes 1216520 | tf_op jit(solution)/shard_map/ppermute | solution.py:431
  88.6 9.1 %collective-permute-start.15 = (bf16[64,2176]{1,0:T(8,128)(2,1)S(1)}, bf16[64,2176]{1,0:T(8,128)(2,1)S(1)}, u32[]{:S(2)}, u32[]{:S(2)}) collective-permute-start(bf16[64,2176]{1,0:T(8,128)(2,1)S(1)} %get-tuple-element.78), channel_id=1, source_target_pairs={{4,0},{8,4},{12,8},{14,12},{10,14},{6,10},{2,6},{0,2},{5,1},{9,5},... | collective-permute-start | bytes 835592 | tf_op jit(solution)/shard_map/ppermute | solution.py:434
  88.9 8.8 %collective-permute-start.16 = (bf16[64,2176]{1,0:T(8,128)(2,1)S(1)}, bf16[64,2176]{1,0:T(8,128)(2,1)S(1)}, u32[]{:S(2)}, u32[]{:S(2)}) collective-permute-start(bf16[64,2176]{1,0:T(8,128)(2,1)S(1)} %get-tuple-element.79), channel_id=1, source_target_pairs={{0,4},{4,8},{8,12},{12,14},{14,10},{10,6},{6,2},{2,0},{1,5},{5,9},... | collective-permute-start | bytes 835592 | tf_op jit(solution)/shard_map/ppermute | solution.py:434
  97.7 7.4 %collective-permute-start.17 = (bf16[48,2176]{1,0:T(8,128)(2,1)S(1)}, bf16[48,2176]{1,0:T(8,128)(2,1)S(1)}, u32[]{:S(2)}, u32[]{:S(2)}) collective-permute-start(bf16[48,2176]{1,0:T(8,128)(2,1)S(1)} %get-tuple-element.80), channel_id=1, source_target_pairs={{4,0},{8,4},{12,8},{14,12},{10,14},{6,10},{2,6},{0,2},{5,1},{9,5},... | collective-permute-start | bytes 626696 | tf_op jit(solution)/shard_map/ppermute | solution.py:434
  98.0 7.3 %collective-permute-start.25 = (bf16[48,2176]{1,0:T(8,128)(2,1)S(1)}, bf16[48,2176]{1,0:T(8,128)(2,1)S(1)}, u32[]{:S(2)}, u32[]{:S(2)}) collective-permute-start(bf16[48,2176]{1,0:T(8,128)(2,1)S(1)} %get-tuple-element.87), channel_id=1, source_target_pairs={{0,4},{4,8},{8,12},{12,14},{14,10},{10,6},{6,2},{2,0},{1,5},{5,9},... | collective-permute-start | bytes 626696 | tf_op jit(solution)/shard_map/ppermute | solution.py:434
  105.2 9.6 %collective-permute-start.18 = (bf16[64,2176]{1,0:T(8,128)(2,1)S(1)}, bf16[64,2176]{1,0:T(8,128)(2,1)S(1)}, u32[]{:S(2)}, u32[]{:S(2)}) collective-permute-start(bf16[64,2176]{1,0:T(8,128)(2,1)S(1)} %shard_map.95), channel_id=1, source_target_pairs={{4,0},{8,4},{12,8},{14,12},{10,14},{6,10},{2,6},{0,2},{5,1},{9,5},... | collective-permute-start | bytes 835592 | tf_op jit(solution)/shard_map/ppermute | solution.py:434
  105.3 9.6 %collective-permute-start.26 = (bf16[64,2176]{1,0:T(8,128)(2,1)S(1)}, bf16[64,2176]{1,0:T(8,128)(2,1)S(1)}, u32[]{:S(2)}, u32[]{:S(2)}) collective-permute-start(bf16[64,2176]{1,0:T(8,128)(2,1)S(1)} %shard_map.102), channel_id=1, source_target_pairs={{0,4},{4,8},{8,12},{12,14},{14,10},{10,6},{6,2},{2,0},{1,5},{5,9},... | collective-permute-start | bytes 835592 | tf_op jit(solution)/shard_map/ppermute | solution.py:434
  107.6 13.4 %collective-permute-start.21 = (bf16[64,2176]{1,0:T(8,128)(2,1)S(1)}, bf16[64,2176]{1,0:T(8,128)(2,1)S(1)}, u32[]{:S(2)}, u32[]{:S(2)}) collective-permute-start(bf16[64,2176]{1,0:T(8,128)(2,1)S(1)} %shard_map.98), channel_id=1, source_target_pairs={{0,4},{4,8},{8,12},{12,14},{14,10},{10,6},{6,2},{2,0},{1,5},{5,9},... | collective-permute-start | bytes 835592 | tf_op jit(solution)/shard_map/ppermute | solution.py:434
  109.3 24.3 %copy-start.4 = (s32[128,8]{0,1:T(8,128)S(1)}, s32[128,8]{0,1:T(8,128)}, u32[]{:S(2)}) copy-start(s32[128,8]{0,1:T(8,128)} %param.9) | copy-start | bytes 12292
  109.3 13.8 %collective-permute-start.23 = (bf16[64,2176]{1,0:T(8,128)(2,1)S(1)}, bf16[64,2176]{1,0:T(8,128)(2,1)S(1)}, u32[]{:S(2)}, u32[]{:S(2)}) collective-permute-start(bf16[64,2176]{1,0:T(8,128)(2,1)S(1)} %shard_map.100), channel_id=1, source_target_pairs={{4,0},{8,4},{12,8},{14,12},{10,14},{6,10},{2,6},{0,2},{5,1},{9,5},... | collective-permute-start | bytes 835592 | tf_op jit(solution)/shard_map/ppermute | solution.py:434
  114.9 11.9 %collective-permute-start.19 = (bf16[64,2176]{1,0:T(8,128)(2,1)S(1)}, bf16[64,2176]{1,0:T(8,128)(2,1)S(1)}, u32[]{:S(2)}, u32[]{:S(2)}) collective-permute-start(bf16[64,2176]{1,0:T(8,128)(2,1)S(1)} %shard_map.96), channel_id=1, source_target_pairs={{4,0},{8,4},{12,8},{14,12},{10,14},{6,10},{2,6},{0,2},{5,1},{9,5},... | collective-permute-start | bytes 835592 | tf_op jit(solution)/shard_map/ppermute | solution.py:434
  115.0 11.9 %collective-permute-start.27 = (bf16[64,2176]{1,0:T(8,128)(2,1)S(1)}, bf16[64,2176]{1,0:T(8,128)(2,1)S(1)}, u32[]{:S(2)}, u32[]{:S(2)}) collective-permute-start(bf16[64,2176]{1,0:T(8,128)(2,1)S(1)} %shard_map.103), channel_id=1, source_target_pairs={{0,4},{4,8},{8,12},{12,14},{14,10},{10,6},{6,2},{2,0},{1,5},{5,9},... | collective-permute-start | bytes 835592 | tf_op jit(solution)/shard_map/ppermute | solution.py:434
  121.0 9.6 %collective-permute-start.22 = (bf16[64,2176]{1,0:T(8,128)(2,1)S(1)}, bf16[64,2176]{1,0:T(8,128)(2,1)S(1)}, u32[]{:S(2)}, u32[]{:S(2)}) collective-permute-start(bf16[64,2176]{1,0:T(8,128)(2,1)S(1)} %shard_map.99), channel_id=1, source_target_pairs={{0,4},{4,8},{8,12},{12,14},{14,10},{10,6},{6,2},{2,0},{1,5},{5,9},... | collective-permute-start | bytes 835592 | tf_op jit(solution)/shard_map/ppermute | solution.py:434
  123.2 7.4 %collective-permute-start.24 = (bf16[64,2176]{1,0:T(8,128)(2,1)S(1)}, bf16[64,2176]{1,0:T(8,128)(2,1)S(1)}, u32[]{:S(2)}, u32[]{:S(2)}) collective-permute-start(bf16[64,2176]{1,0:T(8,128)(2,1)S(1)} %shard_map.101), channel_id=1, source_target_pairs={{4,0},{8,4},{12,8},{14,12},{10,14},{6,10},{2,6},{0,2},{5,1},{9,5},... | collective-permute-start | bytes 835592 | tf_op jit(solution)/shard_map/ppermute | solution.py:434
  126.8 6.6 %collective-permute-start.20 = (bf16[64,2176]{1,0:T(8,128)(2,1)S(1)}, bf16[64,2176]{1,0:T(8,128)(2,1)S(1)}, u32[]{:S(2)}, u32[]{:S(2)}) collective-permute-start(bf16[64,2176]{1,0:T(8,128)(2,1)S(1)} %shard_map.97), channel_id=1, source_target_pairs={{4,0},{8,4},{12,8},{14,12},{10,14},{6,10},{2,6},{0,2},{5,1},{9,5},... | collective-permute-start | bytes 835592 | tf_op jit(solution)/shard_map/ppermute | solution.py:434
  127.0 6.6 %collective-permute-start.28 = (bf16[64,2176]{1,0:T(8,128)(2,1)S(1)}, bf16[64,2176]{1,0:T(8,128)(2,1)S(1)}, u32[]{:S(2)}, u32[]{:S(2)}) collective-permute-start(bf16[64,2176]{1,0:T(8,128)(2,1)S(1)} %shard_map.104), channel_id=1, source_target_pairs={{0,4},{4,8},{8,12},{12,14},{14,10},{10,6},{6,2},{2,0},{1,5},{5,9},... | collective-permute-start | bytes 835592 | tf_op jit(solution)/shard_map/ppermute | solution.py:434

commit v2 on v0

--- a/solution.py
+++ b/solution.py
@@ -183,43 +183,124 @@
 TOKEN = jax.ShapeDtypeStruct((8, LANES), jnp.float32)
 
 
-def pack_kernel(tokens, cotangent, ids, weights, block, ids_here, weights_here, sems):
+def ring_rank(steps):
+    total, rank = lax.axis_size("grp"), lax.axis_index("grp")
+    half = lax.shift_right_logical(rank + 1, 1)
+    place = jnp.where(lax.rem(rank, 2) == 0, half, total - half) + steps
+    place = jnp.where(place >= total, place - total, place)
+    return jnp.where(2 * place < total, 2 * place, 2 * (total - place) - 1)
+
+
+def pack_kernel(per_group, tokens, cotangent, ids, weights, *refs):
+    up_block, down_block, table_out, *orders, ids_here, weights_here, rows_here, sems = refs
     rows, width = tokens.shape
+    half = lax.axis_size("grp") // 2
     small = (
         pltpu.make_async_copy(ids, ids_here, sems.at[0]),
         pltpu.make_async_copy(weights, weights_here, sems.at[1]),
     )
     large = (
-        pltpu.make_async_copy(tokens, block.at[:, pl.ds(0, width)], sems.at[2]),
-        pltpu.make_async_copy(cotangent, block.at[:, pl.ds(width, width)], sems.at[3]),
+        pltpu.make_async_copy(tokens, rows_here.at[:, pl.ds(0, width)], sems.at[2]),
+        pltpu.make_async_copy(cotangent, rows_here.at[:, pl.ds(width, width)], sems.at[3]),
     )
     for copy in small + large:
         copy.start()
     for copy in small:
         copy.wait()
-    expert = lax.broadcasted_iota(jnp.int32, (LANES, rows), 0)
+    first_experts = [ring_rank(steps) * per_group for steps in (half - 1, half + 1, half)]
+    sublane = lax.broadcasted_iota(jnp.int32, (LANES, rows), 0)
     table = jnp.zeros((LANES, rows), jnp.float32)
+    named = [jnp.zeros((1, rows), jnp.int32) for _ in first_experts]
     for k in range(ids.shape[0]):
-        chosen = expert == ids_here[k : k + 1, :]
-        table += jnp.where(chosen, weights_here[k : k + 1, :].astype(jnp.float32), 0.0)
-    block[:, 2 * width :] = table.T.astype(jnp.bfloat16)
+        chosen = ids_here[k : k + 1, :]
+        table += jnp.where(sublane == chosen, weights_here[k : k + 1, :].astype(jnp.float32), 0.0)
+        named = [
+            n | jnp.where((chosen >= first) & (chosen < first + per_group), 1, 0)
+            for n, first in zip(named, first_experts)
+        ]
+    from_row = lax.broadcasted_iota(jnp.int32, (rows, rows), 0)
+    to_row = lax.broadcasted_iota(jnp.int32, (rows, rows), 1)
+    upper = jnp.where(from_row <= to_row, 1.0, 0.0).astype(jnp.bfloat16)
+    sixteen = lax.broadcasted_iota(jnp.int32, (16, rows), 0)
+
+    def ranks(flags):
+        stacked = jnp.zeros((16, rows), jnp.float32)
+        for i, flag in enumerate(flags):
+            stacked = jnp.where(sixteen == i, flag.astype(jnp.float32), stacked)
+        stacked = stacked.astype(jnp.bfloat16)
+        counts = jnp.dot(stacked, upper, preferred_element_type=jnp.float32).astype(jnp.int32)
+        totals = jnp.dot(stacked, jnp.ones_like(upper), preferred_element_type=jnp.float32).astype(jnp.int32)
+        rows_of = range(len(flags))
+        return [counts[i : i + 1, :] - 1 for i in rows_of], [totals[i : i + 1, :] for i in rows_of]
+
+    up, down, across = named
+    kinds = (across * up * (1 - down), across * (1 - up) * (1 - down), across * up * down, across * (1 - up) * down)
+    (only_up, neither, both, only_down), (n_up, n_neither, n_both, n_down) = ranks(kinds)
+    early = lax.shift_right_logical(n_neither + 1, 1)
+    on_line = jnp.where(
+        kinds[0] > 0,
+        only_up,
+        jnp.where(
+            kinds[1] > 0,
+            n_up + neither + jnp.where(neither < early, 0, n_both),
+            jnp.where(kinds[2] > 0, n_up + early + both, n_up + n_neither + n_both + only_down),
+        ),
+    )
+    middle = lax.shift_right_logical(n_up + n_neither + n_both + n_down + 1, 1)
+    ahead = across * jnp.where(on_line < middle, 1, 0)
+    firsts = (ahead, across - ahead)
+    sets = []
+    for first, near in zip(firsts, (up, down)):
+        second = near * (1 - first)
+        sets += [first, second, (1 - first) * (1 - second)]
+    places, totals = ranks(sets)
+    for i in range(2):
+        target = jnp.where(
+            sets[3 * i] > 0,
+            places[3 * i],
+            totals[3 * i]
+            + jnp.where(sets[3 * i + 1] > 0, places[3 * i + 1], totals[3 * i + 1] + places[3 * i + 2]),
+        )
+        orders[i][...] = jnp.where(from_row == target, 1.0, 0.0).astype(jnp.bfloat16)
+    table_out[...] = table.T.astype(jnp.bfloat16)
+    blocks = up_block, down_block
+    far = (sublane >= first_experts[2]) & (sublane < first_experts[2] + per_group)
+    for block, order, first in zip(blocks, orders, firsts):
+        mine = jnp.where(far & (first == 0), 0.0, table).astype(jnp.bfloat16)
+        block[:, 2 * width :] = lax.dot_general(order[...], mine, NT, preferred_element_type=jnp.float32).astype(
+            jnp.bfloat16
+        )
     for copy in large:
         copy.wait()
-
-
-def pack(tokens, cotangent, ids, weights):
+    for block, order in zip(blocks, orders):
+        for lanes in (slice(0, width), slice(width, 2 * width)):
+            block[:, lanes] = jnp.dot(order[...], rows_here[:, lanes], preferred_element_type=jnp.float32).astype(
+                jnp.bfloat16
+            )
+
+
+def pack(per_group, tokens, cotangent, ids, weights):
     rows, width = tokens.shape
+    shape = (rows, 2 * width + LANES)
+    order = jax.ShapeDtypeStruct((rows, rows), jnp.bfloat16)
     return pl.pallas_call(
-        pack_kernel,
-        out_shape=pltpu.VMEM((rows, 2 * width + LANES), jnp.bfloat16),
+        functools.partial(pack_kernel, per_group),
+        out_shape=(
+            jax.ShapeDtypeStruct(shape, jnp.bfloat16),
+            jax.ShapeDtypeStruct(shape, jnp.bfloat16),
+            jax.ShapeDtypeStruct((rows, LANES), jnp.bfloat16),
+            order,
+            order,
+        ),
         in_specs=[ANYWHERE] * 4,
-        out_specs=IN_VMEM,
+        out_specs=(IN_VMEM,) * 5,
         scratch_shapes=[
             pltpu.VMEM((ids.shape[1], rows), jnp.int32),
             pltpu.VMEM((ids.shape[1], rows), jnp.bfloat16),
+            pltpu.VMEM((rows, 2 * width), jnp.bfloat16),
             pltpu.SemaphoreType.DMA((4,)),
         ],
-        compiler_params=pltpu.CompilerParams(vmem_limit_bytes=8 * MIB),
+        compiler_params=pltpu.CompilerParams(vmem_limit_bytes=7 * MIB),
     )(*(in_hbm(a) for a in (tokens, cotangent, ids.T, weights.T)))
 
 
@@ -273,17 +354,24 @@
     )(after_this, gate, up, down)
 
 
-def experts_kernel(pieces, place, after_this, *refs):
+def experts_kernel(inputs, pieces, unrolled, place, after_this, *refs):
     del after_this
-    packed, refs = refs[:pieces], refs[pieces:]
+    given, refs = refs[:inputs], refs[inputs:]
     loaded, refs = (refs[:3], refs[3:6]), refs[6:]
     outs, token = refs[:pieces], refs[pieces]
     token[...] = jnp.zeros_like(token)
     per_device, width, both_hidden = loaded[0][0].shape
     hidden = both_hidden // 2
-    x = jnp.concatenate([a[:, :width] for a in packed], axis=0)
-    g = jnp.concatenate([a[:, width : 2 * width] for a in packed], axis=0)
-    table = jnp.concatenate([a[:, 2 * width :] for a in packed], axis=0).astype(jnp.float32)
+    if inputs == pieces:
+        x = jnp.concatenate([a[:, :width] for a in given], axis=0)
+        g = jnp.concatenate([a[:, width : 2 * width] for a in given], axis=0)
+        table = jnp.concatenate([a[:, 2 * width :] for a in given], axis=0)
+    else:
+        x, g, table = (a[...] for a in given)
+    spare = -x.shape[0] % LANES
+    if spare:
+        x, g, table = (jnp.concatenate([a, jnp.zeros((spare, a.shape[1]), a.dtype)], axis=0) for a in (x, g, table))
+    table = table.astype(jnp.float32)
     lane = lax.broadcasted_iota(jnp.int32, table.shape, 1)
     route = jnp.zeros(table.shape, jnp.float32)
     grads = []
@@ -302,7 +390,7 @@
             route_grad = jnp.sum(back_up * silu, axis=1, keepdims=True)
             mine.append((weight * back_up * sig * (1.0 + gate_act * (1.0 - sig))).astype(jnp.bfloat16))
             mine.append((weight * back * silu).astype(jnp.bfloat16))
-            route += jnp.where(lane == column, route_grad, 0.0)
+            route += jnp.where((lane == column) & (weight > 0.0), route_grad, 0.0)
         grads.append(jnp.concatenate(mine, axis=1))
     step = 4 * LANES
 
@@ -317,36 +405,34 @@
             start += out.shape[0]
         return carry
 
-    lax.fori_loop(0, width // step, chunk, 0)
+    lax.fori_loop(0, width // step, chunk, 0, unroll=unrolled)
     start = 0
     for out in outs:
         out[:, width:] = route[start : start + out.shape[0]].astype(out.dtype)
         start += out.shape[0]
 
 
-def experts_call(place, after_this, packed, loaded):
+def experts_call(place, after_this, given, rows, loaded, unrolled):
     width = loaded[0].shape[1]
     return pl.pallas_call(
-        functools.partial(experts_kernel, len(packed)),
-        out_shape=[jax.ShapeDtypeStruct((a.shape[0], width + LANES), jnp.bfloat16) for a in packed] + [TOKEN],
-        in_specs=[IN_SMEM, ANYWHERE] + [IN_VMEM] * (len(packed) + 6),
-        out_specs=[IN_VMEM] * (len(packed) + 1),
+        functools.partial(experts_kernel, len(given), len(rows), unrolled),
+        out_shape=[jax.ShapeDtypeStruct((r, width + LANES), jnp.bfloat16) for r in rows] + [TOKEN],
+        in_specs=[IN_SMEM, ANYWHERE] + [IN_VMEM] * (len(given) + 6),
+        out_specs=[IN_VMEM] * (len(rows) + 1),
         compiler_params=pltpu.CompilerParams(vmem_limit_bytes=12 * MIB),
         cost_estimate=pl.CostEstimate(flops=1, bytes_accessed=1, transcendentals=0),
-    )(place, after_this, *(in_vmem(a) for a in packed), *loaded)
-
-
-def finish_kernel(ids, mine, top0, top1, low0, low1, grad_tokens, grad_weights):
-    rows, width = grad_tokens.shape
-    cut = rows // 2
-    routes = []
-    for start, terms in ((0, (top0, top1)), (cut, (low0, low1))):
-        summed = mine[start : start + cut, :].astype(jnp.float32)
-        for term in terms:
-            summed += term[...].astype(jnp.float32)
-        grad_tokens[start : start + cut, :] = summed[:, :width].astype(grad_tokens.dtype)
-        routes.append(summed[:, width:])
-    route = jnp.concatenate(routes, axis=0).T
+    )(place, after_this, *(in_vmem(a) for a in given), *loaded)
+
+
+def finish_kernel(ids, order_up, order_down, mine, long_up, short_up, long_down, short_down, grad_tokens, grad_weights):
+    width = grad_tokens.shape[1]
+    backs = order_up[...].T, order_down[...].T
+    came = tuple(jnp.concatenate([a[...], b[...]], axis=0) for a, b in ((long_up, short_up), (long_down, short_down)))
+    summed = mine[...].astype(jnp.float32)
+    for back, rows in zip(backs, came):
+        summed += jnp.dot(back, rows, preferred_element_type=jnp.float32)
+    grad_tokens[...] = summed[:, :width].astype(grad_tokens.dtype)
+    route = summed[:, width:].T
     expert = lax.broadcasted_iota(jnp.int32, route.shape, 0)
     found = [
         jnp.sum(jnp.where(expert == ids[k : k + 1, :], route, 0.0), axis=0, keepdims=True) for k in range(ids.shape[0])
@@ -362,7 +448,7 @@
             jax.ShapeDtypeStruct((rows, width), jnp.bfloat16),
             jax.ShapeDtypeStruct((top, rows), jnp.bfloat16),
         ),
-        in_specs=[IN_VMEM] * 6,
+        in_specs=[IN_VMEM] * 8,
         out_specs=(IN_VMEM, IN_VMEM),
         compiler_params=pltpu.CompilerParams(vmem_limit_bytes=12 * MIB),
     )(ids.T, *terms)
@@ -370,7 +456,10 @@
 
 
 def add_kernel(a, b, out):
-    out[...] = (a[...].astype(jnp.float32) + b[...].astype(jnp.float32)).astype(out.dtype)
+    rows = b.shape[0]
+    if rows < a.shape[0]:
+        out[rows:, :] = a[rows:, :]
+    out[:rows, :] = (a[:rows, :].astype(jnp.float32) + b[...].astype(jnp.float32)).astype(out.dtype)
 
 
 def added(a, b):
@@ -405,25 +494,29 @@
 
     own = (gate_weight, up_weight, down_weight)
     other = [lax.ppermute(a, "loc", [(i, loc_total - 1 - i) for i in range(loc_total)]) for a in own]
-    block = pack(tokens, cotangent, expert_ids, route_weights)
-    came = send((block, block))
-    place = jnp.stack([rank * (loc_total * per_device), loc * per_device]).astype(jnp.int32)
+    per_group = loc_total * per_device
+    place = jnp.stack([rank * per_group, loc * per_device]).astype(jnp.int32)
+    *blocks, table, order_up, order_down = pack(per_group, tokens, cotangent, expert_ids, route_weights)
+    came = send(blocks)
     *loaded, loaded_own = load(place, *(in_hbm(a) for a in own))
     *others, last = load(loaded_own, *tie(other[:2], *came), other[2])
     loaded += others
 
-    def call(after_this, *packed):
-        *parts, token = experts_call(place, after_this, packed, loaded)
+    def call(after_this, *packed, unrolled=False):
+        rows = [a.shape[0] for a in packed]
+        *parts, token = experts_call(place, after_this, packed, rows, loaded, unrolled)
         return parts, token
 
-    half, cut = ring_total // 2, block.shape[0] // 2
+    block = tokens.shape[0]
+    half, most = ring_total // 2, 6 * block // ring_total
+    cut, last_short = most // 2, block // 2
 
     def split(pair):
-        return (pair[0][:cut], pair[1][cut:]), (pair[0][cut:], pair[1][:cut])
+        return [a[:cut] for a in pair], [a[cut:] for a in pair]
 
     long, short = split(came)
     long_next, short_next = send(tie(long, loaded_own, *other)), send(tie(short, loaded_own, *other))
-    (mine,), last = call(last, block)
+    mine, last = experts_call(place, last, (tokens, cotangent, table), tokens.shape[:1], loaded, False)
     filler = last
     parts, last = call(last, *came)
     ahead_terms, behind_terms = split(parts)
@@ -431,30 +524,31 @@
     for s in range(2, half - 1):
         long, short = long_next, short_next
         long_next = send(tie(long, filler))
-        short_next = send(tie(short, last))
+        short_next = send(tie([a[:last_short] for a in short] if s + 2 == half else short, last))
         parts, last = call(last, long[0], short[0], long[1], short[1])
         long_terms.append((parts[0], parts[2]))
         short_terms.append((parts[1], parts[3]))
     long, short = long_next, short_next
+    parts, last = call(last, *short)
     long_last = send(tie(long, last))
+    short_back = send_back(parts)
     parts, last = call(last, *long)
     long_terms.append(tuple(parts))
-    parts, last = call(last, *short)
-    short_back = send_back(parts)
-    parts, last = call(last, *long_last)
+    parts, last = call(last, *long_last, unrolled=True)
     long_back = send_back(tie(parts, *short_back))
     for s in range(half - 1, 0, -1):
         if s < half - 1:
             short_back = send_back([added(a, b) for a, b in zip(short_terms[s], short_back)])
         long_back = send_back([added(a, b) for a, b in zip(long_terms[s], long_back)])
-    return finish(expert_ids, (mine, long_back[0], short_back[1], short_back[0], long_back[1]), width)
+    terms = (order_up, order_down, mine, long_back[0], short_back[0], long_back[1], short_back[1])
+    return finish(expert_ids, terms, width)
 
 
 def body(tokens, cotangent, expert_ids, route_weights, gate_weight, up_weight, down_weight):
     args = (tokens, cotangent, expert_ids, route_weights, gate_weight, up_weight, down_weight)
     ring_total, loc_total = lax.axis_size("grp"), lax.axis_size("loc")
     experts = ring_total * loc_total * gate_weight.shape[0]
-    if loc_total == 2 and ring_total in (6, 8) and experts <= LANES and tokens.shape[0] % 32 == 0:
+    if loc_total == 2 and ring_total == 8 and experts <= LANES and tokens.shape[0] % 32 == 0:
         return ring_body(*args)
     return routed_body(*args)
 

time: 138 us -> 131 us (0.949)
  waiting for transfers between devices: 50.2 us -> 41.5 us
  Pallas kernels: 57.1 us -> 58.7 us
    ppermute x7, waiting for transfers between devices: 5.43 us -> 0.71 us  [send_back(): lax.ppermute(pair[1], 'grp', ahead)]
    ppermute x7, starting transfers between devices: 13.7 us -> 10.5 us  [send_back(): lax.ppermute(pair[1], 'grp', ahead)]
    ppermute x7, starting transfers between devices: 1.25 us -> 4.19 us  [send_back(): lax.ppermute(pair[0], 'grp', behind)]
    ppermute x6, waiting for transfers between devices: 23.1 us -> 21.1 us  [send(): lax.ppermute(pair[0], 'grp', ahead)]
    pallas_call x7, Pallas kernels: 45.7 us -> 47.3 us  [the longest x6 44.1 us: experts_call(): pl.pallas_call(functools.partial(experts_kernel, len(given), len(rows), u...]
  transfers between devices with their start and end apart: 29 -> 29, of which waited for: 14 -> 11; matrix products, arithmetic and copies ran while one was open for 0% -> 0% of each run, Pallas kernels for 41% -> 44%
where the time goes in v2:
time: 131 us
  Pallas kernels  58.7 us (45%)
  waiting for transfers between devices  41.5 us (32%)
  starting transfers between devices  29.1 us (22%)
    pallas_call x6, Pallas kernels, experts_call(): pl.pallas_call(functools.partial(experts_kernel, len(given), len(rows), u...  44.1 us
    ppermute x6, waiting for transfers between devices, send(): lax.ppermute(pair[0], 'grp', ahead)  21.1 us
    ppermute x7, waiting for transfers between devices, send_back(): lax.ppermute(pair[0], 'grp', behind)  16.6 us
    ppermute x6, starting transfers between devices, send(): lax.ppermute(pair[0], 'grp', ahead)  11.7 us
    ppermute x7, starting transfers between devices, send_back(): lax.ppermute(pair[1], 'grp', ahead)  10.5 us
    pallas_call x2, Pallas kernels, load(): pl.pallas_call(load_kernel, out_shape=(pltpu.VMEM((per_device, width, 2 *...  9.49 us
    ppermute x7, starting transfers between devices, send_back(): lax.ppermute(pair[0], 'grp', behind)  4.19 us
    pallas_call x1, Pallas kernels, pack(): pl.pallas_call(functools.partial(pack_kernel, per_group), out_shape=(jax....  3.13 us
  transfers between devices with their start and end apart: 29, of which 11 were waited for; matrix products, arithmetic and copies ran while one was open for 0% of the time, Pallas kernels for 44%

profile of v2, /device:TPU:0, one launch (start us, length us, event | category | flops | bytes accessed | tf_op | source)
XLA Modules:
  0.0 130.6 jit_solution(7550635155564081674)
XLA Ops:
  0.6 0.5 collective-permute-start
  1.2 0.4 collective-permute-start.4
  1.7 3.1 %shard_map.86 = (bf16[128,4224]{1,0:T(8,128)(2,1)}, bf16[128,4224]{1,0:T(8,128)(2,1)}, bf16[128,128]{1,0:T(8,128)(2,1)S(1)}, bf16[128,128]{1,0:T(8,128)(2,1)S(1)}, bf16[128,128]{1,0:T(8,128)(2,1)S(1)}) custom-call(bf16[128,2048]{1,0:T(8,128)(2,1)} %refs_0_.1, bf16[128,2048]{1,0:T(8,128)(2,1)} %refs_1_.1, s32[8,128]{1,0:T(8,128)} %bitcast.5, ...), custom_call_target="tpu_custom_call" | custom-call | tf_op jit(solution)/shard_map/pallas_call | solution.py:286
  4.8 2.7 %collective-permute-start.1 = (bf16[128,4224]{1,0:T(8,128)(2,1)}, bf16[128,4224]{1,0:T(8,128)(2,1)S(1)}, u32[]{:S(2)}, u32[]{:S(2)}) collective-permute-start(bf16[128,4224]{1,0:T(8,128)(2,1)} %get-tuple-element.52), channel_id=1, source_target_pairs={{0,4},{4,8},{8,12},{12,14},{14,10},{10,6},{6,2},{2,0},{1,5},{5,9},... | collective-permute-start | bytes 3244040 | tf_op jit(solution)/shard_map/ppermute | solution.py:487
  7.6 4.7 %shard_map.87 = (bf16[2,2048,768]{2,1,0:T(8,128)(2,1)S(1)}, bf16[1536,2048]{1,0:T(8,128)(2,1)S(1)}, bf16[2048,768]{1,0:T(8,128)(2,1)S(1)}, f32[8,128]{1,0:T(8,128)S(1)}) custom-call(s32[2]{0:T(128)S(1)} %pad_add_fusion.after_this.place, bf16[2,2048,384]{2,1,0:T(8,128)(2,1)} %gate.1, bf16[2,2048,384]{2,1,0:T(8,128)(2,1)} %up.1, bf16[2,384,2048]{2,1,0:T(8,128)(2,1)} %down.1), custom_call_target="tpu_custom_call" | custom-call | flops 1 | bytes 25165824 | tf_op jit(solution)/shard_map/pallas_call | solution.py:341
  12.3 19.8 %collective-permute-done.1.refs_0_ = bf16[128,4224]{1,0:T(8,128)(2,1)S(1)} collective-permute-done((bf16[128,4224]{1,0:T(8,128)(2,1)}, bf16[128,4224]{1,0:T(8,128)(2,1)S(1)}, u32[]{:S(2)}, u32[]{:S(2)}) %collective-permute-start.1) | collective-permute-done | bytes 1081376 | tf_op jit(solution)/shard_map/ppermute | solution.py:487
  32.2 1.9 %collective-permute-start.6 = (bf16[80,4224]{1,0:T(8,128)(2,1)S(1)}, bf16[80,4224]{1,0:T(8,128)(2,1)S(1)}, u32[]{:S(2)}, u32[]{:S(2)}) collective-permute-start(bf16[80,4224]{1,0:T(8,128)(2,1)S(1)} %slice.41), channel_id=1, source_target_pairs={{0,4},{4,8},{8,12},{12,14},{14,10},{10,6},{6,2},{2,0},{1,5},{5,9},... | collective-permute-start | bytes 2027528 | tf_op jit(solution)/shard_map/ppermute | solution.py:487
  34.1 0.3 collective-permute-start.8
  34.4 1.9 %collective-permute-start.5 = (bf16[48,4224]{1,0:T(8,128)(2,1)S(1)}, bf16[48,4224]{1,0:T(8,128)(2,1)S(1)}, u32[]{:S(2)}, u32[]{:S(2)}) collective-permute-start(bf16[48,4224]{1,0:T(8,128)(2,1)S(1)} %slice.40), channel_id=1, source_target_pairs={{0,4},{4,8},{8,12},{12,14},{14,10},{10,6},{6,2},{2,0},{1,5},{5,9},... | collective-permute-start | bytes 1216520 | tf_op jit(solution)/shard_map/ppermute | solution.py:487
  36.4 0.4 collective-permute-start.7
  36.8 4.7 %shard_map.88 = (bf16[2,2048,768]{2,1,0:T(8,128)(2,1)S(1)}, bf16[1536,2048]{1,0:T(8,128)(2,1)S(1)}, bf16[2048,768]{1,0:T(8,128)(2,1)S(1)}, f32[8,128]{1,0:T(8,128)S(1)}) custom-call(f32[8,128]{1,0:T(8,128)S(1)} %get-tuple-element.51.after_this, bf16[2,2048,384]{2,1,0:T(8,128)(2,1)} %collective-permute-done.gate, ...), custom_call_target="tpu_custom_call" | custom-call | flops 1 | bytes 25165824 | tf_op jit(solution)/shard_map/pallas_call | solution.py:341
  41.6 6.2 %shard_map.89 = (bf16[128,2176]{1,0:T(8,128)(2,1)S(1)}, f32[8,128]{1,0:T(8,128)S(1)}) custom-call(s32[2]{0:T(128)S(1)} %pad_add_fusion.after_this.place, f32[8,128]{1,0:T(8,128)S(1)} %get-tuple-element.56.after_this, bf16[128,2048]{1,0:T(8,128)(2,1)S(1)} %copy-done.4, bf16[128,2048]{1,0:T(8,128)(2,1)S(1)} %copy-done.5, ...), custom_call_target="tpu_custom_call" | custom-call | flops 1 | bytes 1 | tf_op jit(solution)/shard_map/pallas_call | solution.py:417
  47.8 10.1 %shard_map.90 = (bf16[128,2176]{1,0:T(8,128)(2,1)S(1)}, bf16[128,2176]{1,0:T(8,128)(2,1)S(1)}, f32[8,128]{1,0:T(8,128)S(1)}) custom-call(s32[2]{0:T(128)S(1)} %pad_add_fusion.after_this.place, f32[8,128]{1,0:T(8,128)S(1)} %get-tuple-element.65.after_this, bf16[128,4224]{1,0:T(8,128)(2,1)S(1)} %copy-done.1, bf16[128,4224]{1,0:T(8,128)(2,1)S(1)} %copy-done.3, ...), custom_call_target="tpu_custom_call" | custom-call | flops 1 | bytes 1 | tf_op jit(solution)/shard_map/pallas_call | solution.py:417
  58.0 1.9 %collective-permute-start.9 = (bf16[64,4224]{1,0:T(8,128)(2,1)S(1)}, bf16[64,4224]{1,0:T(8,128)(2,1)S(1)}, u32[]{:S(2)}, u32[]{:S(2)}) collective-permute-start(bf16[64,4224]{1,0:T(8,128)(2,1)S(1)} %slice.44), channel_id=1, source_target_pairs={{0,4},{4,8},{8,12},{12,14},{14,10},{10,6},{6,2},{2,0},{1,5},{5,9},... | collective-permute-start | bytes 1622024 | tf_op jit(solution)/shard_map/ppermute | solution.py:487
  59.9 0.3 collective-permute-start.10
  60.2 1.8 %collective-permute-start.11 = (bf16[48,4224]{1,0:T(8,128)(2,1)S(1)}, bf16[48,4224]{1,0:T(8,128)(2,1)S(1)}, u32[]{:S(2)}, u32[]{:S(2)}) collective-permute-start(bf16[48,4224]{1,0:T(8,128)(2,1)S(1)} %collective-permute-done.5.refs_0_), channel_id=1, source_target_pairs={{0,4},{4,8},{8,12},{12,14},{14,10},{10,6},{6,2},{2,0},{1,5},{5,9},... | collective-permute-start | bytes 1216520 | tf_op jit(solution)/shard_map/ppermute | solution.py:487
  62.0 0.2 collective-permute-start.12
  62.2 10.1 %shard_map.91 = (bf16[48,2176]{1,0:T(8,128)(2,1)S(1)}, bf16[80,2176]{1,0:T(8,128)(2,1)S(1)}, bf16[48,2176]{1,0:T(8,128)(2,1)S(1)}, bf16[80,2176]{1,0:T(8,128)(2,1)S(1)}, f32[8,128]{1,0:T(8,128)S(1)}) custom-call(s32[2]{0:T(128)S(1)} %pad_add_fusion.after_this.place, f32[8,128]{1,0:T(8,128)S(1)} %get-tuple-element.67.after_this, ...), custom_call_target="tpu_custom_call" | custom-call | flops 1 | bytes 1 | tf_op jit(solution)/shard_map/pallas_call | solution.py:417
  72.3 0.9 collective-permute-done.9.refs_0_
  73.2 1.9 %collective-permute-done.10.refs_1_ = bf16[64,4224]{1,0:T(8,128)(2,1)S(1)} collective-permute-done((bf16[64,4224]{1,0:T(8,128)(2,1)S(1)}, bf16[64,4224]{1,0:T(8,128)(2,1)S(1)}, u32[]{:S(2)}, u32[]{:S(2)}) %collective-permute-start.10) | collective-permute-done | bytes 540704 | tf_op jit(solution)/shard_map/ppermute | solution.py:487
  75.2 6.0 %shard_map.92 = (bf16[64,2176]{1,0:T(8,128)(2,1)S(1)}, bf16[64,2176]{1,0:T(8,128)(2,1)S(1)}, f32[8,128]{1,0:T(8,128)S(1)}) custom-call(s32[2]{0:T(128)S(1)} %pad_add_fusion.after_this.place, f32[8,128]{1,0:T(8,128)S(1)} %get-tuple-element.73.after_this, bf16[64,4224]{1,0:T(8,128)(2,1)S(1)} %collective-permute-done.9.refs_0_, ...), custom_call_target="tpu_custom_call" | custom-call | flops 1 | bytes 1 | tf_op jit(solution)/shard_map/pallas_call | solution.py:417
  81.1 1.6 %collective-permute-start.13 = (bf16[48,4224]{1,0:T(8,128)(2,1)S(1)}, bf16[48,4224]{1,0:T(8,128)(2,1)S(1)}, u32[]{:S(2)}, u32[]{:S(2)}) collective-permute-start(bf16[48,4224]{1,0:T(8,128)(2,1)S(1)} %collective-permute-done.11.refs_0_), channel_id=1, source_target_pairs={{0,4},{4,8},{8,12},{12,14},{14,10},{10,6},{6,2},{2,0},{1,5},{5,9},... | collective-permute-start | bytes 1216520 | tf_op jit(solution)/shard_map/ppermute | solution.py:487
  82.8 0.5 collective-permute-start.14
  83.2 0.2 collective-permute-start.15
  83.4 1.8 %collective-permute-start.16 = (bf16[64,2176]{1,0:T(8,128)(2,1)S(1)}, bf16[64,2176]{1,0:T(8,128)(2,1)S(1)}, u32[]{:S(2)}, u32[]{:S(2)}) collective-permute-start(bf16[64,2176]{1,0:T(8,128)(2,1)S(1)} %get-tuple-element.85), channel_id=1, source_target_pairs={{0,4},{4,8},{8,12},{12,14},{14,10},{10,6},{6,2},{2,0},{1,5},{5,9},... | collective-permute-start | bytes 835592 | tf_op jit(solution)/shard_map/ppermute | solution.py:490
  85.3 6.0 %shard_map.93 = (bf16[48,2176]{1,0:T(8,128)(2,1)S(1)}, bf16[48,2176]{1,0:T(8,128)(2,1)S(1)}, f32[8,128]{1,0:T(8,128)S(1)}) custom-call(s32[2]{0:T(128)S(1)} %pad_add_fusion.after_this.place, f32[8,128]{1,0:T(8,128)S(1)} %get-tuple-element.76.after_this, bf16[48,4224]{1,0:T(8,128)(2,1)S(1)} %collective-permute-done.11.refs_0_, ...), custom_call_target="tpu_custom_call" | custom-call | flops 1 | bytes 1 | tf_op jit(solution)/shard_map/pallas_call | solution.py:417
  91.3 0.4 collective-permute-done.13.refs_0_
  91.7 1.1 collective-permute-done.14.refs_1_
  92.8 5.7 %shard_map.94 = (bf16[48,2176]{1,0:T(8,128)(2,1)S(1)}, bf16[48,2176]{1,0:T(8,128)(2,1)S(1)}, f32[8,128]{1,0:T(8,128)}) custom-call(s32[2]{0:T(128)S(1)} %pad_add_fusion.after_this.place, f32[8,128]{1,0:T(8,128)S(1)} %get-tuple-element.80.after_this, bf16[48,4224]{1,0:T(8,128)(2,1)S(1)} %collective-permute-done.13.refs_0_, ...), custom_call_target="tpu_custom_call" | custom-call | flops 1 | bytes 1 | tf_op jit(solution)/shard_map/pallas_call | solution.py:417
  98.6 0.6 collective-permute-start.17
  99.2 1.4 %collective-permute-start.23 = (bf16[48,2176]{1,0:T(8,128)(2,1)S(1)}, bf16[48,2176]{1,0:T(8,128)(2,1)S(1)}, u32[]{:S(2)}, u32[]{:S(2)}) collective-permute-start(bf16[48,2176]{1,0:T(8,128)(2,1)S(1)} %get-tuple-element.92), channel_id=1, source_target_pairs={{0,4},{4,8},{8,12},{12,14},{14,10},{10,6},{6,2},{2,0},{1,5},{5,9},... | collective-permute-start | bytes 626696 | tf_op jit(solution)/shard_map/ppermute | solution.py:490
  100.7 0.7 collective-permute-start.21
  101.4 1.5 %collective-permute-start.27 = (bf16[80,2176]{1,0:T(8,128)(2,1)S(1)}, bf16[80,2176]{1,0:T(8,128)(2,1)S(1)}, u32[]{:S(2)}, u32[]{:S(2)}) collective-permute-start(bf16[80,2176]{1,0:T(8,128)(2,1)S(1)} %shard_map.103), channel_id=1, source_target_pairs={{0,4},{4,8},{8,12},{12,14},{14,10},{10,6},{6,2},{2,0},{1,5},{5,9},... | collective-permute-start | bytes 1044488 | tf_op jit(solution)/shard_map/ppermute | solution.py:490
  102.9 3.4 %collective-permute-done.17.b = bf16[48,2176]{1,0:T(8,128)(2,1)S(1)} collective-permute-done((bf16[48,2176]{1,0:T(8,128)(2,1)S(1)}, bf16[48,2176]{1,0:T(8,128)(2,1)S(1)}, u32[]{:S(2)}, u32[]{:S(2)}) %collective-permute-start.17) | collective-permute-done | bytes 208928 | tf_op jit(solution)/shard_map/ppermute | solution.py:490
  106.3 0.7 collective-permute-start.18
  107.1 1.5 %collective-permute-start.24 = (bf16[48,2176]{1,0:T(8,128)(2,1)S(1)}, bf16[48,2176]{1,0:T(8,128)(2,1)S(1)}, u32[]{:S(2)}, u32[]{:S(2)}) collective-permute-start(bf16[48,2176]{1,0:T(8,128)(2,1)S(1)} %shard_map.100), channel_id=1, source_target_pairs={{0,4},{4,8},{8,12},{12,14},{14,10},{10,6},{6,2},{2,0},{1,5},{5,9},... | collective-permute-start | bytes 626696 | tf_op jit(solution)/shard_map/ppermute | solution.py:490
  108.5 7.2 %collective-permute-done.18.b = bf16[48,2176]{1,0:T(8,128)(2,1)S(1)} collective-permute-done((bf16[48,2176]{1,0:T(8,128)(2,1)S(1)}, bf16[48,2176]{1,0:T(8,128)(2,1)S(1)}, u32[]{:S(2)}, u32[]{:S(2)}) %collective-permute-start.18) | collective-permute-done | bytes 208928 | tf_op jit(solution)/shard_map/ppermute | solution.py:490
  115.8 0.7 collective-permute-start.19
  116.5 1.5 %collective-permute-start.25 = (bf16[48,2176]{1,0:T(8,128)(2,1)S(1)}, bf16[48,2176]{1,0:T(8,128)(2,1)S(1)}, u32[]{:S(2)}, u32[]{:S(2)}) collective-permute-start(bf16[48,2176]{1,0:T(8,128)(2,1)S(1)} %shard_map.101), channel_id=1, source_target_pairs={{0,4},{4,8},{8,12},{12,14},{14,10},{10,6},{6,2},{2,0},{1,5},{5,9},... | collective-permute-start | bytes 626696 | tf_op jit(solution)/shard_map/ppermute | solution.py:490
  118.2 0.7 collective-permute-start.22
  118.9 1.5 %collective-permute-start.28 = (bf16[80,2176]{1,0:T(8,128)(2,1)S(1)}, bf16[80,2176]{1,0:T(8,128)(2,1)S(1)}, u32[]{:S(2)}, u32[]{:S(2)}) collective-permute-start(bf16[80,2176]{1,0:T(8,128)(2,1)S(1)} %shard_map.104), channel_id=1, source_target_pairs={{0,4},{4,8},{8,12},{12,14},{14,10},{10,6},{6,2},{2,0},{1,5},{5,9},... | collective-permute-start | bytes 1044488 | tf_op jit(solution)/shard_map/ppermute | solution.py:490
  120.4 2.3 %collective-permute-done.19.b = bf16[48,2176]{1,0:T(8,128)(2,1)S(1)} collective-permute-done((bf16[48,2176]{1,0:T(8,128)(2,1)S(1)}, bf16[48,2176]{1,0:T(8,128)(2,1)S(1)}, u32[]{:S(2)}, u32[]{:S(2)}) %collective-permute-start.19) | collective-permute-done | bytes 208928 | tf_op jit(solution)/shard_map/ppermute | solution.py:490
  122.7 0.7 collective-permute-start.20
  123.5 1.5 %collective-permute-start.26 = (bf16[48,2176]{1,0:T(8,128)(2,1)S(1)}, bf16[48,2176]{1,0:T(8,128)(2,1)S(1)}, u32[]{:S(2)}, u32[]{:S(2)}) collective-permute-start(bf16[48,2176]{1,0:T(8,128)(2,1)S(1)} %shard_map.102), channel_id=1, source_target_pairs={{0,4},{4,8},{8,12},{12,14},{14,10},{10,6},{6,2},{2,0},{1,5},{5,9},... | collective-permute-start | bytes 626696 | tf_op jit(solution)/shard_map/ppermute | solution.py:490
  124.9 1.5 %collective-permute-done.22.short_up = bf16[80,2176]{1,0:T(8,128)(2,1)S(1)} collective-permute-done((bf16[80,2176]{1,0:T(8,128)(2,1)S(1)}, bf16[80,2176]{1,0:T(8,128)(2,1)S(1)}, u32[]{:S(2)}, u32[]{:S(2)}) %collective-permute-start.22) | collective-permute-done | bytes 348192 | tf_op jit(solution)/shard_map/ppermute | solution.py:490
  126.4 2.2 %collective-permute-done.20.long_up = bf16[48,2176]{1,0:T(8,128)(2,1)S(1)} collective-permute-done((bf16[48,2176]{1,0:T(8,128)(2,1)S(1)}, bf16[48,2176]{1,0:T(8,128)(2,1)S(1)}, u32[]{:S(2)}, u32[]{:S(2)}) %collective-permute-start.20) | collective-permute-done | bytes 208928 | tf_op jit(solution)/shard_map/ppermute | solution.py:490
  128.7 0.7 collective-permute-done.26.long_down
  129.3 1.3 shard_map.105
  (55 shorter events, 1.2 us)
Async XLA Ops:
  0.6 31.5 %collective-permute-start = (bf16[2,2048,384]{2,1,0:T(8,128)(2,1)}, bf16[2,2048,384]{2,1,0:T(8,128)(2,1)}, u32[]{:S(2)}, u32[]{:S(2)}) collective-permute-start(bf16[2,2048,384]{2,1,0:T(8,128)(2,1)} %gate.1), channel_id=1, source_target_pairs={{0,1},{1,0},{2,3},{3,2},{4,5},{5,4},{6,7},{7,6},{8,9},{9,8},{10,11... | collective-permute-start | bytes 9437192 | tf_op jit(solution)/shard_map/ppermute | solution.py:496
  1.1 31.0 %collective-permute-start.3 = (bf16[2,2048,384]{2,1,0:T(8,128)(2,1)}, bf16[2,2048,384]{2,1,0:T(8,128)(2,1)}, u32[]{:S(2)}, u32[]{:S(2)}) collective-permute-start(bf16[2,2048,384]{2,1,0:T(8,128)(2,1)} %up.1), channel_id=1, source_target_pairs={{0,1},{1,0},{2,3},{3,2},{4,5},{5,4},{6,7},{7,6},{8,9},{9,8},{10,11... | collective-permute-start | bytes 9437192 | tf_op jit(solution)/shard_map/ppermute | solution.py:496
  1.2 31.0 %collective-permute-start.4 = (bf16[2,384,2048]{2,1,0:T(8,128)(2,1)}, bf16[2,384,2048]{2,1,0:T(8,128)(2,1)}, u32[]{:S(2)}, u32[]{:S(2)}) collective-permute-start(bf16[2,384,2048]{2,1,0:T(8,128)(2,1)} %down.1), channel_id=1, source_target_pairs={{0,1},{1,0},{2,3},{3,2},{4,5},{5,4},{6,7},{7,6},{8,9},{9,8},{10,11... | collective-permute-start | bytes 9437192 | tf_op jit(solution)/shard_map/ppermute | solution.py:496
  4.8 27.3 %collective-permute-start.1 = (bf16[128,4224]{1,0:T(8,128)(2,1)}, bf16[128,4224]{1,0:T(8,128)(2,1)S(1)}, u32[]{:S(2)}, u32[]{:S(2)}) collective-permute-start(bf16[128,4224]{1,0:T(8,128)(2,1)} %get-tuple-element.52), channel_id=1, source_target_pairs={{0,4},{4,8},{8,12},{12,14},{14,10},{10,6},{6,2},{2,0},{1,5},{5,9},... | collective-permute-start | bytes 3244040 | tf_op jit(solution)/shard_map/ppermute | solution.py:487
  7.5 26.6 %collective-permute-start.2 = (bf16[128,4224]{1,0:T(8,128)(2,1)}, bf16[128,4224]{1,0:T(8,128)(2,1)S(1)}, u32[]{:S(2)}, u32[]{:S(2)}) collective-permute-start(bf16[128,4224]{1,0:T(8,128)(2,1)} %get-tuple-element.53), channel_id=1, source_target_pairs={{4,0},{8,4},{12,8},{14,12},{10,14},{6,10},{2,6},{0,2},{5,1},{9,5},... | collective-permute-start | bytes 3244040 | tf_op jit(solution)/shard_map/ppermute | solution.py:487
  32.1 4.2 %copy-start = (bf16[128,4224]{1,0:T(8,128)(2,1)}, bf16[128,4224]{1,0:T(8,128)(2,1)S(1)}, u32[]{:S(2)}) copy-start(bf16[128,4224]{1,0:T(8,128)(2,1)S(1)} %collective-permute-done.1.refs_0_) | copy-start | bytes 3244036
  32.2 25.7 %collective-permute-start.6 = (bf16[80,4224]{1,0:T(8,128)(2,1)S(1)}, bf16[80,4224]{1,0:T(8,128)(2,1)S(1)}, u32[]{:S(2)}, u32[]{:S(2)}) collective-permute-start(bf16[80,4224]{1,0:T(8,128)(2,1)S(1)} %slice.41), channel_id=1, source_target_pairs={{0,4},{4,8},{8,12},{12,14},{14,10},{10,6},{6,2},{2,0},{1,5},{5,9},... | collective-permute-start | bytes 2027528 | tf_op jit(solution)/shard_map/ppermute | solution.py:487
  34.1 2.3 %copy-start.2 = (bf16[128,4224]{1,0:T(8,128)(2,1)}, bf16[128,4224]{1,0:T(8,128)(2,1)S(1)}, u32[]{:S(2)}) copy-start(bf16[128,4224]{1,0:T(8,128)(2,1)S(1)} %collective-permute-done.2.refs_1_) | copy-start | bytes 3244036
  34.1 25.7 %collective-permute-start.8 = (bf16[80,4224]{1,0:T(8,128)(2,1)S(1)}, bf16[80,4224]{1,0:T(8,128)(2,1)S(1)}, u32[]{:S(2)}, u32[]{:S(2)}) collective-permute-start(bf16[80,4224]{1,0:T(8,128)(2,1)S(1)} %slice.43), channel_id=1, source_target_pairs={{4,0},{8,4},{12,8},{14,12},{10,14},{6,10},{2,6},{0,2},{5,1},{9,5},... | collective-permute-start | bytes 2027528 | tf_op jit(solution)/shard_map/ppermute | solution.py:487
  34.4 25.7 %collective-permute-start.5 = (bf16[48,4224]{1,0:T(8,128)(2,1)S(1)}, bf16[48,4224]{1,0:T(8,128)(2,1)S(1)}, u32[]{:S(2)}, u32[]{:S(2)}) collective-permute-start(bf16[48,4224]{1,0:T(8,128)(2,1)S(1)} %slice.40), channel_id=1, source_target_pairs={{0,4},{4,8},{8,12},{12,14},{14,10},{10,6},{6,2},{2,0},{1,5},{5,9},... | collective-permute-start | bytes 1216520 | tf_op jit(solution)/shard_map/ppermute | solution.py:487
  36.3 5.2 %copy-start.4 = (bf16[128,2048]{1,0:T(8,128)(2,1)S(1)}, bf16[128,2048]{1,0:T(8,128)(2,1)}, u32[]{:S(2)}) copy-start(bf16[128,2048]{1,0:T(8,128)(2,1)} %refs_0_.1) | copy-start | bytes 1572868
  36.3 5.2 %copy-start.5 = (bf16[128,2048]{1,0:T(8,128)(2,1)S(1)}, bf16[128,2048]{1,0:T(8,128)(2,1)}, u32[]{:S(2)}) copy-start(bf16[128,2048]{1,0:T(8,128)(2,1)} %refs_1_.1) | copy-start | bytes 1572868
  36.4 25.6 %collective-permute-start.7 = (bf16[48,4224]{1,0:T(8,128)(2,1)S(1)}, bf16[48,4224]{1,0:T(8,128)(2,1)S(1)}, u32[]{:S(2)}, u32[]{:S(2)}) collective-permute-start(bf16[48,4224]{1,0:T(8,128)(2,1)S(1)} %slice.42), channel_id=1, source_target_pairs={{4,0},{8,4},{12,8},{14,12},{10,14},{6,10},{2,6},{0,2},{5,1},{9,5},... | collective-permute-start | bytes 1216520 | tf_op jit(solution)/shard_map/ppermute | solution.py:487
  41.6 6.2 %copy-start.1 = (bf16[128,4224]{1,0:T(8,128)(2,1)S(1)}, bf16[128,4224]{1,0:T(8,128)(2,1)}, u32[]{:S(2)}) copy-start(bf16[128,4224]{1,0:T(8,128)(2,1)} %copy-done) | copy-start | bytes 3244036
  41.6 6.2 %copy-start.3 = (bf16[128,4224]{1,0:T(8,128)(2,1)S(1)}, bf16[128,4224]{1,0:T(8,128)(2,1)}, u32[]{:S(2)}) copy-start(bf16[128,4224]{1,0:T(8,128)(2,1)} %copy-done.2) | copy-start | bytes 3244036
  58.0 15.3 %collective-permute-start.9 = (bf16[64,4224]{1,0:T(8,128)(2,1)S(1)}, bf16[64,4224]{1,0:T(8,128)(2,1)S(1)}, u32[]{:S(2)}, u32[]{:S(2)}) collective-permute-start(bf16[64,4224]{1,0:T(8,128)(2,1)S(1)} %slice.44), channel_id=1, source_target_pairs={{0,4},{4,8},{8,12},{12,14},{14,10},{10,6},{6,2},{2,0},{1,5},{5,9},... | collective-permute-start | bytes 1622024 | tf_op jit(solution)/shard_map/ppermute | solution.py:487
  59.9 15.3 %collective-permute-start.10 = (bf16[64,4224]{1,0:T(8,128)(2,1)S(1)}, bf16[64,4224]{1,0:T(8,128)(2,1)S(1)}, u32[]{:S(2)}, u32[]{:S(2)}) collective-permute-start(bf16[64,4224]{1,0:T(8,128)(2,1)S(1)} %slice.45), channel_id=1, source_target_pairs={{4,0},{8,4},{12,8},{14,12},{10,14},{6,10},{2,6},{0,2},{5,1},{9,5},... | collective-permute-start | bytes 1622024 | tf_op jit(solution)/shard_map/ppermute | solution.py:487
  60.2 21.0 %collective-permute-start.11 = (bf16[48,4224]{1,0:T(8,128)(2,1)S(1)}, bf16[48,4224]{1,0:T(8,128)(2,1)S(1)}, u32[]{:S(2)}, u32[]{:S(2)}) collective-permute-start(bf16[48,4224]{1,0:T(8,128)(2,1)S(1)} %collective-permute-done.5.refs_0_), channel_id=1, source_target_pairs={{0,4},{4,8},{8,12},{12,14},{14,10},{10,6},{6,2},{2,0},{1,5},{5,9},... | collective-permute-start | bytes 1216520 | tf_op jit(solution)/shard_map/ppermute | solution.py:487
  62.0 20.8 %collective-permute-start.12 = (bf16[48,4224]{1,0:T(8,128)(2,1)S(1)}, bf16[48,4224]{1,0:T(8,128)(2,1)S(1)}, u32[]{:S(2)}, u32[]{:S(2)}) collective-permute-start(bf16[48,4224]{1,0:T(8,128)(2,1)S(1)} %collective-permute-done.7.refs_2_), channel_id=1, source_target_pairs={{4,0},{8,4},{12,8},{14,12},{10,14},{6,10},{2,6},{0,2},{5,1},{9,5},... | collective-permute-start | bytes 1216520 | tf_op jit(solution)/shard_map/ppermute | solution.py:487
  81.1 10.6 %collective-permute-start.13 = (bf16[48,4224]{1,0:T(8,128)(2,1)S(1)}, bf16[48,4224]{1,0:T(8,128)(2,1)S(1)}, u32[]{:S(2)}, u32[]{:S(2)}) collective-permute-start(bf16[48,4224]{1,0:T(8,128)(2,1)S(1)} %collective-permute-done.11.refs_0_), channel_id=1, source_target_pairs={{0,4},{4,8},{8,12},{12,14},{14,10},{10,6},{6,2},{2,0},{1,5},{5,9},... | collective-permute-start | bytes 1216520 | tf_op jit(solution)/shard_map/ppermute | solution.py:487
  82.8 10.1 %collective-permute-start.14 = (bf16[48,4224]{1,0:T(8,128)(2,1)S(1)}, bf16[48,4224]{1,0:T(8,128)(2,1)S(1)}, u32[]{:S(2)}, u32[]{:S(2)}) collective-permute-start(bf16[48,4224]{1,0:T(8,128)(2,1)S(1)} %collective-permute-done.12.refs_1_), channel_id=1, source_target_pairs={{4,0},{8,4},{12,8},{14,12},{10,14},{6,10},{2,6},{0,2},{5,1},{9,5},... | collective-permute-start | bytes 1216520 | tf_op jit(solution)/shard_map/ppermute | solution.py:487
  83.2 15.4 %collective-permute-start.15 = (bf16[64,2176]{1,0:T(8,128)(2,1)S(1)}, bf16[64,2176]{1,0:T(8,128)(2,1)S(1)}, u32[]{:S(2)}, u32[]{:S(2)}) collective-permute-start(bf16[64,2176]{1,0:T(8,128)(2,1)S(1)} %get-tuple-element.84), channel_id=1, source_target_pairs={{4,0},{8,4},{12,8},{14,12},{10,14},{6,10},{2,6},{0,2},{5,1},{9,5},... | collective-permute-start | bytes 835592 | tf_op jit(solution)/shard_map/ppermute | solution.py:490
  83.4 15.2 %collective-permute-start.16 = (bf16[64,2176]{1,0:T(8,128)(2,1)S(1)}, bf16[64,2176]{1,0:T(8,128)(2,1)S(1)}, u32[]{:S(2)}, u32[]{:S(2)}) collective-permute-start(bf16[64,2176]{1,0:T(8,128)(2,1)S(1)} %get-tuple-element.85), channel_id=1, source_target_pairs={{0,4},{4,8},{8,12},{12,14},{14,10},{10,6},{6,2},{2,0},{1,5},{5,9},... | collective-permute-start | bytes 835592 | tf_op jit(solution)/shard_map/ppermute | solution.py:490
  98.6 7.7 %collective-permute-start.17 = (bf16[48,2176]{1,0:T(8,128)(2,1)S(1)}, bf16[48,2176]{1,0:T(8,128)(2,1)S(1)}, u32[]{:S(2)}, u32[]{:S(2)}) collective-permute-start(bf16[48,2176]{1,0:T(8,128)(2,1)S(1)} %get-tuple-element.86), channel_id=1, source_target_pairs={{4,0},{8,4},{12,8},{14,12},{10,14},{6,10},{2,6},{0,2},{5,1},{9,5},... | collective-permute-start | bytes 626696 | tf_op jit(solution)/shard_map/ppermute | solution.py:490
  99.2 7.8 %collective-permute-start.23 = (bf16[48,2176]{1,0:T(8,128)(2,1)S(1)}, bf16[48,2176]{1,0:T(8,128)(2,1)S(1)}, u32[]{:S(2)}, u32[]{:S(2)}) collective-permute-start(bf16[48,2176]{1,0:T(8,128)(2,1)S(1)} %get-tuple-element.92), channel_id=1, source_target_pairs={{0,4},{4,8},{8,12},{12,14},{14,10},{10,6},{6,2},{2,0},{1,5},{5,9},... | collective-permute-start | bytes 626696 | tf_op jit(solution)/shard_map/ppermute | solution.py:490
  100.7 17.4 %collective-permute-start.21 = (bf16[80,2176]{1,0:T(8,128)(2,1)S(1)}, bf16[80,2176]{1,0:T(8,128)(2,1)S(1)}, u32[]{:S(2)}, u32[]{:S(2)}) collective-permute-start(bf16[80,2176]{1,0:T(8,128)(2,1)S(1)} %shard_map.98), channel_id=1, source_target_pairs={{4,0},{8,4},{12,8},{14,12},{10,14},{6,10},{2,6},{0,2},{5,1},{9,5},... | collective-permute-start | bytes 1044488 | tf_op jit(solution)/shard_map/ppermute | solution.py:490
  101.4 17.4 %collective-permute-start.27 = (bf16[80,2176]{1,0:T(8,128)(2,1)S(1)}, bf16[80,2176]{1,0:T(8,128)(2,1)S(1)}, u32[]{:S(2)}, u32[]{:S(2)}) collective-permute-start(bf16[80,2176]{1,0:T(8,128)(2,1)S(1)} %shard_map.103), channel_id=1, source_target_pairs={{0,4},{4,8},{8,12},{12,14},{14,10},{10,6},{6,2},{2,0},{1,5},{5,9},... | collective-permute-start | bytes 1044488 | tf_op jit(solution)/shard_map/ppermute | solution.py:490
  106.3 9.4 %collective-permute-start.18 = (bf16[48,2176]{1,0:T(8,128)(2,1)S(1)}, bf16[48,2176]{1,0:T(8,128)(2,1)S(1)}, u32[]{:S(2)}, u32[]{:S(2)}) collective-permute-start(bf16[48,2176]{1,0:T(8,128)(2,1)S(1)} %shard_map.95), channel_id=1, source_target_pairs={{4,0},{8,4},{12,8},{14,12},{10,14},{6,10},{2,6},{0,2},{5,1},{9,5},... | collective-permute-start | bytes 626696 | tf_op jit(solution)/shard_map/ppermute | solution.py:490
  107.1 9.4 %collective-permute-start.24 = (bf16[48,2176]{1,0:T(8,128)(2,1)S(1)}, bf16[48,2176]{1,0:T(8,128)(2,1)S(1)}, u32[]{:S(2)}, u32[]{:S(2)}) collective-permute-start(bf16[48,2176]{1,0:T(8,128)(2,1)S(1)} %shard_map.100), channel_id=1, source_target_pairs={{0,4},{4,8},{8,12},{12,14},{14,10},{10,6},{6,2},{2,0},{1,5},{5,9},... | collective-permute-start | bytes 626696 | tf_op jit(solution)/shard_map/ppermute | solution.py:490
  115.8 13.5 %copy-start.6 = (s32[128,8]{0,1:T(8,128)S(1)}, s32[128,8]{0,1:T(8,128)}, u32[]{:S(2)}) copy-start(s32[128,8]{0,1:T(8,128)} %param.9) | copy-start | bytes 12292
  115.8 6.9 %collective-permute-start.19 = (bf16[48,2176]{1,0:T(8,128)(2,1)S(1)}, bf16[48,2176]{1,0:T(8,128)(2,1)S(1)}, u32[]{:S(2)}, u32[]{:S(2)}) collective-permute-start(bf16[48,2176]{1,0:T(8,128)(2,1)S(1)} %shard_map.96), channel_id=1, source_target_pairs={{4,0},{8,4},{12,8},{14,12},{10,14},{6,10},{2,6},{0,2},{5,1},{9,5},... | collective-permute-start | bytes 626696 | tf_op jit(solution)/shard_map/ppermute | solution.py:490
  116.5 6.9 %collective-permute-start.25 = (bf16[48,2176]{1,0:T(8,128)(2,1)S(1)}, bf16[48,2176]{1,0:T(8,128)(2,1)S(1)}, u32[]{:S(2)}, u32[]{:S(2)}) collective-permute-start(bf16[48,2176]{1,0:T(8,128)(2,1)S(1)} %shard_map.101), channel_id=1, source_target_pairs={{0,4},{4,8},{8,12},{12,14},{14,10},{10,6},{6,2},{2,0},{1,5},{5,9},... | collective-permute-start | bytes 626696 | tf_op jit(solution)/shard_map/ppermute | solution.py:490
  118.2 8.3 %collective-permute-start.22 = (bf16[80,2176]{1,0:T(8,128)(2,1)S(1)}, bf16[80,2176]{1,0:T(8,128)(2,1)S(1)}, u32[]{:S(2)}, u32[]{:S(2)}) collective-permute-start(bf16[80,2176]{1,0:T(8,128)(2,1)S(1)} %shard_map.99), channel_id=1, source_target_pairs={{4,0},{8,4},{12,8},{14,12},{10,14},{6,10},{2,6},{0,2},{5,1},{9,5},... | collective-permute-start | bytes 1044488 | tf_op jit(solution)/shard_map/ppermute | solution.py:490
  118.9 7.5 %collective-permute-start.28 = (bf16[80,2176]{1,0:T(8,128)(2,1)S(1)}, bf16[80,2176]{1,0:T(8,128)(2,1)S(1)}, u32[]{:S(2)}, u32[]{:S(2)}) collective-permute-start(bf16[80,2176]{1,0:T(8,128)(2,1)S(1)} %shard_map.104), channel_id=1, source_target_pairs={{0,4},{4,8},{8,12},{12,14},{14,10},{10,6},{6,2},{2,0},{1,5},{5,9},... | collective-permute-start | bytes 1044488 | tf_op jit(solution)/shard_map/ppermute | solution.py:490
  122.7 5.9 %collective-permute-start.20 = (bf16[48,2176]{1,0:T(8,128)(2,1)S(1)}, bf16[48,2176]{1,0:T(8,128)(2,1)S(1)}, u32[]{:S(2)}, u32[]{:S(2)}) collective-permute-start(bf16[48,2176]{1,0:T(8,128)(2,1)S(1)} %shard_map.97), channel_id=1, source_target_pairs={{4,0},{8,4},{12,8},{14,12},{10,14},{6,10},{2,6},{0,2},{5,1},{9,5},... | collective-permute-start | bytes 626696 | tf_op jit(solution)/shard_map/ppermute | solution.py:490
  123.5 5.9 %collective-permute-start.26 = (bf16[48,2176]{1,0:T(8,128)(2,1)S(1)}, bf16[48,2176]{1,0:T(8,128)(2,1)S(1)}, u32[]{:S(2)}, u32[]{:S(2)}) collective-permute-start(bf16[48,2176]{1,0:T(8,128)(2,1)S(1)} %shard_map.102), channel_id=1, source_target_pairs={{0,4},{4,8},{8,12},{12,14},{14,10},{10,6},{6,2},{2,0},{1,5},{5,9},... | collective-permute-start | bytes 626696 | tf_op jit(solution)/shard_map/ppermute | solution.py:490

commit v3 on v2

--- a/solution.py
+++ b/solution.py
@@ -362,13 +362,13 @@
     token[...] = jnp.zeros_like(token)
     per_device, width, both_hidden = loaded[0][0].shape
     hidden = both_hidden // 2
-    if inputs == pieces:
+    if given[0].shape[1] > width:
         x = jnp.concatenate([a[:, :width] for a in given], axis=0)
         g = jnp.concatenate([a[:, width : 2 * width] for a in given], axis=0)
         table = jnp.concatenate([a[:, 2 * width :] for a in given], axis=0)
     else:
         x, g, table = (a[...] for a in given)
-    spare = -x.shape[0] % LANES
+    spare = -x.shape[0] % (LANES // 2)
     if spare:
         x, g, table = (jnp.concatenate([a, jnp.zeros((spare, a.shape[1]), a.dtype)], axis=0) for a in (x, g, table))
     table = table.astype(jnp.float32)
@@ -462,6 +462,23 @@
     out[:rows, :] = (a[:rows, :].astype(jnp.float32) + b[...].astype(jnp.float32)).astype(out.dtype)
 
 
+def join_kernel(a, b, out):
+    rows = a.shape[0]
+    out[:rows, :] = a[...]
+    out[rows:, :] = b[...]
+
+
+def joined(a, b):
+    return pl.pallas_call(
+        join_kernel,
+        out_shape=jax.ShapeDtypeStruct((a.shape[0] + b.shape[0], a.shape[1]), a.dtype),
+        in_specs=[IN_VMEM] * 2,
+        out_specs=IN_VMEM,
+        compiler_params=pltpu.CompilerParams(vmem_limit_bytes=8 * MIB),
+        cost_estimate=pl.CostEstimate(flops=1, bytes_accessed=1, transcendentals=0),
+    )(a, b)
+
+
 def added(a, b):
     return pl.pallas_call(
         add_kernel,
@@ -502,39 +519,35 @@
     *others, last = load(loaded_own, *tie(other[:2], *came), other[2])
     loaded += others
 
-    def call(after_this, *packed, unrolled=False):
-        rows = [a.shape[0] for a in packed]
+    def call(after_this, rows, *packed, unrolled=False):
         *parts, token = experts_call(place, after_this, packed, rows, loaded, unrolled)
         return parts, token
 
     block = tokens.shape[0]
     half, most = ring_total // 2, 6 * block // ring_total
-    cut, last_short = most // 2, block // 2
-
-    def split(pair):
-        return [a[:cut] for a in pair], [a[cut:] for a in pair]
-
-    long, short = split(came)
+    half_block, cut = block // 2, most // 2
+    rest, needed = block - cut, (block + most) // 2 - half_block
+    long, short = [a[:half_block] for a in came], [a[half_block:] for a in came]
     long_next, short_next = send(tie(long, loaded_own, *other)), send(tie(short, loaded_own, *other))
     mine, last = experts_call(place, last, (tokens, cotangent, table), tokens.shape[:1], loaded, False)
     filler = last
-    parts, last = call(last, *came)
-    ahead_terms, behind_terms = split(parts)
-    long_terms, short_terms = [None, ahead_terms], [None, behind_terms]
+    parts, last = call(last, (block, block), *came)
+    long_terms, short_terms = [None, [a[:cut] for a in parts]], [None, [a[cut:] for a in parts]]
     for s in range(2, half - 1):
         long, short = long_next, short_next
         long_next = send(tie(long, filler))
-        short_next = send(tie([a[:last_short] for a in short] if s + 2 == half else short, last))
-        parts, last = call(last, long[0], short[0], long[1], short[1])
+        short_next = send(tie([a[:needed] for a in short] if s + 2 == half else short, last))
+        parts, last = call(last, (cut, rest, cut, rest), long[0], short[0], long[1], short[1])
         long_terms.append((parts[0], parts[2]))
         short_terms.append((parts[1], parts[3]))
     long, short = long_next, short_next
-    parts, last = call(last, *short)
-    long_last = send(tie(long, last))
-    short_back = send_back(parts)
-    parts, last = call(last, *long)
-    long_terms.append(tuple(parts))
-    parts, last = call(last, *long_last, unrolled=True)
+    long_last = send(tie([a[:cut] for a in long], last))
+    parts, last = call(last, (cut, half_block - cut) * 2, *long)
+    long_terms.append((parts[0], parts[2]))
+    lower = parts[1], parts[3]
+    parts, last = call(last, (needed, needed), *short, unrolled=True)
+    short_back = send_back([joined(a, b) for a, b in zip(lower, parts)])
+    parts, last = call(last, (cut, cut), *long_last, unrolled=True)
     long_back = send_back(tie(parts, *short_back))
     for s in range(half - 1, 0, -1):
         if s < half - 1:

time: 131 us -> 129 us (0.985)
    ppermute x7, waiting for transfers between devices: 16.6 us -> 18.4 us  [send_back(): lax.ppermute(pair[0], 'grp', behind)]
    ppermute x7, starting transfers between devices: 10.5 us -> 12 us  [send_back(): lax.ppermute(pair[1], 'grp', ahead)]
    ppermute x6, waiting for transfers between devices: 21.1 us -> 19.8 us  [send(): lax.ppermute(pair[0], 'grp', ahead)]
where the time goes in v3:
time: 129 us
  Pallas kernels  57.6 us (45%)
  waiting for transfers between devices  40.8 us (32%)
  starting transfers between devices  29.4 us (23%)
    pallas_call x6, Pallas kernels, experts_call(): pl.pallas_call(functools.partial(experts_kernel, len(given), len(rows), u...  43.4 us
    ppermute x6, waiting for transfers between devices, send(): lax.ppermute(pair[0], 'grp', ahead)  19.8 us
    ppermute x7, waiting for transfers between devices, send_back(): lax.ppermute(pair[0], 'grp', behind)  18.4 us
    ppermute x7, starting transfers between devices, send_back(): lax.ppermute(pair[1], 'grp', ahead)  12 us
    ppermute x6, starting transfers between devices, send(): lax.ppermute(pair[0], 'grp', ahead)  11.9 us
    pallas_call x2, Pallas kernels, load(): pl.pallas_call(load_kernel, out_shape=(pltpu.VMEM((per_device, width, 2 *...  9.59 us
    ppermute x7, starting transfers between devices, send_back(): lax.ppermute(pair[0], 'grp', behind)  3.06 us
    pallas_call x1, Pallas kernels, pack(): pl.pallas_call(functools.partial(pack_kernel, per_group), out_shape=(jax....  2.67 us
  transfers between devices with their start and end apart: 29, of which 11 were waited for; matrix products, arithmetic and copies ran while one was open for 0% of the time, Pallas kernels for 44%

profile of v3, /device:TPU:0, one launch (start us, length us, event | category | flops | bytes accessed | tf_op | source)
XLA Modules:
  0.0 129.2 jit_solution(17822608748467500768)
XLA Ops:
  0.6 0.5 collective-permute-start
  1.2 0.4 collective-permute-start.4
  1.7 2.7 %shard_map.86 = (bf16[128,4224]{1,0:T(8,128)(2,1)}, bf16[128,4224]{1,0:T(8,128)(2,1)S(1)}, bf16[128,128]{1,0:T(8,128)(2,1)S(1)}, bf16[128,128]{1,0:T(8,128)(2,1)S(1)}, bf16[128,128]{1,0:T(8,128)(2,1)S(1)}) custom-call(bf16[128,2048]{1,0:T(8,128)(2,1)} %refs_0_.1, bf16[128,2048]{1,0:T(8,128)(2,1)} %refs_1_.1, s32[8,128]{1,0:T(8,128)} %bitcast.5, ...), custom_call_target="tpu_custom_call" | custom-call | tf_op jit(solution)/shard_map/pallas_call | solution.py:286
  4.3 2.7 %collective-permute-start.1 = (bf16[128,4224]{1,0:T(8,128)(2,1)}, bf16[128,4224]{1,0:T(8,128)(2,1)S(1)}, u32[]{:S(2)}, u32[]{:S(2)}) collective-permute-start(bf16[128,4224]{1,0:T(8,128)(2,1)} %get-tuple-element.54), channel_id=1, source_target_pairs={{0,4},{4,8},{8,12},{12,14},{14,10},{10,6},{6,2},{2,0},{1,5},{5,9},... | collective-permute-start | bytes 3244040 | tf_op jit(solution)/shard_map/ppermute | solution.py:504
  7.1 4.7 %shard_map.87 = (bf16[2,2048,768]{2,1,0:T(8,128)(2,1)S(1)}, bf16[1536,2048]{1,0:T(8,128)(2,1)S(1)}, bf16[2048,768]{1,0:T(8,128)(2,1)S(1)}, f32[8,128]{1,0:T(8,128)S(1)}) custom-call(s32[2]{0:T(128)S(1)} %pad_add_fusion.after_this.place, bf16[2,2048,384]{2,1,0:T(8,128)(2,1)} %gate.1, bf16[2,2048,384]{2,1,0:T(8,128)(2,1)} %up.1, bf16[2,384,2048]{2,1,0:T(8,128)(2,1)} %down.1), custom_call_target="tpu_custom_call" | custom-call | flops 1 | bytes 25165824 | tf_op jit(solution)/shard_map/pallas_call | solution.py:341
  11.9 19.8 %collective-permute-done.1.refs_0_ = bf16[128,4224]{1,0:T(8,128)(2,1)S(1)} collective-permute-done((bf16[128,4224]{1,0:T(8,128)(2,1)}, bf16[128,4224]{1,0:T(8,128)(2,1)S(1)}, u32[]{:S(2)}, u32[]{:S(2)}) %collective-permute-start.1) | collective-permute-done | bytes 1081376 | tf_op jit(solution)/shard_map/ppermute | solution.py:504
  31.8 1.9 %collective-permute-start.5 = (bf16[64,4224]{1,0:T(8,128)(2,1)S(1)}, bf16[64,4224]{1,0:T(8,128)(2,1)S(1)}, u32[]{:S(2)}, u32[]{:S(2)}) collective-permute-start(bf16[64,4224]{1,0:T(8,128)(2,1)S(1)} %get-tuple-element.70), channel_id=1, source_target_pairs={{0,4},{4,8},{8,12},{12,14},{14,10},{10,6},{6,2},{2,0},{1,5},{5,9},... | collective-permute-start | bytes 1622024 | tf_op jit(solution)/shard_map/ppermute | solution.py:504
  33.7 0.3 collective-permute-start.7
  34.0 1.8 %collective-permute-start.6 = (bf16[64,4224]{1,0:T(8,128)(2,1)S(1)}, bf16[64,4224]{1,0:T(8,128)(2,1)S(1)}, u32[]{:S(2)}, u32[]{:S(2)}) collective-permute-start(bf16[64,4224]{1,0:T(8,128)(2,1)S(1)} %get-tuple-element.71), channel_id=1, source_target_pairs={{0,4},{4,8},{8,12},{12,14},{14,10},{10,6},{6,2},{2,0},{1,5},{5,9},... | collective-permute-start | bytes 1622024 | tf_op jit(solution)/shard_map/ppermute | solution.py:504
  35.8 0.2 collective-permute-start.8
  36.0 4.8 %shard_map.88 = (bf16[2,2048,768]{2,1,0:T(8,128)(2,1)S(1)}, bf16[1536,2048]{1,0:T(8,128)(2,1)S(1)}, bf16[2048,768]{1,0:T(8,128)(2,1)S(1)}, f32[8,128]{1,0:T(8,128)S(1)}) custom-call(f32[8,128]{1,0:T(8,128)S(1)} %get-tuple-element.53.after_this, bf16[2,2048,384]{2,1,0:T(8,128)(2,1)} %collective-permute-done.gate, ...), custom_call_target="tpu_custom_call" | custom-call | flops 1 | bytes 25165824 | tf_op jit(solution)/shard_map/pallas_call | solution.py:341
  40.9 6.2 %shard_map.89 = (bf16[128,2176]{1,0:T(8,128)(2,1)S(1)}, f32[8,128]{1,0:T(8,128)S(1)}) custom-call(s32[2]{0:T(128)S(1)} %pad_add_fusion.after_this.place, f32[8,128]{1,0:T(8,128)S(1)} %get-tuple-element.58.after_this, bf16[128,2048]{1,0:T(8,128)(2,1)S(1)} %copy-done.2, bf16[128,2048]{1,0:T(8,128)(2,1)S(1)} %copy-done.3, ...), custom_call_target="tpu_custom_call" | custom-call | flops 1 | bytes 1 | tf_op jit(solution)/shard_map/pallas_call | solution.py:417
  47.1 1.8 %collective-permute-start.9 = (bf16[64,4224]{1,0:T(8,128)(2,1)S(1)}, bf16[64,4224]{1,0:T(8,128)(2,1)S(1)}, u32[]{:S(2)}, u32[]{:S(2)}) collective-permute-start(bf16[64,4224]{1,0:T(8,128)(2,1)S(1)} %collective-permute-done.5.refs_0_), channel_id=1, source_target_pairs={{0,4},{4,8},{8,12},{12,14},{14,10},{10,6},{6,2},{2,0},{1,5},{5,9},... | collective-permute-start | bytes 1622024 | tf_op jit(solution)/shard_map/ppermute | solution.py:504
  48.8 0.1 collective-permute-done.7.refs_2_
  49.0 0.2 collective-permute-start.10
  49.2 10.1 %shard_map.90 = (bf16[128,2176]{1,0:T(8,128)(2,1)S(1)}, bf16[128,2176]{1,0:T(8,128)(2,1)S(1)}, f32[8,128]{1,0:T(8,128)S(1)}) custom-call(s32[2]{0:T(128)S(1)} %pad_add_fusion.after_this.place, f32[8,128]{1,0:T(8,128)S(1)} %get-tuple-element.67.after_this, bf16[128,4224]{1,0:T(8,128)(2,1)S(1)} %copy-done.1, ...), custom_call_target="tpu_custom_call" | custom-call | flops 1 | bytes 1 | tf_op jit(solution)/shard_map/pallas_call | solution.py:417
  59.3 1.9 %collective-permute-start.11 = (bf16[48,4224]{1,0:T(8,128)(2,1)S(1)}, bf16[48,4224]{1,0:T(8,128)(2,1)S(1)}, u32[]{:S(2)}, u32[]{:S(2)}) collective-permute-start(bf16[48,4224]{1,0:T(8,128)(2,1)S(1)} %slice.52), channel_id=1, source_target_pairs={{0,4},{4,8},{8,12},{12,14},{14,10},{10,6},{6,2},{2,0},{1,5},{5,9},... | collective-permute-start | bytes 1216520 | tf_op jit(solution)/shard_map/ppermute | solution.py:504
  61.3 0.2 collective-permute-start.12
  61.5 10.1 %shard_map.91 = (bf16[48,2176]{1,0:T(8,128)(2,1)S(1)}, bf16[80,2176]{1,0:T(8,128)(2,1)S(1)}, bf16[48,2176]{1,0:T(8,128)(2,1)S(1)}, bf16[80,2176]{1,0:T(8,128)(2,1)S(1)}, f32[8,128]{1,0:T(8,128)S(1)}) custom-call(s32[2]{0:T(128)S(1)} %pad_add_fusion.after_this.place, f32[8,128]{1,0:T(8,128)S(1)} %get-tuple-element.69.after_this, ...), custom_call_target="tpu_custom_call" | custom-call | flops 1 | bytes 1 | tf_op jit(solution)/shard_map/pallas_call | solution.py:417
  71.6 1.9 %collective-permute-start.13 = (bf16[48,4224]{1,0:T(8,128)(2,1)S(1)}, bf16[48,4224]{1,0:T(8,128)(2,1)S(1)}, u32[]{:S(2)}, u32[]{:S(2)}) collective-permute-start(bf16[48,4224]{1,0:T(8,128)(2,1)S(1)} %slice.54), channel_id=1, source_target_pairs={{0,4},{4,8},{8,12},{12,14},{14,10},{10,6},{6,2},{2,0},{1,5},{5,9},... | collective-permute-start | bytes 1216520 | tf_op jit(solution)/shard_map/ppermute | solution.py:504
  73.6 0.5 collective-permute-start.14
  74.0 5.9 %shard_map.92 = (bf16[48,2176]{1,0:T(8,128)(2,1)S(1)}, bf16[16,2176]{1,0:T(8,128)(2,1)S(1)}, bf16[48,2176]{1,0:T(8,128)(2,1)S(1)}, bf16[16,2176]{1,0:T(8,128)(2,1)S(1)}, f32[8,128]{1,0:T(8,128)S(1)}) custom-call(s32[2]{0:T(128)S(1)} %pad_add_fusion.after_this.place, f32[8,128]{1,0:T(8,128)S(1)} %get-tuple-element.75.after_this, ...), custom_call_target="tpu_custom_call" | custom-call | flops 1 | bytes 1 | tf_op jit(solution)/shard_map/pallas_call | solution.py:417
  80.0 0.9 collective-permute-done.12.refs_1_
  80.8 5.3 %shard_map.93 = (bf16[48,2176]{1,0:T(8,128)(2,1)S(1)}, bf16[48,2176]{1,0:T(8,128)(2,1)S(1)}, f32[8,128]{1,0:T(8,128)S(1)}) custom-call(s32[2]{0:T(128)S(1)} %pad_add_fusion.after_this.place, f32[8,128]{1,0:T(8,128)S(1)} %get-tuple-element.79.after_this, bf16[48,4224]{1,0:T(8,128)(2,1)S(1)} %collective-permute-done.11.refs_0_, ...), custom_call_target="tpu_custom_call" | custom-call | flops 1 | bytes 1 | tf_op jit(solution)/shard_map/pallas_call | solution.py:417
  86.2 1.0 collective-permute-start.15
  87.2 1.4 %collective-permute-start.16 = (bf16[64,2176]{1,0:T(8,128)(2,1)S(1)}, bf16[64,2176]{1,0:T(8,128)(2,1)S(1)}, u32[]{:S(2)}, u32[]{:S(2)}) collective-permute-start(bf16[64,2176]{1,0:T(8,128)(2,1)S(1)} %shard_map.96), channel_id=1, source_target_pairs={{0,4},{4,8},{8,12},{12,14},{14,10},{10,6},{6,2},{2,0},{1,5},{5,9},... | collective-permute-start | bytes 835592 | tf_op jit(solution)/shard_map/ppermute | solution.py:507
  88.6 0.9 collective-permute-done.14.refs_1_
  89.5 5.8 %shard_map.94 = (bf16[48,2176]{1,0:T(8,128)(2,1)S(1)}, bf16[48,2176]{1,0:T(8,128)(2,1)S(1)}, f32[8,128]{1,0:T(8,128)}) custom-call(s32[2]{0:T(128)S(1)} %pad_add_fusion.after_this.place, f32[8,128]{1,0:T(8,128)S(1)} %get-tuple-element.82.after_this, bf16[48,4224]{1,0:T(8,128)(2,1)S(1)} %collective-permute-done.13.refs_0_, ...), custom_call_target="tpu_custom_call" | custom-call | flops 1 | bytes 1 | tf_op jit(solution)/shard_map/pallas_call | solution.py:417
  95.3 0.3 collective-permute-start.17
  95.6 1.7 %collective-permute-start.23 = (bf16[48,2176]{1,0:T(8,128)(2,1)S(1)}, bf16[48,2176]{1,0:T(8,128)(2,1)S(1)}, u32[]{:S(2)}, u32[]{:S(2)}) collective-permute-start(bf16[48,2176]{1,0:T(8,128)(2,1)S(1)} %get-tuple-element.96), channel_id=1, source_target_pairs={{0,4},{4,8},{8,12},{12,14},{14,10},{10,6},{6,2},{2,0},{1,5},{5,9},... | collective-permute-start | bytes 626696 | tf_op jit(solution)/shard_map/ppermute | solution.py:507
  97.4 0.4 collective-permute-start.21
  97.9 1.8 %collective-permute-start.27 = (bf16[80,2176]{1,0:T(8,128)(2,1)S(1)}, bf16[80,2176]{1,0:T(8,128)(2,1)S(1)}, u32[]{:S(2)}, u32[]{:S(2)}) collective-permute-start(bf16[80,2176]{1,0:T(8,128)(2,1)S(1)} %shard_map.105), channel_id=1, source_target_pairs={{0,4},{4,8},{8,12},{12,14},{14,10},{10,6},{6,2},{2,0},{1,5},{5,9},... | collective-permute-start | bytes 1044488 | tf_op jit(solution)/shard_map/ppermute | solution.py:507
  99.6 3.8 %collective-permute-done.17.b = bf16[48,2176]{1,0:T(8,128)(2,1)S(1)} collective-permute-done((bf16[48,2176]{1,0:T(8,128)(2,1)S(1)}, bf16[48,2176]{1,0:T(8,128)(2,1)S(1)}, u32[]{:S(2)}, u32[]{:S(2)}) %collective-permute-start.17) | collective-permute-done | bytes 208928 | tf_op jit(solution)/shard_map/ppermute | solution.py:507
  103.5 0.4 collective-permute-start.18
  103.9 1.8 %collective-permute-start.24 = (bf16[48,2176]{1,0:T(8,128)(2,1)S(1)}, bf16[48,2176]{1,0:T(8,128)(2,1)S(1)}, u32[]{:S(2)}, u32[]{:S(2)}) collective-permute-start(bf16[48,2176]{1,0:T(8,128)(2,1)S(1)} %shard_map.102), channel_id=1, source_target_pairs={{0,4},{4,8},{8,12},{12,14},{14,10},{10,6},{6,2},{2,0},{1,5},{5,9},... | collective-permute-start | bytes 626696 | tf_op jit(solution)/shard_map/ppermute | solution.py:507
  105.7 6.8 %collective-permute-done.18.b = bf16[48,2176]{1,0:T(8,128)(2,1)S(1)} collective-permute-done((bf16[48,2176]{1,0:T(8,128)(2,1)S(1)}, bf16[48,2176]{1,0:T(8,128)(2,1)S(1)}, u32[]{:S(2)}, u32[]{:S(2)}) %collective-permute-start.18) | collective-permute-done | bytes 208928 | tf_op jit(solution)/shard_map/ppermute | solution.py:507
  112.5 0.4 collective-permute-start.19
  112.9 1.8 %collective-permute-start.25 = (bf16[48,2176]{1,0:T(8,128)(2,1)S(1)}, bf16[48,2176]{1,0:T(8,128)(2,1)S(1)}, u32[]{:S(2)}, u32[]{:S(2)}) collective-permute-start(bf16[48,2176]{1,0:T(8,128)(2,1)S(1)} %shard_map.103), channel_id=1, source_target_pairs={{0,4},{4,8},{8,12},{12,14},{14,10},{10,6},{6,2},{2,0},{1,5},{5,9},... | collective-permute-start | bytes 626696 | tf_op jit(solution)/shard_map/ppermute | solution.py:507
  114.9 0.4 collective-permute-start.22
  115.3 1.8 %collective-permute-start.28 = (bf16[80,2176]{1,0:T(8,128)(2,1)S(1)}, bf16[80,2176]{1,0:T(8,128)(2,1)S(1)}, u32[]{:S(2)}, u32[]{:S(2)}) collective-permute-start(bf16[80,2176]{1,0:T(8,128)(2,1)S(1)} %shard_map.106), channel_id=1, source_target_pairs={{0,4},{4,8},{8,12},{12,14},{14,10},{10,6},{6,2},{2,0},{1,5},{5,9},... | collective-permute-start | bytes 1044488 | tf_op jit(solution)/shard_map/ppermute | solution.py:507
  117.1 3.5 %collective-permute-done.19.b = bf16[48,2176]{1,0:T(8,128)(2,1)S(1)} collective-permute-done((bf16[48,2176]{1,0:T(8,128)(2,1)S(1)}, bf16[48,2176]{1,0:T(8,128)(2,1)S(1)}, u32[]{:S(2)}, u32[]{:S(2)}) %collective-permute-start.19) | collective-permute-done | bytes 208928 | tf_op jit(solution)/shard_map/ppermute | solution.py:507
  120.7 0.4 collective-permute-start.20
  121.1 1.8 %collective-permute-start.26 = (bf16[48,2176]{1,0:T(8,128)(2,1)S(1)}, bf16[48,2176]{1,0:T(8,128)(2,1)S(1)}, u32[]{:S(2)}, u32[]{:S(2)}) collective-permute-start(bf16[48,2176]{1,0:T(8,128)(2,1)S(1)} %shard_map.104), channel_id=1, source_target_pairs={{0,4},{4,8},{8,12},{12,14},{14,10},{10,6},{6,2},{2,0},{1,5},{5,9},... | collective-permute-start | bytes 626696 | tf_op jit(solution)/shard_map/ppermute | solution.py:507
  122.9 2.4 %collective-permute-done.22.short_up = bf16[80,2176]{1,0:T(8,128)(2,1)S(1)} collective-permute-done((bf16[80,2176]{1,0:T(8,128)(2,1)S(1)}, bf16[80,2176]{1,0:T(8,128)(2,1)S(1)}, u32[]{:S(2)}, u32[]{:S(2)}) %collective-permute-start.22) | collective-permute-done | bytes 348192 | tf_op jit(solution)/shard_map/ppermute | solution.py:507
  125.3 0.3 collective-permute-done.28.short_down
  125.6 1.9 %collective-permute-done.20.long_up = bf16[48,2176]{1,0:T(8,128)(2,1)S(1)} collective-permute-done((bf16[48,2176]{1,0:T(8,128)(2,1)S(1)}, bf16[48,2176]{1,0:T(8,128)(2,1)S(1)}, u32[]{:S(2)}, u32[]{:S(2)}) %collective-permute-start.20) | collective-permute-done | bytes 208928 | tf_op jit(solution)/shard_map/ppermute | solution.py:507
  127.5 0.3 collective-permute-done.26.long_down
  127.9 1.3 %shard_map.107 = (bf16[128,2048]{1,0:T(8,128)(2,1)}, bf16[8,128]{1,0:T(8,128)(2,1)}) custom-call(s32[8,128]{1,0:T(8,128)S(1)} %bitcast.6, bf16[128,128]{1,0:T(8,128)(2,1)S(1)} %get-tuple-element.51.order_up, bf16[128,128]{1,0:T(8,128)(2,1)S(1)} %get-tuple-element.52.order_down, bf16[128,2176]{1,0:T(8,128)(2,1)S(1)} %get-tuple-element.66.mine, ...), custom_call_target="tpu_custom_call" | custom-call | tf_op jit(solution)/shard_map/pallas_call | solution.py:445
  (53 shorter events, 1.2 us)
Async XLA Ops:
  0.6 31.1 %collective-permute-start = (bf16[2,2048,384]{2,1,0:T(8,128)(2,1)}, bf16[2,2048,384]{2,1,0:T(8,128)(2,1)}, u32[]{:S(2)}, u32[]{:S(2)}) collective-permute-start(bf16[2,2048,384]{2,1,0:T(8,128)(2,1)} %gate.1), channel_id=1, source_target_pairs={{0,1},{1,0},{2,3},{3,2},{4,5},{5,4},{6,7},{7,6},{8,9},{9,8},{10,11... | collective-permute-start | bytes 9437192 | tf_op jit(solution)/shard_map/ppermute | solution.py:513
  1.1 30.6 %collective-permute-start.3 = (bf16[2,2048,384]{2,1,0:T(8,128)(2,1)}, bf16[2,2048,384]{2,1,0:T(8,128)(2,1)}, u32[]{:S(2)}, u32[]{:S(2)}) collective-permute-start(bf16[2,2048,384]{2,1,0:T(8,128)(2,1)} %up.1), channel_id=1, source_target_pairs={{0,1},{1,0},{2,3},{3,2},{4,5},{5,4},{6,7},{7,6},{8,9},{9,8},{10,11... | collective-permute-start | bytes 9437192 | tf_op jit(solution)/shard_map/ppermute | solution.py:513
  1.2 30.5 %collective-permute-start.4 = (bf16[2,384,2048]{2,1,0:T(8,128)(2,1)}, bf16[2,384,2048]{2,1,0:T(8,128)(2,1)}, u32[]{:S(2)}, u32[]{:S(2)}) collective-permute-start(bf16[2,384,2048]{2,1,0:T(8,128)(2,1)} %down.1), channel_id=1, source_target_pairs={{0,1},{1,0},{2,3},{3,2},{4,5},{5,4},{6,7},{7,6},{8,9},{9,8},{10,11... | collective-permute-start | bytes 9437192 | tf_op jit(solution)/shard_map/ppermute | solution.py:513
  4.3 27.3 %collective-permute-start.1 = (bf16[128,4224]{1,0:T(8,128)(2,1)}, bf16[128,4224]{1,0:T(8,128)(2,1)S(1)}, u32[]{:S(2)}, u32[]{:S(2)}) collective-permute-start(bf16[128,4224]{1,0:T(8,128)(2,1)} %get-tuple-element.54), channel_id=1, source_target_pairs={{0,4},{4,8},{8,12},{12,14},{14,10},{10,6},{6,2},{2,0},{1,5},{5,9},... | collective-permute-start | bytes 3244040 | tf_op jit(solution)/shard_map/ppermute | solution.py:504
  7.1 26.5 %collective-permute-start.2 = (bf16[128,4224]{1,0:T(8,128)(2,1)S(1)}, bf16[128,4224]{1,0:T(8,128)(2,1)S(1)}, u32[]{:S(2)}, u32[]{:S(2)}) collective-permute-start(bf16[128,4224]{1,0:T(8,128)(2,1)S(1)} %get-tuple-element.55), channel_id=1, source_target_pairs={{4,0},{8,4},{12,8},{14,12},{10,14},{6,10},{2,6},{0,2},{5,1},{9,5},... | collective-permute-start | bytes 3244040 | tf_op jit(solution)/shard_map/ppermute | solution.py:504
  31.6 4.1 %copy-start = (bf16[128,4224]{1,0:T(8,128)(2,1)}, bf16[128,4224]{1,0:T(8,128)(2,1)S(1)}, u32[]{:S(2)}) copy-start(bf16[128,4224]{1,0:T(8,128)(2,1)S(1)} %collective-permute-done.1.refs_0_) | copy-start | bytes 3244036
  31.8 15.3 %collective-permute-start.5 = (bf16[64,4224]{1,0:T(8,128)(2,1)S(1)}, bf16[64,4224]{1,0:T(8,128)(2,1)S(1)}, u32[]{:S(2)}, u32[]{:S(2)}) collective-permute-start(bf16[64,4224]{1,0:T(8,128)(2,1)S(1)} %get-tuple-element.70), channel_id=1, source_target_pairs={{0,4},{4,8},{8,12},{12,14},{14,10},{10,6},{6,2},{2,0},{1,5},{5,9},... | collective-permute-start | bytes 1622024 | tf_op jit(solution)/shard_map/ppermute | solution.py:504
  33.7 15.3 %collective-permute-start.7 = (bf16[64,4224]{1,0:T(8,128)(2,1)S(1)}, bf16[64,4224]{1,0:T(8,128)(2,1)S(1)}, u32[]{:S(2)}, u32[]{:S(2)}) collective-permute-start(bf16[64,4224]{1,0:T(8,128)(2,1)S(1)} %get-tuple-element.72), channel_id=1, source_target_pairs={{4,0},{8,4},{12,8},{14,12},{10,14},{6,10},{2,6},{0,2},{5,1},{9,5},... | collective-permute-start | bytes 1622024 | tf_op jit(solution)/shard_map/ppermute | solution.py:504
  34.0 25.3 %collective-permute-start.6 = (bf16[64,4224]{1,0:T(8,128)(2,1)S(1)}, bf16[64,4224]{1,0:T(8,128)(2,1)S(1)}, u32[]{:S(2)}, u32[]{:S(2)}) collective-permute-start(bf16[64,4224]{1,0:T(8,128)(2,1)S(1)} %get-tuple-element.71), channel_id=1, source_target_pairs={{0,4},{4,8},{8,12},{12,14},{14,10},{10,6},{6,2},{2,0},{1,5},{5,9},... | collective-permute-start | bytes 1622024 | tf_op jit(solution)/shard_map/ppermute | solution.py:504
  35.8 5.1 %copy-start.2 = (bf16[128,2048]{1,0:T(8,128)(2,1)S(1)}, bf16[128,2048]{1,0:T(8,128)(2,1)}, u32[]{:S(2)}) copy-start(bf16[128,2048]{1,0:T(8,128)(2,1)} %refs_0_.1) | copy-start | bytes 1572868
  35.8 5.1 %copy-start.3 = (bf16[128,2048]{1,0:T(8,128)(2,1)S(1)}, bf16[128,2048]{1,0:T(8,128)(2,1)}, u32[]{:S(2)}) copy-start(bf16[128,2048]{1,0:T(8,128)(2,1)} %refs_1_.1) | copy-start | bytes 1572868
  35.8 25.4 %collective-permute-start.8 = (bf16[64,4224]{1,0:T(8,128)(2,1)S(1)}, bf16[64,4224]{1,0:T(8,128)(2,1)S(1)}, u32[]{:S(2)}, u32[]{:S(2)}) collective-permute-start(bf16[64,4224]{1,0:T(8,128)(2,1)S(1)} %get-tuple-element.73), channel_id=1, source_target_pairs={{4,0},{8,4},{12,8},{14,12},{10,14},{6,10},{2,6},{0,2},{5,1},{9,5},... | collective-permute-start | bytes 1622024 | tf_op jit(solution)/shard_map/ppermute | solution.py:504
  40.9 8.3 %copy-start.1 = (bf16[128,4224]{1,0:T(8,128)(2,1)S(1)}, bf16[128,4224]{1,0:T(8,128)(2,1)}, u32[]{:S(2)}) copy-start(bf16[128,4224]{1,0:T(8,128)(2,1)} %copy-done) | copy-start | bytes 3244036
  47.1 24.5 %collective-permute-start.9 = (bf16[64,4224]{1,0:T(8,128)(2,1)S(1)}, bf16[64,4224]{1,0:T(8,128)(2,1)S(1)}, u32[]{:S(2)}, u32[]{:S(2)}) collective-permute-start(bf16[64,4224]{1,0:T(8,128)(2,1)S(1)} %collective-permute-done.5.refs_0_), channel_id=1, source_target_pairs={{0,4},{4,8},{8,12},{12,14},{14,10},{10,6},{6,2},{2,0},{1,5},{5,9},... | collective-permute-start | bytes 1622024 | tf_op jit(solution)/shard_map/ppermute | solution.py:504
  49.0 24.6 %collective-permute-start.10 = (bf16[64,4224]{1,0:T(8,128)(2,1)S(1)}, bf16[64,4224]{1,0:T(8,128)(2,1)S(1)}, u32[]{:S(2)}, u32[]{:S(2)}) collective-permute-start(bf16[64,4224]{1,0:T(8,128)(2,1)S(1)} %collective-permute-done.7.refs_2_), channel_id=1, source_target_pairs={{4,0},{8,4},{12,8},{14,12},{10,14},{6,10},{2,6},{0,2},{5,1},{9,5},... | collective-permute-start | bytes 1622024 | tf_op jit(solution)/shard_map/ppermute | solution.py:504
  59.3 20.6 %collective-permute-start.11 = (bf16[48,4224]{1,0:T(8,128)(2,1)S(1)}, bf16[48,4224]{1,0:T(8,128)(2,1)S(1)}, u32[]{:S(2)}, u32[]{:S(2)}) collective-permute-start(bf16[48,4224]{1,0:T(8,128)(2,1)S(1)} %slice.52), channel_id=1, source_target_pairs={{0,4},{4,8},{8,12},{12,14},{14,10},{10,6},{6,2},{2,0},{1,5},{5,9},... | collective-permute-start | bytes 1216520 | tf_op jit(solution)/shard_map/ppermute | solution.py:504
  61.3 19.6 %collective-permute-start.12 = (bf16[48,4224]{1,0:T(8,128)(2,1)S(1)}, bf16[48,4224]{1,0:T(8,128)(2,1)S(1)}, u32[]{:S(2)}, u32[]{:S(2)}) collective-permute-start(bf16[48,4224]{1,0:T(8,128)(2,1)S(1)} %slice.53), channel_id=1, source_target_pairs={{4,0},{8,4},{12,8},{14,12},{10,14},{6,10},{2,6},{0,2},{5,1},{9,5},... | collective-permute-start | bytes 1216520 | tf_op jit(solution)/shard_map/ppermute | solution.py:504
  71.6 16.9 %collective-permute-start.13 = (bf16[48,4224]{1,0:T(8,128)(2,1)S(1)}, bf16[48,4224]{1,0:T(8,128)(2,1)S(1)}, u32[]{:S(2)}, u32[]{:S(2)}) collective-permute-start(bf16[48,4224]{1,0:T(8,128)(2,1)S(1)} %slice.54), channel_id=1, source_target_pairs={{0,4},{4,8},{8,12},{12,14},{14,10},{10,6},{6,2},{2,0},{1,5},{5,9},... | collective-permute-start | bytes 1216520 | tf_op jit(solution)/shard_map/ppermute | solution.py:504
  73.6 16.0 %collective-permute-start.14 = (bf16[48,4224]{1,0:T(8,128)(2,1)S(1)}, bf16[48,4224]{1,0:T(8,128)(2,1)S(1)}, u32[]{:S(2)}, u32[]{:S(2)}) collective-permute-start(bf16[48,4224]{1,0:T(8,128)(2,1)S(1)} %slice.55), channel_id=1, source_target_pairs={{4,0},{8,4},{12,8},{14,12},{10,14},{6,10},{2,6},{0,2},{5,1},{9,5},... | collective-permute-start | bytes 1216520 | tf_op jit(solution)/shard_map/ppermute | solution.py:504
  86.2 9.1 %collective-permute-start.15 = (bf16[64,2176]{1,0:T(8,128)(2,1)S(1)}, bf16[64,2176]{1,0:T(8,128)(2,1)S(1)}, u32[]{:S(2)}, u32[]{:S(2)}) collective-permute-start(bf16[64,2176]{1,0:T(8,128)(2,1)S(1)} %shard_map.95), channel_id=1, source_target_pairs={{4,0},{8,4},{12,8},{14,12},{10,14},{6,10},{2,6},{0,2},{5,1},{9,5},... | collective-permute-start | bytes 835592 | tf_op jit(solution)/shard_map/ppermute | solution.py:507
  87.2 8.1 %collective-permute-start.16 = (bf16[64,2176]{1,0:T(8,128)(2,1)S(1)}, bf16[64,2176]{1,0:T(8,128)(2,1)S(1)}, u32[]{:S(2)}, u32[]{:S(2)}) collective-permute-start(bf16[64,2176]{1,0:T(8,128)(2,1)S(1)} %shard_map.96), channel_id=1, source_target_pairs={{0,4},{4,8},{8,12},{12,14},{14,10},{10,6},{6,2},{2,0},{1,5},{5,9},... | collective-permute-start | bytes 835592 | tf_op jit(solution)/shard_map/ppermute | solution.py:507
  95.3 8.1 %collective-permute-start.17 = (bf16[48,2176]{1,0:T(8,128)(2,1)S(1)}, bf16[48,2176]{1,0:T(8,128)(2,1)S(1)}, u32[]{:S(2)}, u32[]{:S(2)}) collective-permute-start(bf16[48,2176]{1,0:T(8,128)(2,1)S(1)} %get-tuple-element.90), channel_id=1, source_target_pairs={{4,0},{8,4},{12,8},{14,12},{10,14},{6,10},{2,6},{0,2},{5,1},{9,5},... | collective-permute-start | bytes 626696 | tf_op jit(solution)/shard_map/ppermute | solution.py:507
  95.6 8.2 %collective-permute-start.23 = (bf16[48,2176]{1,0:T(8,128)(2,1)S(1)}, bf16[48,2176]{1,0:T(8,128)(2,1)S(1)}, u32[]{:S(2)}, u32[]{:S(2)}) collective-permute-start(bf16[48,2176]{1,0:T(8,128)(2,1)S(1)} %get-tuple-element.96), channel_id=1, source_target_pairs={{0,4},{4,8},{8,12},{12,14},{14,10},{10,6},{6,2},{2,0},{1,5},{5,9},... | collective-permute-start | bytes 626696 | tf_op jit(solution)/shard_map/ppermute | solution.py:507
  97.4 17.4 %collective-permute-start.21 = (bf16[80,2176]{1,0:T(8,128)(2,1)S(1)}, bf16[80,2176]{1,0:T(8,128)(2,1)S(1)}, u32[]{:S(2)}, u32[]{:S(2)}) collective-permute-start(bf16[80,2176]{1,0:T(8,128)(2,1)S(1)} %shard_map.100), channel_id=1, source_target_pairs={{4,0},{8,4},{12,8},{14,12},{10,14},{6,10},{2,6},{0,2},{5,1},{9,5},... | collective-permute-start | bytes 1044488 | tf_op jit(solution)/shard_map/ppermute | solution.py:507
  97.9 17.4 %collective-permute-start.27 = (bf16[80,2176]{1,0:T(8,128)(2,1)S(1)}, bf16[80,2176]{1,0:T(8,128)(2,1)S(1)}, u32[]{:S(2)}, u32[]{:S(2)}) collective-permute-start(bf16[80,2176]{1,0:T(8,128)(2,1)S(1)} %shard_map.105), channel_id=1, source_target_pairs={{0,4},{4,8},{8,12},{12,14},{14,10},{10,6},{6,2},{2,0},{1,5},{5,9},... | collective-permute-start | bytes 1044488 | tf_op jit(solution)/shard_map/ppermute | solution.py:507
  103.5 9.0 %collective-permute-start.18 = (bf16[48,2176]{1,0:T(8,128)(2,1)S(1)}, bf16[48,2176]{1,0:T(8,128)(2,1)S(1)}, u32[]{:S(2)}, u32[]{:S(2)}) collective-permute-start(bf16[48,2176]{1,0:T(8,128)(2,1)S(1)} %shard_map.97), channel_id=1, source_target_pairs={{4,0},{8,4},{12,8},{14,12},{10,14},{6,10},{2,6},{0,2},{5,1},{9,5},... | collective-permute-start | bytes 626696 | tf_op jit(solution)/shard_map/ppermute | solution.py:507
  103.9 9.0 %collective-permute-start.24 = (bf16[48,2176]{1,0:T(8,128)(2,1)S(1)}, bf16[48,2176]{1,0:T(8,128)(2,1)S(1)}, u32[]{:S(2)}, u32[]{:S(2)}) collective-permute-start(bf16[48,2176]{1,0:T(8,128)(2,1)S(1)} %shard_map.102), channel_id=1, source_target_pairs={{0,4},{4,8},{8,12},{12,14},{14,10},{10,6},{6,2},{2,0},{1,5},{5,9},... | collective-permute-start | bytes 626696 | tf_op jit(solution)/shard_map/ppermute | solution.py:507
  112.5 15.4 %copy-start.4 = (s32[128,8]{0,1:T(8,128)S(1)}, s32[128,8]{0,1:T(8,128)}, u32[]{:S(2)}) copy-start(s32[128,8]{0,1:T(8,128)} %param.9) | copy-start | bytes 12292
  112.5 8.2 %collective-permute-start.19 = (bf16[48,2176]{1,0:T(8,128)(2,1)S(1)}, bf16[48,2176]{1,0:T(8,128)(2,1)S(1)}, u32[]{:S(2)}, u32[]{:S(2)}) collective-permute-start(bf16[48,2176]{1,0:T(8,128)(2,1)S(1)} %shard_map.98), channel_id=1, source_target_pairs={{4,0},{8,4},{12,8},{14,12},{10,14},{6,10},{2,6},{0,2},{5,1},{9,5},... | collective-permute-start | bytes 626696 | tf_op jit(solution)/shard_map/ppermute | solution.py:507
  112.9 8.2 %collective-permute-start.25 = (bf16[48,2176]{1,0:T(8,128)(2,1)S(1)}, bf16[48,2176]{1,0:T(8,128)(2,1)S(1)}, u32[]{:S(2)}, u32[]{:S(2)}) collective-permute-start(bf16[48,2176]{1,0:T(8,128)(2,1)S(1)} %shard_map.103), channel_id=1, source_target_pairs={{0,4},{4,8},{8,12},{12,14},{14,10},{10,6},{6,2},{2,0},{1,5},{5,9},... | collective-permute-start | bytes 626696 | tf_op jit(solution)/shard_map/ppermute | solution.py:507
  114.9 10.4 %collective-permute-start.22 = (bf16[80,2176]{1,0:T(8,128)(2,1)S(1)}, bf16[80,2176]{1,0:T(8,128)(2,1)S(1)}, u32[]{:S(2)}, u32[]{:S(2)}) collective-permute-start(bf16[80,2176]{1,0:T(8,128)(2,1)S(1)} %shard_map.101), channel_id=1, source_target_pairs={{4,0},{8,4},{12,8},{14,12},{10,14},{6,10},{2,6},{0,2},{5,1},{9,5},... | collective-permute-start | bytes 1044488 | tf_op jit(solution)/shard_map/ppermute | solution.py:507
  115.3 10.3 %collective-permute-start.28 = (bf16[80,2176]{1,0:T(8,128)(2,1)S(1)}, bf16[80,2176]{1,0:T(8,128)(2,1)S(1)}, u32[]{:S(2)}, u32[]{:S(2)}) collective-permute-start(bf16[80,2176]{1,0:T(8,128)(2,1)S(1)} %shard_map.106), channel_id=1, source_target_pairs={{0,4},{4,8},{8,12},{12,14},{14,10},{10,6},{6,2},{2,0},{1,5},{5,9},... | collective-permute-start | bytes 1044488 | tf_op jit(solution)/shard_map/ppermute | solution.py:507
  120.7 6.8 %collective-permute-start.20 = (bf16[48,2176]{1,0:T(8,128)(2,1)S(1)}, bf16[48,2176]{1,0:T(8,128)(2,1)S(1)}, u32[]{:S(2)}, u32[]{:S(2)}) collective-permute-start(bf16[48,2176]{1,0:T(8,128)(2,1)S(1)} %shard_map.99), channel_id=1, source_target_pairs={{4,0},{8,4},{12,8},{14,12},{10,14},{6,10},{2,6},{0,2},{5,1},{9,5},... | collective-permute-start | bytes 626696 | tf_op jit(solution)/shard_map/ppermute | solution.py:507
  121.1 6.7 %collective-permute-start.26 = (bf16[48,2176]{1,0:T(8,128)(2,1)S(1)}, bf16[48,2176]{1,0:T(8,128)(2,1)S(1)}, u32[]{:S(2)}, u32[]{:S(2)}) collective-permute-start(bf16[48,2176]{1,0:T(8,128)(2,1)S(1)} %shard_map.104), channel_id=1, source_target_pairs={{0,4},{4,8},{8,12},{12,14},{14,10},{10,6},{6,2},{2,0},{1,5},{5,9},... | collective-permute-start | bytes 626696 | tf_op jit(solution)/shard_map/ppermute | solution.py:507

commit v4 on v3

--- a/solution.py
+++ b/solution.py
@@ -175,6 +175,7 @@
 
 
 LANES = 128
+SLOT = 32
 NT = (((1,), (1,)), ((), ()))
 ANYWHERE = pl.BlockSpec(memory_space=pl.ANY)
 IN_VMEM = pl.BlockSpec(memory_space=pltpu.VMEM)
@@ -354,11 +355,11 @@
     )(after_this, gate, up, down)
 
 
-def experts_kernel(inputs, pieces, unrolled, place, after_this, *refs):
+def experts_kernel(inputs, plan, unrolled, place, after_this, *refs):
     del after_this
     given, refs = refs[:inputs], refs[inputs:]
     loaded, refs = (refs[:3], refs[3:6]), refs[6:]
-    outs, token = refs[:pieces], refs[pieces]
+    *outs, token = refs
     token[...] = jnp.zeros_like(token)
     per_device, width, both_hidden = loaded[0][0].shape
     hidden = both_hidden // 2
@@ -399,26 +400,57 @@
         total = sum(
             jnp.dot(a, back[:, part], preferred_element_type=jnp.float32) for a, (_, back, _) in zip(grads, loaded)
         ).astype(jnp.bfloat16)
-        start = 0
-        for out in outs:
-            out[:, part] = total[start : start + out.shape[0]]
-            start += out.shape[0]
+        for out, start, rows in grads_at:
+            out[:, part] = total[start : start + rows]
         return carry
 
+    grads_at, routes_at = [], []
+    start = at_out = 0
+    for long, short, first in plan:
+        if long:
+            grads_at.append((outs[at_out], start, long))
+            routes_at.append((outs[at_out], width, (start, long), (start + long, short, first)))
+            at_out += 1
+        if short:
+            grads_at.append((outs[at_out], start + long, short))
+            at_out += 1
+            if not long:
+                routes_at.append((outs[at_out], 0, (start, 0), (start, short, first)))
+                at_out += 1
+        start += long + short
     lax.fori_loop(0, width // step, chunk, 0, unroll=unrolled)
-    start = 0
-    for out in outs:
-        out[:, width:] = route[start : start + out.shape[0]].astype(out.dtype)
-        start += out.shape[0]
-
-
-def experts_call(place, after_this, given, rows, loaded, unrolled):
+    for out, lanes, (start, long), (short_start, short, first) in routes_at:
+        rows = out.shape[0]
+        carried = route[start : start + long] if long else jnp.zeros((rows, LANES), jnp.float32)
+        if short:
+            split = min(short, rows - first)
+            carried += shifted(route[short_start : short_start + split], 1, first, rows)
+            if short > split:
+                carried += shifted(route[short_start + split : short_start + short], 2, 0, rows)
+        out[:, lanes : lanes + LANES] = carried.astype(out.dtype)
+
+
+def shifted(route, slot, first, rows):
+    moved = pltpu.roll(route, slot * SLOT, 1)
+    parts = [moved]
+    if first:
+        parts.insert(0, jnp.zeros((first, LANES), route.dtype))
+    if rows > first + route.shape[0]:
+        parts.append(jnp.zeros((rows - first - route.shape[0], LANES), route.dtype))
+    return jnp.concatenate(parts, axis=0) if len(parts) > 1 else moved
+
+
+def experts_call(place, after_this, given, plan, loaded, unrolled):
     width = loaded[0].shape[1]
+    shapes = []
+    for long, short, _ in plan:
+        shapes += [(long, width + LANES)] * (long > 0) + [(short, width)] * (short > 0)
+        shapes += [(short, LANES)] * (not long)
     return pl.pallas_call(
-        functools.partial(experts_kernel, len(given), len(rows), unrolled),
-        out_shape=[jax.ShapeDtypeStruct((r, width + LANES), jnp.bfloat16) for r in rows] + [TOKEN],
+        functools.partial(experts_kernel, len(given), plan, unrolled),
+        out_shape=[jax.ShapeDtypeStruct(shape, jnp.bfloat16) for shape in shapes] + [TOKEN],
         in_specs=[IN_SMEM, ANYWHERE] + [IN_VMEM] * (len(given) + 6),
-        out_specs=[IN_VMEM] * (len(rows) + 1),
+        out_specs=[IN_VMEM] * (len(shapes) + 1),
         compiler_params=pltpu.CompilerParams(vmem_limit_bytes=12 * MIB),
         cost_estimate=pl.CostEstimate(flops=1, bytes_accessed=1, transcendentals=0),
     )(place, after_this, *(in_vmem(a) for a in given), *loaded)
@@ -427,12 +459,19 @@
 def finish_kernel(ids, order_up, order_down, mine, long_up, short_up, long_down, short_down, grad_tokens, grad_weights):
     width = grad_tokens.shape[1]
     backs = order_up[...].T, order_down[...].T
-    came = tuple(jnp.concatenate([a[...], b[...]], axis=0) for a, b in ((long_up, short_up), (long_down, short_down)))
-    summed = mine[...].astype(jnp.float32)
-    for back, rows in zip(backs, came):
-        summed += jnp.dot(back, rows, preferred_element_type=jnp.float32)
-    grad_tokens[...] = summed[:, :width].astype(grad_tokens.dtype)
-    route = summed[:, width:].T
+    summed = mine[:, :width].astype(jnp.float32)
+    route = mine[:, width:].astype(jnp.float32)
+    for back, long, short in zip(backs, (long_up, long_down), (short_up, short_down)):
+        rows, spare = long.shape[0], short.shape[0] - long.shape[0]
+        came = jnp.concatenate([long[:, :width], short[...]], axis=0)
+        summed += jnp.dot(back, came, preferred_element_type=jnp.float32)
+        carried = long[:, width:].astype(jnp.float32)
+        first = lax.broadcasted_iota(jnp.int32, carried.shape, 1) < SLOT
+        slots = [jnp.where(first, pltpu.roll(carried, (LANES - k * SLOT) % LANES, 1), 0.0) for k in range(3)]
+        came = jnp.concatenate([slots[0], slots[1], slots[2][:spare]], axis=0).astype(jnp.bfloat16)
+        route += jnp.dot(back, came, preferred_element_type=jnp.float32)
+    grad_tokens[...] = summed.astype(grad_tokens.dtype)
+    route = route.T
     expert = lax.broadcasted_iota(jnp.int32, route.shape, 0)
     found = [
         jnp.sum(jnp.where(expert == ids[k : k + 1, :], route, 0.0), axis=0, keepdims=True) for k in range(ids.shape[0])
@@ -455,11 +494,16 @@
     return grad_tokens, grad_weights.T
 
 
-def add_kernel(a, b, out):
+def add_kernel(a, b, *refs):
+    *more, out = refs
     rows = b.shape[0]
     if rows < a.shape[0]:
         out[rows:, :] = a[rows:, :]
     out[:rows, :] = (a[:rows, :].astype(jnp.float32) + b[...].astype(jnp.float32)).astype(out.dtype)
+    for c in more:
+        width = a.shape[1] - c.shape[1]
+        total = a[:, width:].astype(jnp.float32) + b[:, width:].astype(jnp.float32) + c[...].astype(jnp.float32)
+        out[:, width:] = total.astype(out.dtype)
 
 
 def join_kernel(a, b, out):
@@ -479,15 +523,15 @@
     )(a, b)
 
 
-def added(a, b):
+def added(a, b, *more):
     return pl.pallas_call(
         add_kernel,
         out_shape=jax.ShapeDtypeStruct(a.shape, a.dtype),
-        in_specs=[IN_VMEM] * 2,
+        in_specs=[IN_VMEM] * (2 + len(more)),
         out_specs=IN_VMEM,
         compiler_params=pltpu.CompilerParams(vmem_limit_bytes=8 * MIB),
         cost_estimate=pl.CostEstimate(flops=1, bytes_accessed=1, transcendentals=0),
-    )(a, b)
+    )(a, b, *more)
 
 
 def ring_body(tokens, cotangent, expert_ids, route_weights, gate_weight, up_weight, down_weight):
@@ -519,40 +563,45 @@
     *others, last = load(loaded_own, *tie(other[:2], *came), other[2])
     loaded += others
 
-    def call(after_this, rows, *packed, unrolled=False):
-        *parts, token = experts_call(place, after_this, packed, rows, loaded, unrolled)
+    def call(after_this, plan, *packed, unrolled=False):
+        *parts, token = experts_call(place, after_this, packed, plan, loaded, unrolled)
         return parts, token
 
     block = tokens.shape[0]
     half, most = ring_total // 2, 6 * block // ring_total
     half_block, cut = block // 2, most // 2
-    rest, needed = block - cut, (block + most) // 2 - half_block
+    rest, needed, extra = block - cut, (block + most) // 2 - half_block, half_block - cut
     long, short = [a[:half_block] for a in came], [a[half_block:] for a in came]
     long_next, short_next = send(tie(long, loaded_own, *other)), send(tie(short, loaded_own, *other))
-    mine, last = experts_call(place, last, (tokens, cotangent, table), tokens.shape[:1], loaded, False)
+    own_plan = ((block, 0, 0),)
+    mine, last = experts_call(place, last, (tokens, cotangent, table), own_plan, loaded, False)
     filler = last
-    parts, last = call(last, (block, block), *came)
-    long_terms, short_terms = [None, [a[:cut] for a in parts]], [None, [a[cut:] for a in parts]]
+    both_plan = ((cut, rest, 0),) * 2
+    parts, last = call(last, both_plan, *came)
+    long_terms, short_terms = [None, parts[0::2]], [None, parts[1::2]]
     for s in range(2, half - 1):
         long, short = long_next, short_next
         long_next = send(tie(long, filler))
         short_next = send(tie([a[:needed] for a in short] if s + 2 == half else short, last))
-        parts, last = call(last, (cut, rest, cut, rest), long[0], short[0], long[1], short[1])
-        long_terms.append((parts[0], parts[2]))
-        short_terms.append((parts[1], parts[3]))
+        parts, last = call(last, both_plan, long[0], short[0], long[1], short[1])
+        long_terms.append(parts[0::2])
+        short_terms.append(parts[1::2])
     long, short = long_next, short_next
     long_last = send(tie([a[:cut] for a in long], last))
-    parts, last = call(last, (cut, half_block - cut) * 2, *long)
-    long_terms.append((parts[0], parts[2]))
-    lower = parts[1], parts[3]
-    parts, last = call(last, (needed, needed), *short, unrolled=True)
-    short_back = send_back([joined(a, b) for a, b in zip(lower, parts)])
-    parts, last = call(last, (cut, cut), *long_last, unrolled=True)
+    parts, last = call(last, ((cut, extra, 0),) * 2, *long)
+    long_terms.append(parts[0::2])
+    lower = parts[1::2]
+    parts, last = call(last, ((0, needed, extra),) * 2, *short, unrolled=True)
+    short_back = send_back([joined(a, b) for a, b in zip(lower, parts[0::2])])
+    carried = parts[1::2]
+    parts, last = call(last, ((cut, 0, 0),) * 2, *long_last, unrolled=True)
     long_back = send_back(tie(parts, *short_back))
     for s in range(half - 1, 0, -1):
         if s < half - 1:
             short_back = send_back([added(a, b) for a, b in zip(short_terms[s], short_back)])
-        long_back = send_back([added(a, b) for a, b in zip(long_terms[s], long_back)])
+            long_back = send_back([added(a, b) for a, b in zip(long_terms[s], long_back)])
+        else:
+            long_back = send_back([added(a, b, c) for a, b, c in zip(long_terms[s], long_back, carried)])
     terms = (order_up, order_down, mine, long_back[0], short_back[0], long_back[1], short_back[1])
     return finish(expert_ids, terms, width)
 
@@ -561,7 +610,7 @@
     args = (tokens, cotangent, expert_ids, route_weights, gate_weight, up_weight, down_weight)
     ring_total, loc_total = lax.axis_size("grp"), lax.axis_size("loc")
     experts = ring_total * loc_total * gate_weight.shape[0]
-    if loc_total == 2 and ring_total == 8 and experts <= LANES and tokens.shape[0] % 32 == 0:
+    if loc_total == 2 and ring_total == 8 and experts <= SLOT and tokens.shape[0] == LANES:
         return ring_body(*args)
     return routed_body(*args)
 

time: 129 us -> 128 us (level)
  no operation moved by 1% of the time
where the time goes in v4:
time: 128 us
  Pallas kernels  57.3 us (45%)
  waiting for transfers between devices  40.3 us (31%)
  starting transfers between devices  29.4 us (23%)
    pallas_call x6, Pallas kernels, experts_call(): pl.pallas_call(functools.partial(experts_kernel, len(given), plan, unroll...  43.1 us
    ppermute x6, waiting for transfers between devices, send(): lax.ppermute(pair[0], 'grp', ahead)  19.8 us
    ppermute x7, waiting for transfers between devices, send_back(): lax.ppermute(pair[0], 'grp', behind)  17.6 us
    ppermute x7, starting transfers between devices, send_back(): lax.ppermute(pair[1], 'grp', ahead)  12.7 us
    ppermute x6, starting transfers between devices, send(): lax.ppermute(pair[0], 'grp', ahead)  11.9 us
    pallas_call x2, Pallas kernels, load(): pl.pallas_call(load_kernel, out_shape=(pltpu.VMEM((per_device, width, 2 *...  9.58 us
    pallas_call x1, Pallas kernels, pack(): pl.pallas_call(functools.partial(pack_kernel, per_group), out_shape=(jax....  2.66 us
  transfers between devices with their start and end apart: 29, of which 11 were waited for; matrix products, arithmetic and copies ran while one was open for 0% of the time, Pallas kernels for 44%

profile of v4, /device:TPU:0, one launch (start us, length us, event | category | flops | bytes accessed | tf_op | source)
XLA Modules:
  0.0 128.2 jit_solution(8381519571117741044)
XLA Ops:
  0.6 0.5 collective-permute-start
  1.2 0.4 collective-permute-start.4
  1.7 2.7 %shard_map.86 = (bf16[128,4224]{1,0:T(8,128)(2,1)}, bf16[128,4224]{1,0:T(8,128)(2,1)S(1)}, bf16[128,128]{1,0:T(8,128)(2,1)S(1)}, bf16[128,128]{1,0:T(8,128)(2,1)S(1)}, bf16[128,128]{1,0:T(8,128)(2,1)S(1)}) custom-call(bf16[128,2048]{1,0:T(8,128)(2,1)} %refs_0_.1, bf16[128,2048]{1,0:T(8,128)(2,1)} %refs_1_.1, s32[8,128]{1,0:T(8,128)} %bitcast.5, ...), custom_call_target="tpu_custom_call" | custom-call | tf_op jit(solution)/shard_map/pallas_call | solution.py:287
  4.3 2.7 %collective-permute-start.1 = (bf16[128,4224]{1,0:T(8,128)(2,1)}, bf16[128,4224]{1,0:T(8,128)(2,1)S(1)}, u32[]{:S(2)}, u32[]{:S(2)}) collective-permute-start(bf16[128,4224]{1,0:T(8,128)(2,1)} %get-tuple-element.58), channel_id=1, source_target_pairs={{0,4},{4,8},{8,12},{12,14},{14,10},{10,6},{6,2},{2,0},{1,5},{5,9},... | collective-permute-start | bytes 3244040 | tf_op jit(solution)/shard_map/ppermute | solution.py:548
  7.1 4.7 %shard_map.87 = (bf16[2,2048,768]{2,1,0:T(8,128)(2,1)S(1)}, bf16[1536,2048]{1,0:T(8,128)(2,1)S(1)}, bf16[2048,768]{1,0:T(8,128)(2,1)S(1)}, f32[8,128]{1,0:T(8,128)S(1)}) custom-call(s32[2]{0:T(128)S(1)} %pad_add_fusion.after_this.place, bf16[2,2048,384]{2,1,0:T(8,128)(2,1)} %gate.1, bf16[2,2048,384]{2,1,0:T(8,128)(2,1)} %up.1, bf16[2,384,2048]{2,1,0:T(8,128)(2,1)} %down.1), custom_call_target="tpu_custom_call" | custom-call | flops 1 | bytes 25165824 | tf_op jit(solution)/shard_map/pallas_call | solution.py:342
  11.9 19.8 %collective-permute-done.1.refs_0_ = bf16[128,4224]{1,0:T(8,128)(2,1)S(1)} collective-permute-done((bf16[128,4224]{1,0:T(8,128)(2,1)}, bf16[128,4224]{1,0:T(8,128)(2,1)S(1)}, u32[]{:S(2)}, u32[]{:S(2)}) %collective-permute-start.1) | collective-permute-done | bytes 1081376 | tf_op jit(solution)/shard_map/ppermute | solution.py:548
  31.8 1.9 %collective-permute-start.5 = (bf16[64,4224]{1,0:T(8,128)(2,1)S(1)}, bf16[64,4224]{1,0:T(8,128)(2,1)S(1)}, u32[]{:S(2)}, u32[]{:S(2)}) collective-permute-start(bf16[64,4224]{1,0:T(8,128)(2,1)S(1)} %get-tuple-element.74), channel_id=1, source_target_pairs={{0,4},{4,8},{8,12},{12,14},{14,10},{10,6},{6,2},{2,0},{1,5},{5,9},... | collective-permute-start | bytes 1622024 | tf_op jit(solution)/shard_map/ppermute | solution.py:548
  33.7 0.3 collective-permute-start.7
  34.0 1.8 %collective-permute-start.6 = (bf16[64,4224]{1,0:T(8,128)(2,1)S(1)}, bf16[64,4224]{1,0:T(8,128)(2,1)S(1)}, u32[]{:S(2)}, u32[]{:S(2)}) collective-permute-start(bf16[64,4224]{1,0:T(8,128)(2,1)S(1)} %get-tuple-element.75), channel_id=1, source_target_pairs={{0,4},{4,8},{8,12},{12,14},{14,10},{10,6},{6,2},{2,0},{1,5},{5,9},... | collective-permute-start | bytes 1622024 | tf_op jit(solution)/shard_map/ppermute | solution.py:548
  35.8 0.2 collective-permute-start.8
  36.0 4.8 %shard_map.88 = (bf16[2,2048,768]{2,1,0:T(8,128)(2,1)S(1)}, bf16[1536,2048]{1,0:T(8,128)(2,1)S(1)}, bf16[2048,768]{1,0:T(8,128)(2,1)S(1)}, f32[8,128]{1,0:T(8,128)S(1)}) custom-call(f32[8,128]{1,0:T(8,128)S(1)} %get-tuple-element.57.after_this, bf16[2,2048,384]{2,1,0:T(8,128)(2,1)} %collective-permute-done.gate, ...), custom_call_target="tpu_custom_call" | custom-call | flops 1 | bytes 25165824 | tf_op jit(solution)/shard_map/pallas_call | solution.py:342
  40.9 6.2 %shard_map.89 = (bf16[128,2176]{1,0:T(8,128)(2,1)S(1)}, f32[8,128]{1,0:T(8,128)S(1)}) custom-call(s32[2]{0:T(128)S(1)} %pad_add_fusion.after_this.place, f32[8,128]{1,0:T(8,128)S(1)} %get-tuple-element.62.after_this, bf16[128,2048]{1,0:T(8,128)(2,1)S(1)} %copy-done.2, bf16[128,2048]{1,0:T(8,128)(2,1)S(1)} %copy-done.3, ...), custom_call_target="tpu_custom_call" | custom-call | flops 1 | bytes 1 | tf_op jit(solution)/shard_map/pallas_call | solution.py:449
  47.1 1.8 %collective-permute-start.9 = (bf16[64,4224]{1,0:T(8,128)(2,1)S(1)}, bf16[64,4224]{1,0:T(8,128)(2,1)S(1)}, u32[]{:S(2)}, u32[]{:S(2)}) collective-permute-start(bf16[64,4224]{1,0:T(8,128)(2,1)S(1)} %collective-permute-done.5.refs_0_), channel_id=1, source_target_pairs={{0,4},{4,8},{8,12},{12,14},{14,10},{10,6},{6,2},{2,0},{1,5},{5,9},... | collective-permute-start | bytes 1622024 | tf_op jit(solution)/shard_map/ppermute | solution.py:548
  48.8 0.1 collective-permute-done.7.refs_2_
  49.0 0.2 collective-permute-start.10
  49.2 10.1 %shard_map.90 = (bf16[48,2176]{1,0:T(8,128)(2,1)S(1)}, bf16[80,2048]{1,0:T(8,128)(2,1)S(1)}, bf16[48,2176]{1,0:T(8,128)(2,1)S(1)}, bf16[80,2048]{1,0:T(8,128)(2,1)S(1)}, f32[8,128]{1,0:T(8,128)S(1)}) custom-call(s32[2]{0:T(128)S(1)} %pad_add_fusion.after_this.place, f32[8,128]{1,0:T(8,128)S(1)} %get-tuple-element.71.after_this, ...), custom_call_target="tpu_custom_call" | custom-call | flops 1 | bytes 1 | tf_op jit(solution)/shard_map/pallas_call | solution.py:449
  59.3 1.9 %collective-permute-start.11 = (bf16[48,4224]{1,0:T(8,128)(2,1)S(1)}, bf16[48,4224]{1,0:T(8,128)(2,1)S(1)}, u32[]{:S(2)}, u32[]{:S(2)}) collective-permute-start(bf16[48,4224]{1,0:T(8,128)(2,1)S(1)} %slice.36), channel_id=1, source_target_pairs={{0,4},{4,8},{8,12},{12,14},{14,10},{10,6},{6,2},{2,0},{1,5},{5,9},... | collective-permute-start | bytes 1216520 | tf_op jit(solution)/shard_map/ppermute | solution.py:548
  61.2 0.3 collective-permute-start.12
  61.4 10.1 %shard_map.91 = (bf16[48,2176]{1,0:T(8,128)(2,1)S(1)}, bf16[80,2048]{1,0:T(8,128)(2,1)S(1)}, bf16[48,2176]{1,0:T(8,128)(2,1)S(1)}, bf16[80,2048]{1,0:T(8,128)(2,1)S(1)}, f32[8,128]{1,0:T(8,128)S(1)}) custom-call(s32[2]{0:T(128)S(1)} %pad_add_fusion.after_this.place, f32[8,128]{1,0:T(8,128)S(1)} %get-tuple-element.73.after_this, ...), custom_call_target="tpu_custom_call" | custom-call | flops 1 | bytes 1 | tf_op jit(solution)/shard_map/pallas_call | solution.py:449
  71.6 1.9 %collective-permute-start.13 = (bf16[48,4224]{1,0:T(8,128)(2,1)S(1)}, bf16[48,4224]{1,0:T(8,128)(2,1)S(1)}, u32[]{:S(2)}, u32[]{:S(2)}) collective-permute-start(bf16[48,4224]{1,0:T(8,128)(2,1)S(1)} %slice.38), channel_id=1, source_target_pairs={{0,4},{4,8},{8,12},{12,14},{14,10},{10,6},{6,2},{2,0},{1,5},{5,9},... | collective-permute-start | bytes 1216520 | tf_op jit(solution)/shard_map/ppermute | solution.py:548
  73.5 0.5 collective-permute-start.14
  74.0 5.9 %shard_map.92 = (bf16[48,2176]{1,0:T(8,128)(2,1)S(1)}, bf16[16,2048]{1,0:T(8,128)(2,1)S(1)}, bf16[48,2176]{1,0:T(8,128)(2,1)S(1)}, bf16[16,2048]{1,0:T(8,128)(2,1)S(1)}, f32[8,128]{1,0:T(8,128)S(1)}) custom-call(s32[2]{0:T(128)S(1)} %pad_add_fusion.after_this.place, f32[8,128]{1,0:T(8,128)S(1)} %get-tuple-element.79.after_this, ...), custom_call_target="tpu_custom_call" | custom-call | flops 1 | bytes 1 | tf_op jit(solution)/shard_map/pallas_call | solution.py:449
  79.9 1.0 collective-permute-done.12.refs_1_
  80.8 5.3 %shard_map.93 = (bf16[48,2048]{1,0:T(8,128)(2,1)S(1)}, bf16[48,128]{1,0:T(8,128)(2,1)S(1)}, bf16[48,2048]{1,0:T(8,128)(2,1)S(1)}, bf16[48,128]{1,0:T(8,128)(2,1)S(1)}, f32[8,128]{1,0:T(8,128)S(1)}) custom-call(s32[2]{0:T(128)S(1)} %pad_add_fusion.after_this.place, f32[8,128]{1,0:T(8,128)S(1)} %get-tuple-element.83.after_this, ...), custom_call_target="tpu_custom_call" | custom-call | flops 1 | bytes 1 | tf_op jit(solution)/shard_map/pallas_call | solution.py:449
  86.1 0.9 collective-permute-start.15
  87.0 1.5 %collective-permute-start.16 = (bf16[64,2048]{1,0:T(8,128)(2,1)S(1)}, bf16[64,2048]{1,0:T(8,128)(2,1)S(1)}, u32[]{:S(2)}, u32[]{:S(2)}) collective-permute-start(bf16[64,2048]{1,0:T(8,128)(2,1)S(1)} %shard_map.96), channel_id=1, source_target_pairs={{0,4},{4,8},{8,12},{12,14},{14,10},{10,6},{6,2},{2,0},{1,5},{5,9},... | collective-permute-start | bytes 786440 | tf_op jit(solution)/shard_map/ppermute | solution.py:551
  88.5 1.0 collective-permute-done.14.refs_1_
  89.5 5.7 %shard_map.94 = (bf16[48,2176]{1,0:T(8,128)(2,1)S(1)}, bf16[48,2176]{1,0:T(8,128)(2,1)S(1)}, f32[8,128]{1,0:T(8,128)}) custom-call(s32[2]{0:T(128)S(1)} %pad_add_fusion.after_this.place, f32[8,128]{1,0:T(8,128)S(1)} %get-tuple-element.86.after_this, bf16[48,4224]{1,0:T(8,128)(2,1)S(1)} %collective-permute-done.13.refs_0_, ...), custom_call_target="tpu_custom_call" | custom-call | flops 1 | bytes 1 | tf_op jit(solution)/shard_map/pallas_call | solution.py:449
  95.2 0.2 collective-permute-start.17
  95.4 1.8 %collective-permute-start.23 = (bf16[48,2176]{1,0:T(8,128)(2,1)S(1)}, bf16[48,2176]{1,0:T(8,128)(2,1)S(1)}, u32[]{:S(2)}, u32[]{:S(2)}) collective-permute-start(bf16[48,2176]{1,0:T(8,128)(2,1)S(1)} %get-tuple-element.102), channel_id=1, source_target_pairs={{0,4},{4,8},{8,12},{12,14},{14,10},{10,6},{6,2},{2,0},{1,5},{5,9},... | collective-permute-start | bytes 626696 | tf_op jit(solution)/shard_map/ppermute | solution.py:551
  97.3 0.3 collective-permute-start.21
  97.7 1.9 %collective-permute-start.27 = (bf16[80,2048]{1,0:T(8,128)(2,1)S(1)}, bf16[80,2048]{1,0:T(8,128)(2,1)S(1)}, u32[]{:S(2)}, u32[]{:S(2)}) collective-permute-start(bf16[80,2048]{1,0:T(8,128)(2,1)S(1)} %shard_map.105), channel_id=1, source_target_pairs={{0,4},{4,8},{8,12},{12,14},{14,10},{10,6},{6,2},{2,0},{1,5},{5,9},... | collective-permute-start | bytes 983048 | tf_op jit(solution)/shard_map/ppermute | solution.py:551
  99.6 3.8 %collective-permute-done.17.b = bf16[48,2176]{1,0:T(8,128)(2,1)S(1)} collective-permute-done((bf16[48,2176]{1,0:T(8,128)(2,1)S(1)}, bf16[48,2176]{1,0:T(8,128)(2,1)S(1)}, u32[]{:S(2)}, u32[]{:S(2)}) %collective-permute-start.17) | collective-permute-done | bytes 208928 | tf_op jit(solution)/shard_map/ppermute | solution.py:551
  103.4 0.3 collective-permute-start.18
  103.7 1.9 %collective-permute-start.24 = (bf16[48,2176]{1,0:T(8,128)(2,1)S(1)}, bf16[48,2176]{1,0:T(8,128)(2,1)S(1)}, u32[]{:S(2)}, u32[]{:S(2)}) collective-permute-start(bf16[48,2176]{1,0:T(8,128)(2,1)S(1)} %shard_map.102), channel_id=1, source_target_pairs={{0,4},{4,8},{8,12},{12,14},{14,10},{10,6},{6,2},{2,0},{1,5},{5,9},... | collective-permute-start | bytes 626696 | tf_op jit(solution)/shard_map/ppermute | solution.py:551
  105.6 6.4 %collective-permute-done.18.b = bf16[48,2176]{1,0:T(8,128)(2,1)S(1)} collective-permute-done((bf16[48,2176]{1,0:T(8,128)(2,1)S(1)}, bf16[48,2176]{1,0:T(8,128)(2,1)S(1)}, u32[]{:S(2)}, u32[]{:S(2)}) %collective-permute-start.18) | collective-permute-done | bytes 208928 | tf_op jit(solution)/shard_map/ppermute | solution.py:551
  112.0 0.3 collective-permute-start.19
  112.3 1.9 %collective-permute-start.25 = (bf16[48,2176]{1,0:T(8,128)(2,1)S(1)}, bf16[48,2176]{1,0:T(8,128)(2,1)S(1)}, u32[]{:S(2)}, u32[]{:S(2)}) collective-permute-start(bf16[48,2176]{1,0:T(8,128)(2,1)S(1)} %shard_map.103), channel_id=1, source_target_pairs={{0,4},{4,8},{8,12},{12,14},{14,10},{10,6},{6,2},{2,0},{1,5},{5,9},... | collective-permute-start | bytes 626696 | tf_op jit(solution)/shard_map/ppermute | solution.py:551
  114.3 0.3 collective-permute-start.22
  114.6 1.9 %collective-permute-start.28 = (bf16[80,2048]{1,0:T(8,128)(2,1)S(1)}, bf16[80,2048]{1,0:T(8,128)(2,1)S(1)}, u32[]{:S(2)}, u32[]{:S(2)}) collective-permute-start(bf16[80,2048]{1,0:T(8,128)(2,1)S(1)} %shard_map.106), channel_id=1, source_target_pairs={{0,4},{4,8},{8,12},{12,14},{14,10},{10,6},{6,2},{2,0},{1,5},{5,9},... | collective-permute-start | bytes 983048 | tf_op jit(solution)/shard_map/ppermute | solution.py:551
  116.5 3.7 %collective-permute-done.19.b = bf16[48,2176]{1,0:T(8,128)(2,1)S(1)} collective-permute-done((bf16[48,2176]{1,0:T(8,128)(2,1)S(1)}, bf16[48,2176]{1,0:T(8,128)(2,1)S(1)}, u32[]{:S(2)}, u32[]{:S(2)}) %collective-permute-start.19) | collective-permute-done | bytes 208928 | tf_op jit(solution)/shard_map/ppermute | solution.py:551
  120.2 0.3 collective-permute-start.20
  120.5 1.9 %collective-permute-start.26 = (bf16[48,2176]{1,0:T(8,128)(2,1)S(1)}, bf16[48,2176]{1,0:T(8,128)(2,1)S(1)}, u32[]{:S(2)}, u32[]{:S(2)}) collective-permute-start(bf16[48,2176]{1,0:T(8,128)(2,1)S(1)} %shard_map.104), channel_id=1, source_target_pairs={{0,4},{4,8},{8,12},{12,14},{14,10},{10,6},{6,2},{2,0},{1,5},{5,9},... | collective-permute-start | bytes 626696 | tf_op jit(solution)/shard_map/ppermute | solution.py:551
  122.4 1.9 %collective-permute-done.22.short_up = bf16[80,2048]{1,0:T(8,128)(2,1)S(1)} collective-permute-done((bf16[80,2048]{1,0:T(8,128)(2,1)S(1)}, bf16[80,2048]{1,0:T(8,128)(2,1)S(1)}, u32[]{:S(2)}, u32[]{:S(2)}) %collective-permute-start.22) | collective-permute-done | bytes 327712 | tf_op jit(solution)/shard_map/ppermute | solution.py:551
  124.4 0.4 collective-permute-done.28.short_down
  124.7 1.9 %collective-permute-done.20.long_up = bf16[48,2176]{1,0:T(8,128)(2,1)S(1)} collective-permute-done((bf16[48,2176]{1,0:T(8,128)(2,1)S(1)}, bf16[48,2176]{1,0:T(8,128)(2,1)S(1)}, u32[]{:S(2)}, u32[]{:S(2)}) %collective-permute-start.20) | collective-permute-done | bytes 208928 | tf_op jit(solution)/shard_map/ppermute | solution.py:551
  126.6 0.4 collective-permute-done.26.long_down
  127.0 1.3 %shard_map.107 = (bf16[128,2048]{1,0:T(8,128)(2,1)}, bf16[8,128]{1,0:T(8,128)(2,1)}) custom-call(s32[8,128]{1,0:T(8,128)S(1)} %bitcast.6, bf16[128,128]{1,0:T(8,128)(2,1)S(1)} %get-tuple-element.55.order_up, bf16[128,128]{1,0:T(8,128)(2,1)S(1)} %get-tuple-element.56.order_down, bf16[128,2176]{1,0:T(8,128)(2,1)S(1)} %get-tuple-element.70.mine, ...), custom_call_target="tpu_custom_call" | custom-call | tf_op jit(solution)/shard_map/pallas_call | solution.py:484
  (49 shorter events, 1.2 us)
Async XLA Ops:
  0.6 31.1 %collective-permute-start = (bf16[2,2048,384]{2,1,0:T(8,128)(2,1)}, bf16[2,2048,384]{2,1,0:T(8,128)(2,1)}, u32[]{:S(2)}, u32[]{:S(2)}) collective-permute-start(bf16[2,2048,384]{2,1,0:T(8,128)(2,1)} %gate.1), channel_id=1, source_target_pairs={{0,1},{1,0},{2,3},{3,2},{4,5},{5,4},{6,7},{7,6},{8,9},{9,8},{10,11... | collective-permute-start | bytes 9437192 | tf_op jit(solution)/shard_map/ppermute | solution.py:557
  1.1 30.6 %collective-permute-start.3 = (bf16[2,2048,384]{2,1,0:T(8,128)(2,1)}, bf16[2,2048,384]{2,1,0:T(8,128)(2,1)}, u32[]{:S(2)}, u32[]{:S(2)}) collective-permute-start(bf16[2,2048,384]{2,1,0:T(8,128)(2,1)} %up.1), channel_id=1, source_target_pairs={{0,1},{1,0},{2,3},{3,2},{4,5},{5,4},{6,7},{7,6},{8,9},{9,8},{10,11... | collective-permute-start | bytes 9437192 | tf_op jit(solution)/shard_map/ppermute | solution.py:557
  1.2 30.5 %collective-permute-start.4 = (bf16[2,384,2048]{2,1,0:T(8,128)(2,1)}, bf16[2,384,2048]{2,1,0:T(8,128)(2,1)}, u32[]{:S(2)}, u32[]{:S(2)}) collective-permute-start(bf16[2,384,2048]{2,1,0:T(8,128)(2,1)} %down.1), channel_id=1, source_target_pairs={{0,1},{1,0},{2,3},{3,2},{4,5},{5,4},{6,7},{7,6},{8,9},{9,8},{10,11... | collective-permute-start | bytes 9437192 | tf_op jit(solution)/shard_map/ppermute | solution.py:557
  4.3 27.3 %collective-permute-start.1 = (bf16[128,4224]{1,0:T(8,128)(2,1)}, bf16[128,4224]{1,0:T(8,128)(2,1)S(1)}, u32[]{:S(2)}, u32[]{:S(2)}) collective-permute-start(bf16[128,4224]{1,0:T(8,128)(2,1)} %get-tuple-element.58), channel_id=1, source_target_pairs={{0,4},{4,8},{8,12},{12,14},{14,10},{10,6},{6,2},{2,0},{1,5},{5,9},... | collective-permute-start | bytes 3244040 | tf_op jit(solution)/shard_map/ppermute | solution.py:548
  7.1 26.5 %collective-permute-start.2 = (bf16[128,4224]{1,0:T(8,128)(2,1)S(1)}, bf16[128,4224]{1,0:T(8,128)(2,1)S(1)}, u32[]{:S(2)}, u32[]{:S(2)}) collective-permute-start(bf16[128,4224]{1,0:T(8,128)(2,1)S(1)} %get-tuple-element.59), channel_id=1, source_target_pairs={{4,0},{8,4},{12,8},{14,12},{10,14},{6,10},{2,6},{0,2},{5,1},{9,5},... | collective-permute-start | bytes 3244040 | tf_op jit(solution)/shard_map/ppermute | solution.py:548
  31.7 4.1 %copy-start = (bf16[128,4224]{1,0:T(8,128)(2,1)}, bf16[128,4224]{1,0:T(8,128)(2,1)S(1)}, u32[]{:S(2)}) copy-start(bf16[128,4224]{1,0:T(8,128)(2,1)S(1)} %collective-permute-done.1.refs_0_) | copy-start | bytes 3244036
  31.8 15.3 %collective-permute-start.5 = (bf16[64,4224]{1,0:T(8,128)(2,1)S(1)}, bf16[64,4224]{1,0:T(8,128)(2,1)S(1)}, u32[]{:S(2)}, u32[]{:S(2)}) collective-permute-start(bf16[64,4224]{1,0:T(8,128)(2,1)S(1)} %get-tuple-element.74), channel_id=1, source_target_pairs={{0,4},{4,8},{8,12},{12,14},{14,10},{10,6},{6,2},{2,0},{1,5},{5,9},... | collective-permute-start | bytes 1622024 | tf_op jit(solution)/shard_map/ppermute | solution.py:548
  33.7 15.3 %collective-permute-start.7 = (bf16[64,4224]{1,0:T(8,128)(2,1)S(1)}, bf16[64,4224]{1,0:T(8,128)(2,1)S(1)}, u32[]{:S(2)}, u32[]{:S(2)}) collective-permute-start(bf16[64,4224]{1,0:T(8,128)(2,1)S(1)} %get-tuple-element.76), channel_id=1, source_target_pairs={{4,0},{8,4},{12,8},{14,12},{10,14},{6,10},{2,6},{0,2},{5,1},{9,5},... | collective-permute-start | bytes 1622024 | tf_op jit(solution)/shard_map/ppermute | solution.py:548
  34.0 25.3 %collective-permute-start.6 = (bf16[64,4224]{1,0:T(8,128)(2,1)S(1)}, bf16[64,4224]{1,0:T(8,128)(2,1)S(1)}, u32[]{:S(2)}, u32[]{:S(2)}) collective-permute-start(bf16[64,4224]{1,0:T(8,128)(2,1)S(1)} %get-tuple-element.75), channel_id=1, source_target_pairs={{0,4},{4,8},{8,12},{12,14},{14,10},{10,6},{6,2},{2,0},{1,5},{5,9},... | collective-permute-start | bytes 1622024 | tf_op jit(solution)/shard_map/ppermute | solution.py:548
  35.8 5.1 %copy-start.2 = (bf16[128,2048]{1,0:T(8,128)(2,1)S(1)}, bf16[128,2048]{1,0:T(8,128)(2,1)}, u32[]{:S(2)}) copy-start(bf16[128,2048]{1,0:T(8,128)(2,1)} %refs_0_.1) | copy-start | bytes 1572868
  35.8 5.1 %copy-start.3 = (bf16[128,2048]{1,0:T(8,128)(2,1)S(1)}, bf16[128,2048]{1,0:T(8,128)(2,1)}, u32[]{:S(2)}) copy-start(bf16[128,2048]{1,0:T(8,128)(2,1)} %refs_1_.1) | copy-start | bytes 1572868
  35.8 25.4 %collective-permute-start.8 = (bf16[64,4224]{1,0:T(8,128)(2,1)S(1)}, bf16[64,4224]{1,0:T(8,128)(2,1)S(1)}, u32[]{:S(2)}, u32[]{:S(2)}) collective-permute-start(bf16[64,4224]{1,0:T(8,128)(2,1)S(1)} %get-tuple-element.77), channel_id=1, source_target_pairs={{4,0},{8,4},{12,8},{14,12},{10,14},{6,10},{2,6},{0,2},{5,1},{9,5},... | collective-permute-start | bytes 1622024 | tf_op jit(solution)/shard_map/ppermute | solution.py:548
  40.9 8.3 %copy-start.1 = (bf16[128,4224]{1,0:T(8,128)(2,1)S(1)}, bf16[128,4224]{1,0:T(8,128)(2,1)}, u32[]{:S(2)}) copy-start(bf16[128,4224]{1,0:T(8,128)(2,1)} %copy-done) | copy-start | bytes 3244036
  47.1 24.5 %collective-permute-start.9 = (bf16[64,4224]{1,0:T(8,128)(2,1)S(1)}, bf16[64,4224]{1,0:T(8,128)(2,1)S(1)}, u32[]{:S(2)}, u32[]{:S(2)}) collective-permute-start(bf16[64,4224]{1,0:T(8,128)(2,1)S(1)} %collective-permute-done.5.refs_0_), channel_id=1, source_target_pairs={{0,4},{4,8},{8,12},{12,14},{14,10},{10,6},{6,2},{2,0},{1,5},{5,9},... | collective-permute-start | bytes 1622024 | tf_op jit(solution)/shard_map/ppermute | solution.py:548
  49.0 24.5 %collective-permute-start.10 = (bf16[64,4224]{1,0:T(8,128)(2,1)S(1)}, bf16[64,4224]{1,0:T(8,128)(2,1)S(1)}, u32[]{:S(2)}, u32[]{:S(2)}) collective-permute-start(bf16[64,4224]{1,0:T(8,128)(2,1)S(1)} %collective-permute-done.7.refs_2_), channel_id=1, source_target_pairs={{4,0},{8,4},{12,8},{14,12},{10,14},{6,10},{2,6},{0,2},{5,1},{9,5},... | collective-permute-start | bytes 1622024 | tf_op jit(solution)/shard_map/ppermute | solution.py:548
  59.3 20.6 %collective-permute-start.11 = (bf16[48,4224]{1,0:T(8,128)(2,1)S(1)}, bf16[48,4224]{1,0:T(8,128)(2,1)S(1)}, u32[]{:S(2)}, u32[]{:S(2)}) collective-permute-start(bf16[48,4224]{1,0:T(8,128)(2,1)S(1)} %slice.36), channel_id=1, source_target_pairs={{0,4},{4,8},{8,12},{12,14},{14,10},{10,6},{6,2},{2,0},{1,5},{5,9},... | collective-permute-start | bytes 1216520 | tf_op jit(solution)/shard_map/ppermute | solution.py:548
  61.2 19.6 %collective-permute-start.12 = (bf16[48,4224]{1,0:T(8,128)(2,1)S(1)}, bf16[48,4224]{1,0:T(8,128)(2,1)S(1)}, u32[]{:S(2)}, u32[]{:S(2)}) collective-permute-start(bf16[48,4224]{1,0:T(8,128)(2,1)S(1)} %slice.37), channel_id=1, source_target_pairs={{4,0},{8,4},{12,8},{14,12},{10,14},{6,10},{2,6},{0,2},{5,1},{9,5},... | collective-permute-start | bytes 1216520 | tf_op jit(solution)/shard_map/ppermute | solution.py:548
  71.6 17.0 %collective-permute-start.13 = (bf16[48,4224]{1,0:T(8,128)(2,1)S(1)}, bf16[48,4224]{1,0:T(8,128)(2,1)S(1)}, u32[]{:S(2)}, u32[]{:S(2)}) collective-permute-start(bf16[48,4224]{1,0:T(8,128)(2,1)S(1)} %slice.38), channel_id=1, source_target_pairs={{0,4},{4,8},{8,12},{12,14},{14,10},{10,6},{6,2},{2,0},{1,5},{5,9},... | collective-permute-start | bytes 1216520 | tf_op jit(solution)/shard_map/ppermute | solution.py:548
  73.5 16.0 %collective-permute-start.14 = (bf16[48,4224]{1,0:T(8,128)(2,1)S(1)}, bf16[48,4224]{1,0:T(8,128)(2,1)S(1)}, u32[]{:S(2)}, u32[]{:S(2)}) collective-permute-start(bf16[48,4224]{1,0:T(8,128)(2,1)S(1)} %slice.39), channel_id=1, source_target_pairs={{4,0},{8,4},{12,8},{14,12},{10,14},{6,10},{2,6},{0,2},{5,1},{9,5},... | collective-permute-start | bytes 1216520 | tf_op jit(solution)/shard_map/ppermute | solution.py:548
  86.1 9.1 %collective-permute-start.15 = (bf16[64,2048]{1,0:T(8,128)(2,1)S(1)}, bf16[64,2048]{1,0:T(8,128)(2,1)S(1)}, u32[]{:S(2)}, u32[]{:S(2)}) collective-permute-start(bf16[64,2048]{1,0:T(8,128)(2,1)S(1)} %shard_map.95), channel_id=1, source_target_pairs={{4,0},{8,4},{12,8},{14,12},{10,14},{6,10},{2,6},{0,2},{5,1},{9,5},... | collective-permute-start | bytes 786440 | tf_op jit(solution)/shard_map/ppermute | solution.py:551
  87.0 8.2 %collective-permute-start.16 = (bf16[64,2048]{1,0:T(8,128)(2,1)S(1)}, bf16[64,2048]{1,0:T(8,128)(2,1)S(1)}, u32[]{:S(2)}, u32[]{:S(2)}) collective-permute-start(bf16[64,2048]{1,0:T(8,128)(2,1)S(1)} %shard_map.96), channel_id=1, source_target_pairs={{0,4},{4,8},{8,12},{12,14},{14,10},{10,6},{6,2},{2,0},{1,5},{5,9},... | collective-permute-start | bytes 786440 | tf_op jit(solution)/shard_map/ppermute | solution.py:551
  95.2 8.1 %collective-permute-start.17 = (bf16[48,2176]{1,0:T(8,128)(2,1)S(1)}, bf16[48,2176]{1,0:T(8,128)(2,1)S(1)}, u32[]{:S(2)}, u32[]{:S(2)}) collective-permute-start(bf16[48,2176]{1,0:T(8,128)(2,1)S(1)} %get-tuple-element.94), channel_id=1, source_target_pairs={{4,0},{8,4},{12,8},{14,12},{10,14},{6,10},{2,6},{0,2},{5,1},{9,5},... | collective-permute-start | bytes 626696 | tf_op jit(solution)/shard_map/ppermute | solution.py:551
  95.4 8.2 %collective-permute-start.23 = (bf16[48,2176]{1,0:T(8,128)(2,1)S(1)}, bf16[48,2176]{1,0:T(8,128)(2,1)S(1)}, u32[]{:S(2)}, u32[]{:S(2)}) collective-permute-start(bf16[48,2176]{1,0:T(8,128)(2,1)S(1)} %get-tuple-element.102), channel_id=1, source_target_pairs={{0,4},{4,8},{8,12},{12,14},{14,10},{10,6},{6,2},{2,0},{1,5},{5,9},... | collective-permute-start | bytes 626696 | tf_op jit(solution)/shard_map/ppermute | solution.py:551
  97.3 16.9 %collective-permute-start.21 = (bf16[80,2048]{1,0:T(8,128)(2,1)S(1)}, bf16[80,2048]{1,0:T(8,128)(2,1)S(1)}, u32[]{:S(2)}, u32[]{:S(2)}) collective-permute-start(bf16[80,2048]{1,0:T(8,128)(2,1)S(1)} %shard_map.100), channel_id=1, source_target_pairs={{4,0},{8,4},{12,8},{14,12},{10,14},{6,10},{2,6},{0,2},{5,1},{9,5},... | collective-permute-start | bytes 983048 | tf_op jit(solution)/shard_map/ppermute | solution.py:551
  97.6 29.4 %copy-start.4 = (s32[128,8]{0,1:T(8,128)S(1)}, s32[128,8]{0,1:T(8,128)}, u32[]{:S(2)}) copy-start(s32[128,8]{0,1:T(8,128)} %param.9) | copy-start | bytes 12292
  97.7 16.9 %collective-permute-start.27 = (bf16[80,2048]{1,0:T(8,128)(2,1)S(1)}, bf16[80,2048]{1,0:T(8,128)(2,1)S(1)}, u32[]{:S(2)}, u32[]{:S(2)}) collective-permute-start(bf16[80,2048]{1,0:T(8,128)(2,1)S(1)} %shard_map.105), channel_id=1, source_target_pairs={{0,4},{4,8},{8,12},{12,14},{14,10},{10,6},{6,2},{2,0},{1,5},{5,9},... | collective-permute-start | bytes 983048 | tf_op jit(solution)/shard_map/ppermute | solution.py:551
  103.4 8.6 %collective-permute-start.18 = (bf16[48,2176]{1,0:T(8,128)(2,1)S(1)}, bf16[48,2176]{1,0:T(8,128)(2,1)S(1)}, u32[]{:S(2)}, u32[]{:S(2)}) collective-permute-start(bf16[48,2176]{1,0:T(8,128)(2,1)S(1)} %shard_map.97), channel_id=1, source_target_pairs={{4,0},{8,4},{12,8},{14,12},{10,14},{6,10},{2,6},{0,2},{5,1},{9,5},... | collective-permute-start | bytes 626696 | tf_op jit(solution)/shard_map/ppermute | solution.py:551
  103.7 8.6 %collective-permute-start.24 = (bf16[48,2176]{1,0:T(8,128)(2,1)S(1)}, bf16[48,2176]{1,0:T(8,128)(2,1)S(1)}, u32[]{:S(2)}, u32[]{:S(2)}) collective-permute-start(bf16[48,2176]{1,0:T(8,128)(2,1)S(1)} %shard_map.102), channel_id=1, source_target_pairs={{0,4},{4,8},{8,12},{12,14},{14,10},{10,6},{6,2},{2,0},{1,5},{5,9},... | collective-permute-start | bytes 626696 | tf_op jit(solution)/shard_map/ppermute | solution.py:551
  112.0 8.2 %collective-permute-start.19 = (bf16[48,2176]{1,0:T(8,128)(2,1)S(1)}, bf16[48,2176]{1,0:T(8,128)(2,1)S(1)}, u32[]{:S(2)}, u32[]{:S(2)}) collective-permute-start(bf16[48,2176]{1,0:T(8,128)(2,1)S(1)} %shard_map.98), channel_id=1, source_target_pairs={{4,0},{8,4},{12,8},{14,12},{10,14},{6,10},{2,6},{0,2},{5,1},{9,5},... | collective-permute-start | bytes 626696 | tf_op jit(solution)/shard_map/ppermute | solution.py:551
  112.3 8.2 %collective-permute-start.25 = (bf16[48,2176]{1,0:T(8,128)(2,1)S(1)}, bf16[48,2176]{1,0:T(8,128)(2,1)S(1)}, u32[]{:S(2)}, u32[]{:S(2)}) collective-permute-start(bf16[48,2176]{1,0:T(8,128)(2,1)S(1)} %shard_map.103), channel_id=1, source_target_pairs={{0,4},{4,8},{8,12},{12,14},{14,10},{10,6},{6,2},{2,0},{1,5},{5,9},... | collective-permute-start | bytes 626696 | tf_op jit(solution)/shard_map/ppermute | solution.py:551
  114.3 10.1 %collective-permute-start.22 = (bf16[80,2048]{1,0:T(8,128)(2,1)S(1)}, bf16[80,2048]{1,0:T(8,128)(2,1)S(1)}, u32[]{:S(2)}, u32[]{:S(2)}) collective-permute-start(bf16[80,2048]{1,0:T(8,128)(2,1)S(1)} %shard_map.101), channel_id=1, source_target_pairs={{4,0},{8,4},{12,8},{14,12},{10,14},{6,10},{2,6},{0,2},{5,1},{9,5},... | collective-permute-start | bytes 983048 | tf_op jit(solution)/shard_map/ppermute | solution.py:551
  114.6 10.1 %collective-permute-start.28 = (bf16[80,2048]{1,0:T(8,128)(2,1)S(1)}, bf16[80,2048]{1,0:T(8,128)(2,1)S(1)}, u32[]{:S(2)}, u32[]{:S(2)}) collective-permute-start(bf16[80,2048]{1,0:T(8,128)(2,1)S(1)} %shard_map.106), channel_id=1, source_target_pairs={{0,4},{4,8},{8,12},{12,14},{14,10},{10,6},{6,2},{2,0},{1,5},{5,9},... | collective-permute-start | bytes 983048 | tf_op jit(solution)/shard_map/ppermute | solution.py:551
  120.2 6.4 %collective-permute-start.20 = (bf16[48,2176]{1,0:T(8,128)(2,1)S(1)}, bf16[48,2176]{1,0:T(8,128)(2,1)S(1)}, u32[]{:S(2)}, u32[]{:S(2)}) collective-permute-start(bf16[48,2176]{1,0:T(8,128)(2,1)S(1)} %shard_map.99), channel_id=1, source_target_pairs={{4,0},{8,4},{12,8},{14,12},{10,14},{6,10},{2,6},{0,2},{5,1},{9,5},... | collective-permute-start | bytes 626696 | tf_op jit(solution)/shard_map/ppermute | solution.py:551
  120.5 6.4 %collective-permute-start.26 = (bf16[48,2176]{1,0:T(8,128)(2,1)S(1)}, bf16[48,2176]{1,0:T(8,128)(2,1)S(1)}, u32[]{:S(2)}, u32[]{:S(2)}) collective-permute-start(bf16[48,2176]{1,0:T(8,128)(2,1)S(1)} %shard_map.104), channel_id=1, source_target_pairs={{0,4},{4,8},{8,12},{12,14},{14,10},{10,6},{6,2},{2,0},{1,5},{5,9},... | collective-permute-start | bytes 626696 | tf_op jit(solution)/shard_map/ppermute | solution.py:551

commit v5 on v4

--- a/solution.py
+++ b/solution.py
@@ -193,7 +193,7 @@
 
 
 def pack_kernel(per_group, tokens, cotangent, ids, weights, *refs):
-    up_block, down_block, table_out, *orders, ids_here, weights_here, rows_here, sems = refs
+    outs, table_out, orders, (ids_here, weights_here, rows_here, *blocks, sems, out_sems) = refs[:2], refs[2], refs[3:5], refs[5:]
     rows, width = tokens.shape
     half = lax.axis_size("grp") // 2
     small = (
@@ -264,20 +264,26 @@
         )
         orders[i][...] = jnp.where(from_row == target, 1.0, 0.0).astype(jnp.bfloat16)
     table_out[...] = table.T.astype(jnp.bfloat16)
-    blocks = up_block, down_block
     far = (sublane >= first_experts[2]) & (sublane < first_experts[2] + per_group)
     for block, order, first in zip(blocks, orders, firsts):
         mine = jnp.where(far & (first == 0), 0.0, table).astype(jnp.bfloat16)
-        block[:, 2 * width :] = lax.dot_general(order[...], mine, NT, preferred_element_type=jnp.float32).astype(
-            jnp.bfloat16
-        )
-    for copy in large:
+        mine = lax.dot_general(order[...], mine, NT, preferred_element_type=jnp.float32)
+        low = mine[rows // 2 :]
+        block[: rows // 2, 2 * width :] = (mine[: rows // 2] + pltpu.roll(low, SLOT, 1)).astype(jnp.bfloat16)
+        block[rows // 2 :, 2 * width :] = low.astype(jnp.bfloat16)
+    going = []
+    for half_at, copy in enumerate(large):
         copy.wait()
-    for block, order in zip(blocks, orders):
-        for lanes in (slice(0, width), slice(width, 2 * width)):
+        lanes = slice(half_at * width, (half_at + 1) * width)
+        sent = pl.ds(half_at * width, width + half_at * LANES)
+        for way, (block, order, out) in enumerate(zip(blocks, orders, outs)):
             block[:, lanes] = jnp.dot(order[...], rows_here[:, lanes], preferred_element_type=jnp.float32).astype(
                 jnp.bfloat16
             )
+            going.append(pltpu.make_async_copy(block.at[:, sent], out.at[:, sent], out_sems.at[half_at, way]))
+            going[-1].start()
+    for copy in going:
+        copy.wait()
 
 
 def pack(per_group, tokens, cotangent, ids, weights):
@@ -294,12 +300,15 @@
             order,
         ),
         in_specs=[ANYWHERE] * 4,
-        out_specs=(IN_VMEM,) * 5,
+        out_specs=(ANYWHERE, ANYWHERE, IN_VMEM, IN_VMEM, IN_VMEM),
         scratch_shapes=[
             pltpu.VMEM((ids.shape[1], rows), jnp.int32),
             pltpu.VMEM((ids.shape[1], rows), jnp.bfloat16),
             pltpu.VMEM((rows, 2 * width), jnp.bfloat16),
+            pltpu.VMEM(shape, jnp.bfloat16),
+            pltpu.VMEM(shape, jnp.bfloat16),
             pltpu.SemaphoreType.DMA((4,)),
+            pltpu.SemaphoreType.DMA((2, 2)),
         ],
         compiler_params=pltpu.CompilerParams(vmem_limit_bytes=7 * MIB),
     )(*(in_hbm(a) for a in (tokens, cotangent, ids.T, weights.T)))
@@ -364,9 +373,17 @@
     per_device, width, both_hidden = loaded[0][0].shape
     hidden = both_hidden // 2
     if given[0].shape[1] > width:
+        tables = []
+        for a in given:
+            if a.shape[1] > 2 * width:
+                tables.append(a[:, 2 * width :].astype(jnp.float32))
+            else:
+                tables.append(pltpu.roll(tables[-1], LANES - SLOT, 1)[: a.shape[0]])
+        if not any(long for long, _, _ in plan):
+            given, tables = given[1::2], tables[1::2]
         x = jnp.concatenate([a[:, :width] for a in given], axis=0)
         g = jnp.concatenate([a[:, width : 2 * width] for a in given], axis=0)
-        table = jnp.concatenate([a[:, 2 * width :] for a in given], axis=0)
+        table = jnp.concatenate(tables, axis=0)
     else:
         x, g, table = (a[...] for a in given)
     spare = -x.shape[0] % (LANES // 2)
@@ -571,7 +588,7 @@
     half, most = ring_total // 2, 6 * block // ring_total
     half_block, cut = block // 2, most // 2
     rest, needed, extra = block - cut, (block + most) // 2 - half_block, half_block - cut
-    long, short = [a[:half_block] for a in came], [a[half_block:] for a in came]
+    long, short = [a[:half_block] for a in came], [a[half_block:, : 2 * width] for a in came]
     long_next, short_next = send(tie(long, loaded_own, *other)), send(tie(short, loaded_own, *other))
     own_plan = ((block, 0, 0),)
     mine, last = experts_call(place, last, (tokens, cotangent, table), own_plan, loaded, False)
@@ -591,7 +608,7 @@
     parts, last = call(last, ((cut, extra, 0),) * 2, *long)
     long_terms.append(parts[0::2])
     lower = parts[1::2]
-    parts, last = call(last, ((0, needed, extra),) * 2, *short, unrolled=True)
+    parts, last = call(last, ((0, needed, extra),) * 2, long[0], short[0], long[1], short[1], unrolled=True)
     short_back = send_back([joined(a, b) for a, b in zip(lower, parts[0::2])])
     carried = parts[1::2]
     parts, last = call(last, ((cut, 0, 0),) * 2, *long_last, unrolled=True)

time: 128 us -> 128 us (level)
    ppermute x7, starting transfers between devices: 2.37 us -> 7.48 us  [send_back(): lax.ppermute(pair[0], 'grp', behind)]
    ppermute x7, starting transfers between devices: 12.7 us -> 7.64 us  [send_back(): lax.ppermute(pair[1], 'grp', ahead)]
  transfers between devices with their start and end apart: 29 -> 29, of which waited for: 11 -> 10; matrix products, arithmetic and copies ran while one was open for 0% -> 0% of each run, Pallas kernels for 44% -> 44%
where the time goes in v5:
time: 128 us
  Pallas kernels  57.7 us (45%)
  waiting for transfers between devices  39.4 us (31%)
  starting transfers between devices  29.7 us (23%)
    pallas_call x6, Pallas kernels, experts_call(): pl.pallas_call(functools.partial(experts_kernel, len(given), plan, unroll...  43.2 us
    ppermute x6, waiting for transfers between devices, send(): lax.ppermute(pair[0], 'grp', ahead)  19.8 us
    ppermute x7, waiting for transfers between devices, send_back(): lax.ppermute(pair[0], 'grp', behind)  17.6 us
    ppermute x6, starting transfers between devices, send(): lax.ppermute(pair[0], 'grp', ahead)  12 us
    pallas_call x2, Pallas kernels, load(): pl.pallas_call(load_kernel, out_shape=(pltpu.VMEM((per_device, width, 2 *...  9.53 us
    ppermute x7, starting transfers between devices, send_back(): lax.ppermute(pair[1], 'grp', ahead)  7.64 us
    ppermute x7, starting transfers between devices, send_back(): lax.ppermute(pair[0], 'grp', behind)  7.48 us
    pallas_call x1, Pallas kernels, pack(): pl.pallas_call(functools.partial(pack_kernel, per_group), out_shape=(jax....  3.05 us
  transfers between devices with their start and end apart: 29, of which 10 were waited for; matrix products, arithmetic and copies ran while one was open for 0% of the time, Pallas kernels for 44%

profile of v5, /device:TPU:0, one launch (start us, length us, event | category | flops | bytes accessed | tf_op | source)
XLA Modules:
  0.0 128.1 jit_solution(17095865931275243194)
XLA Ops:
  0.6 0.5 collective-permute-start
  1.1 0.1 collective-permute-start.3
  1.2 0.4 collective-permute-start.4
  1.7 3.0 %shard_map.86 = (bf16[128,4224]{1,0:T(8,128)(2,1)}, bf16[128,4224]{1,0:T(8,128)(2,1)}, bf16[128,128]{1,0:T(8,128)(2,1)S(1)}, bf16[128,128]{1,0:T(8,128)(2,1)S(1)}, bf16[128,128]{1,0:T(8,128)(2,1)S(1)}) custom-call(bf16[128,2048]{1,0:T(8,128)(2,1)} %refs_0_.1, bf16[128,2048]{1,0:T(8,128)(2,1)} %refs_1_.1, s32[8,128]{1,0:T(8,128)} %bitcast.5, ...), custom_call_target="tpu_custom_call" | custom-call | tf_op jit(solution)/shard_map/pallas_call | solution.py:293
  4.7 2.7 %collective-permute-start.1 = (bf16[128,4224]{1,0:T(8,128)(2,1)}, bf16[128,4224]{1,0:T(8,128)(2,1)S(1)}, u32[]{:S(2)}, u32[]{:S(2)}) collective-permute-start(bf16[128,4224]{1,0:T(8,128)(2,1)} %get-tuple-element.58), channel_id=1, source_target_pairs={{0,4},{4,8},{8,12},{12,14},{14,10},{10,6},{6,2},{2,0},{1,5},{5,9},... | collective-permute-start | bytes 3244040 | tf_op jit(solution)/shard_map/ppermute | solution.py:565
  7.5 4.7 %shard_map.87 = (bf16[2,2048,768]{2,1,0:T(8,128)(2,1)S(1)}, bf16[1536,2048]{1,0:T(8,128)(2,1)S(1)}, bf16[2048,768]{1,0:T(8,128)(2,1)S(1)}, f32[8,128]{1,0:T(8,128)S(1)}) custom-call(s32[2]{0:T(128)S(1)} %pad_add_fusion.after_this.place, bf16[2,2048,384]{2,1,0:T(8,128)(2,1)} %gate.1, bf16[2,2048,384]{2,1,0:T(8,128)(2,1)} %up.1, bf16[2,384,2048]{2,1,0:T(8,128)(2,1)} %down.1), custom_call_target="tpu_custom_call" | custom-call | flops 1 | bytes 25165824 | tf_op jit(solution)/shard_map/pallas_call | solution.py:351
  12.3 19.8 %collective-permute-done.1.refs_0_ = bf16[128,4224]{1,0:T(8,128)(2,1)S(1)} collective-permute-done((bf16[128,4224]{1,0:T(8,128)(2,1)}, bf16[128,4224]{1,0:T(8,128)(2,1)S(1)}, u32[]{:S(2)}, u32[]{:S(2)}) %collective-permute-start.1) | collective-permute-done | bytes 1081376 | tf_op jit(solution)/shard_map/ppermute | solution.py:565
  32.1 1.9 %collective-permute-start.5 = (bf16[64,4224]{1,0:T(8,128)(2,1)S(1)}, bf16[64,4224]{1,0:T(8,128)(2,1)S(1)}, u32[]{:S(2)}, u32[]{:S(2)}) collective-permute-start(bf16[64,4224]{1,0:T(8,128)(2,1)S(1)} %slice.32), channel_id=1, source_target_pairs={{0,4},{4,8},{8,12},{12,14},{14,10},{10,6},{6,2},{2,0},{1,5},{5,9},... | collective-permute-start | bytes 1622024 | tf_op jit(solution)/shard_map/ppermute | solution.py:565
  34.0 0.3 collective-permute-start.7
  34.3 1.9 %collective-permute-start.6 = (bf16[64,4096]{1,0:T(8,128)(2,1)S(1)}, bf16[64,4096]{1,0:T(8,128)(2,1)S(1)}, u32[]{:S(2)}, u32[]{:S(2)}) collective-permute-start(bf16[64,4096]{1,0:T(8,128)(2,1)S(1)} %slice.33), channel_id=1, source_target_pairs={{0,4},{4,8},{8,12},{12,14},{14,10},{10,6},{6,2},{2,0},{1,5},{5,9},... | collective-permute-start | bytes 1572872 | tf_op jit(solution)/shard_map/ppermute | solution.py:565
  36.3 0.3 collective-permute-start.8
  36.5 4.8 %shard_map.88 = (bf16[2,2048,768]{2,1,0:T(8,128)(2,1)S(1)}, bf16[1536,2048]{1,0:T(8,128)(2,1)S(1)}, bf16[2048,768]{1,0:T(8,128)(2,1)S(1)}, f32[8,128]{1,0:T(8,128)S(1)}) custom-call(f32[8,128]{1,0:T(8,128)S(1)} %get-tuple-element.57.after_this, bf16[2,2048,384]{2,1,0:T(8,128)(2,1)} %collective-permute-done.gate, ...), custom_call_target="tpu_custom_call" | custom-call | flops 1 | bytes 25165824 | tf_op jit(solution)/shard_map/pallas_call | solution.py:351
  41.4 6.2 %shard_map.89 = (bf16[128,2176]{1,0:T(8,128)(2,1)S(1)}, f32[8,128]{1,0:T(8,128)S(1)}) custom-call(s32[2]{0:T(128)S(1)} %pad_add_fusion.after_this.place, f32[8,128]{1,0:T(8,128)S(1)} %get-tuple-element.62.after_this, bf16[128,2048]{1,0:T(8,128)(2,1)S(1)} %copy-done.4, bf16[128,2048]{1,0:T(8,128)(2,1)S(1)} %copy-done.5, ...), custom_call_target="tpu_custom_call" | custom-call | flops 1 | bytes 1 | tf_op jit(solution)/shard_map/pallas_call | solution.py:466
  47.5 1.8 %collective-permute-start.9 = (bf16[64,4224]{1,0:T(8,128)(2,1)S(1)}, bf16[64,4224]{1,0:T(8,128)(2,1)S(1)}, u32[]{:S(2)}, u32[]{:S(2)}) collective-permute-start(bf16[64,4224]{1,0:T(8,128)(2,1)S(1)} %collective-permute-done.5.refs_0_), channel_id=1, source_target_pairs={{0,4},{4,8},{8,12},{12,14},{14,10},{10,6},{6,2},{2,0},{1,5},{5,9},... | collective-permute-start | bytes 1622024 | tf_op jit(solution)/shard_map/ppermute | solution.py:565
  49.4 0.2 collective-permute-start.10
  49.6 10.0 %shard_map.90 = (bf16[48,2176]{1,0:T(8,128)(2,1)S(1)}, bf16[80,2048]{1,0:T(8,128)(2,1)S(1)}, bf16[48,2176]{1,0:T(8,128)(2,1)S(1)}, bf16[80,2048]{1,0:T(8,128)(2,1)S(1)}, f32[8,128]{1,0:T(8,128)S(1)}) custom-call(s32[2]{0:T(128)S(1)} %pad_add_fusion.after_this.place, f32[8,128]{1,0:T(8,128)S(1)} %get-tuple-element.71.after_this, ...), custom_call_target="tpu_custom_call" | custom-call | flops 1 | bytes 1 | tf_op jit(solution)/shard_map/pallas_call | solution.py:466
  59.7 1.8 %collective-permute-start.11 = (bf16[48,4096]{1,0:T(8,128)(2,1)S(1)}, bf16[48,4096]{1,0:T(8,128)(2,1)S(1)}, u32[]{:S(2)}, u32[]{:S(2)}) collective-permute-start(bf16[48,4096]{1,0:T(8,128)(2,1)S(1)} %slice.36), channel_id=1, source_target_pairs={{0,4},{4,8},{8,12},{12,14},{14,10},{10,6},{6,2},{2,0},{1,5},{5,9},... | collective-permute-start | bytes 1179656 | tf_op jit(solution)/shard_map/ppermute | solution.py:565
  61.6 0.3 collective-permute-start.12
  61.9 10.1 %shard_map.91 = (bf16[48,2176]{1,0:T(8,128)(2,1)S(1)}, bf16[80,2048]{1,0:T(8,128)(2,1)S(1)}, bf16[48,2176]{1,0:T(8,128)(2,1)S(1)}, bf16[80,2048]{1,0:T(8,128)(2,1)S(1)}, f32[8,128]{1,0:T(8,128)S(1)}) custom-call(s32[2]{0:T(128)S(1)} %pad_add_fusion.after_this.place, f32[8,128]{1,0:T(8,128)S(1)} %get-tuple-element.73.after_this, ...), custom_call_target="tpu_custom_call" | custom-call | flops 1 | bytes 1 | tf_op jit(solution)/shard_map/pallas_call | solution.py:466
  72.0 1.8 %collective-permute-start.13 = (bf16[48,4224]{1,0:T(8,128)(2,1)S(1)}, bf16[48,4224]{1,0:T(8,128)(2,1)S(1)}, u32[]{:S(2)}, u32[]{:S(2)}) collective-permute-start(bf16[48,4224]{1,0:T(8,128)(2,1)S(1)} %slice.38), channel_id=1, source_target_pairs={{0,4},{4,8},{8,12},{12,14},{14,10},{10,6},{6,2},{2,0},{1,5},{5,9},... | collective-permute-start | bytes 1216520 | tf_op jit(solution)/shard_map/ppermute | solution.py:565
  73.9 0.5 collective-permute-start.14
  74.4 5.9 %shard_map.92 = (bf16[48,2176]{1,0:T(8,128)(2,1)S(1)}, bf16[16,2048]{1,0:T(8,128)(2,1)S(1)}, bf16[48,2176]{1,0:T(8,128)(2,1)S(1)}, bf16[16,2048]{1,0:T(8,128)(2,1)S(1)}, f32[8,128]{1,0:T(8,128)S(1)}) custom-call(s32[2]{0:T(128)S(1)} %pad_add_fusion.after_this.place, f32[8,128]{1,0:T(8,128)S(1)} %get-tuple-element.79.after_this, ...), custom_call_target="tpu_custom_call" | custom-call | flops 1 | bytes 1 | tf_op jit(solution)/shard_map/pallas_call | solution.py:466
  80.4 0.2 collective-permute-done.12.refs_3_
  80.5 5.3 %shard_map.93 = (bf16[48,2048]{1,0:T(8,128)(2,1)S(1)}, bf16[48,128]{1,0:T(8,128)(2,1)S(1)}, bf16[48,2048]{1,0:T(8,128)(2,1)S(1)}, bf16[48,128]{1,0:T(8,128)(2,1)S(1)}, f32[8,128]{1,0:T(8,128)S(1)}) custom-call(s32[2]{0:T(128)S(1)} %pad_add_fusion.after_this.place, f32[8,128]{1,0:T(8,128)S(1)} %get-tuple-element.83.after_this, ...), custom_call_target="tpu_custom_call" | custom-call | flops 1 | bytes 1 | tf_op jit(solution)/shard_map/pallas_call | solution.py:466
  85.9 1.6 %collective-permute-start.15 = (bf16[64,2048]{1,0:T(8,128)(2,1)S(1)}, bf16[64,2048]{1,0:T(8,128)(2,1)S(1)}, u32[]{:S(2)}, u32[]{:S(2)}) collective-permute-start(bf16[64,2048]{1,0:T(8,128)(2,1)S(1)} %shard_map.95), channel_id=1, source_target_pairs={{4,0},{8,4},{12,8},{14,12},{10,14},{6,10},{2,6},{0,2},{5,1},{9,5},... | collective-permute-start | bytes 786440 | tf_op jit(solution)/shard_map/ppermute | solution.py:568
  87.5 0.7 collective-permute-start.16
  88.3 0.9 collective-permute-done.14.refs_1_
  89.2 5.7 %shard_map.94 = (bf16[48,2176]{1,0:T(8,128)(2,1)S(1)}, bf16[48,2176]{1,0:T(8,128)(2,1)S(1)}, f32[8,128]{1,0:T(8,128)}) custom-call(s32[2]{0:T(128)S(1)} %pad_add_fusion.after_this.place, f32[8,128]{1,0:T(8,128)S(1)} %get-tuple-element.86.after_this, bf16[48,4224]{1,0:T(8,128)(2,1)S(1)} %collective-permute-done.13.refs_0_, ...), custom_call_target="tpu_custom_call" | custom-call | flops 1 | bytes 1 | tf_op jit(solution)/shard_map/pallas_call | solution.py:466
  94.9 0.9 collective-permute-start.17
  95.8 1.1 collective-permute-start.23
  97.0 1.0 collective-permute-start.21
  98.0 1.1 collective-permute-start.27
  99.2 3.8 %collective-permute-done.17.b = bf16[48,2176]{1,0:T(8,128)(2,1)S(1)} collective-permute-done((bf16[48,2176]{1,0:T(8,128)(2,1)S(1)}, bf16[48,2176]{1,0:T(8,128)(2,1)S(1)}, u32[]{:S(2)}, u32[]{:S(2)}) %collective-permute-start.17) | collective-permute-done | bytes 208928 | tf_op jit(solution)/shard_map/ppermute | solution.py:568
  103.0 1.0 collective-permute-start.18
  104.1 1.1 collective-permute-start.24
  105.2 6.4 %collective-permute-done.18.b = bf16[48,2176]{1,0:T(8,128)(2,1)S(1)} collective-permute-done((bf16[48,2176]{1,0:T(8,128)(2,1)S(1)}, bf16[48,2176]{1,0:T(8,128)(2,1)S(1)}, u32[]{:S(2)}, u32[]{:S(2)}) %collective-permute-start.18) | collective-permute-done | bytes 208928 | tf_op jit(solution)/shard_map/ppermute | solution.py:568
  111.7 1.0 collective-permute-start.19
  112.7 1.2 collective-permute-start.25
  114.0 1.0 collective-permute-start.22
  115.0 1.1 collective-permute-start.28
  116.2 3.6 %collective-permute-done.19.b = bf16[48,2176]{1,0:T(8,128)(2,1)S(1)} collective-permute-done((bf16[48,2176]{1,0:T(8,128)(2,1)S(1)}, bf16[48,2176]{1,0:T(8,128)(2,1)S(1)}, u32[]{:S(2)}, u32[]{:S(2)}) %collective-permute-start.19) | collective-permute-done | bytes 208928 | tf_op jit(solution)/shard_map/ppermute | solution.py:568
  119.9 1.0 collective-permute-start.20
  120.9 1.2 collective-permute-start.26
  122.1 1.9 %collective-permute-done.22.short_up = bf16[80,2048]{1,0:T(8,128)(2,1)S(1)} collective-permute-done((bf16[80,2048]{1,0:T(8,128)(2,1)S(1)}, bf16[80,2048]{1,0:T(8,128)(2,1)S(1)}, u32[]{:S(2)}, u32[]{:S(2)}) %collective-permute-start.22) | collective-permute-done | bytes 327712 | tf_op jit(solution)/shard_map/ppermute | solution.py:568
  124.0 0.4 collective-permute-done.28.short_down
  124.3 1.9 %collective-permute-done.20.long_up = bf16[48,2176]{1,0:T(8,128)(2,1)S(1)} collective-permute-done((bf16[48,2176]{1,0:T(8,128)(2,1)S(1)}, bf16[48,2176]{1,0:T(8,128)(2,1)S(1)}, u32[]{:S(2)}, u32[]{:S(2)}) %collective-permute-start.20) | collective-permute-done | bytes 208928 | tf_op jit(solution)/shard_map/ppermute | solution.py:568
  126.2 0.6 collective-permute-done.26.long_down
  126.8 1.3 %shard_map.107 = (bf16[128,2048]{1,0:T(8,128)(2,1)}, bf16[8,128]{1,0:T(8,128)(2,1)}) custom-call(s32[8,128]{1,0:T(8,128)S(1)} %bitcast.6, bf16[128,128]{1,0:T(8,128)(2,1)S(1)} %get-tuple-element.55.order_up, bf16[128,128]{1,0:T(8,128)(2,1)S(1)} %get-tuple-element.56.order_down, bf16[128,2176]{1,0:T(8,128)(2,1)S(1)} %get-tuple-element.70.mine, ...), custom_call_target="tpu_custom_call" | custom-call | tf_op jit(solution)/shard_map/pallas_call | solution.py:501
  (55 shorter events, 1.1 us)
Async XLA Ops:
  0.6 31.4 %collective-permute-start = (bf16[2,2048,384]{2,1,0:T(8,128)(2,1)}, bf16[2,2048,384]{2,1,0:T(8,128)(2,1)}, u32[]{:S(2)}, u32[]{:S(2)}) collective-permute-start(bf16[2,2048,384]{2,1,0:T(8,128)(2,1)} %gate.1), channel_id=1, source_target_pairs={{0,1},{1,0},{2,3},{3,2},{4,5},{5,4},{6,7},{7,6},{8,9},{9,8},{10,11... | collective-permute-start | bytes 9437192 | tf_op jit(solution)/shard_map/ppermute | solution.py:574
  1.1 30.9 %collective-permute-start.3 = (bf16[2,2048,384]{2,1,0:T(8,128)(2,1)}, bf16[2,2048,384]{2,1,0:T(8,128)(2,1)}, u32[]{:S(2)}, u32[]{:S(2)}) collective-permute-start(bf16[2,2048,384]{2,1,0:T(8,128)(2,1)} %up.1), channel_id=1, source_target_pairs={{0,1},{1,0},{2,3},{3,2},{4,5},{5,4},{6,7},{7,6},{8,9},{9,8},{10,11... | collective-permute-start | bytes 9437192 | tf_op jit(solution)/shard_map/ppermute | solution.py:574
  1.2 30.9 %collective-permute-start.4 = (bf16[2,384,2048]{2,1,0:T(8,128)(2,1)}, bf16[2,384,2048]{2,1,0:T(8,128)(2,1)}, u32[]{:S(2)}, u32[]{:S(2)}) collective-permute-start(bf16[2,384,2048]{2,1,0:T(8,128)(2,1)} %down.1), channel_id=1, source_target_pairs={{0,1},{1,0},{2,3},{3,2},{4,5},{5,4},{6,7},{7,6},{8,9},{9,8},{10,11... | collective-permute-start | bytes 9437192 | tf_op jit(solution)/shard_map/ppermute | solution.py:574
  4.7 27.3 %collective-permute-start.1 = (bf16[128,4224]{1,0:T(8,128)(2,1)}, bf16[128,4224]{1,0:T(8,128)(2,1)S(1)}, u32[]{:S(2)}, u32[]{:S(2)}) collective-permute-start(bf16[128,4224]{1,0:T(8,128)(2,1)} %get-tuple-element.58), channel_id=1, source_target_pairs={{0,4},{4,8},{8,12},{12,14},{14,10},{10,6},{6,2},{2,0},{1,5},{5,9},... | collective-permute-start | bytes 3244040 | tf_op jit(solution)/shard_map/ppermute | solution.py:565
  7.4 26.5 %collective-permute-start.2 = (bf16[128,4224]{1,0:T(8,128)(2,1)}, bf16[128,4224]{1,0:T(8,128)(2,1)S(1)}, u32[]{:S(2)}, u32[]{:S(2)}) collective-permute-start(bf16[128,4224]{1,0:T(8,128)(2,1)} %get-tuple-element.59), channel_id=1, source_target_pairs={{4,0},{8,4},{12,8},{14,12},{10,14},{6,10},{2,6},{0,2},{5,1},{9,5},... | collective-permute-start | bytes 3244040 | tf_op jit(solution)/shard_map/ppermute | solution.py:565
  32.0 4.2 %copy-start = (bf16[128,4224]{1,0:T(8,128)(2,1)}, bf16[128,4224]{1,0:T(8,128)(2,1)S(1)}, u32[]{:S(2)}) copy-start(bf16[128,4224]{1,0:T(8,128)(2,1)S(1)} %collective-permute-done.1.refs_0_) | copy-start | bytes 3244036
  32.1 15.4 %collective-permute-start.5 = (bf16[64,4224]{1,0:T(8,128)(2,1)S(1)}, bf16[64,4224]{1,0:T(8,128)(2,1)S(1)}, u32[]{:S(2)}, u32[]{:S(2)}) collective-permute-start(bf16[64,4224]{1,0:T(8,128)(2,1)S(1)} %slice.32), channel_id=1, source_target_pairs={{0,4},{4,8},{8,12},{12,14},{14,10},{10,6},{6,2},{2,0},{1,5},{5,9},... | collective-permute-start | bytes 1622024 | tf_op jit(solution)/shard_map/ppermute | solution.py:565
  34.0 2.3 %copy-start.2 = (bf16[128,4224]{1,0:T(8,128)(2,1)}, bf16[128,4224]{1,0:T(8,128)(2,1)S(1)}, u32[]{:S(2)}) copy-start(bf16[128,4224]{1,0:T(8,128)(2,1)S(1)} %collective-permute-done.2.refs_1_) | copy-start | bytes 3244036
  34.0 15.4 %collective-permute-start.7 = (bf16[64,4224]{1,0:T(8,128)(2,1)S(1)}, bf16[64,4224]{1,0:T(8,128)(2,1)S(1)}, u32[]{:S(2)}, u32[]{:S(2)}) collective-permute-start(bf16[64,4224]{1,0:T(8,128)(2,1)S(1)} %slice.34), channel_id=1, source_target_pairs={{4,0},{8,4},{12,8},{14,12},{10,14},{6,10},{2,6},{0,2},{5,1},{9,5},... | collective-permute-start | bytes 1622024 | tf_op jit(solution)/shard_map/ppermute | solution.py:565
  34.3 25.4 %collective-permute-start.6 = (bf16[64,4096]{1,0:T(8,128)(2,1)S(1)}, bf16[64,4096]{1,0:T(8,128)(2,1)S(1)}, u32[]{:S(2)}, u32[]{:S(2)}) collective-permute-start(bf16[64,4096]{1,0:T(8,128)(2,1)S(1)} %slice.33), channel_id=1, source_target_pairs={{0,4},{4,8},{8,12},{12,14},{14,10},{10,6},{6,2},{2,0},{1,5},{5,9},... | collective-permute-start | bytes 1572872 | tf_op jit(solution)/shard_map/ppermute | solution.py:565
  36.2 5.1 %copy-start.4 = (bf16[128,2048]{1,0:T(8,128)(2,1)S(1)}, bf16[128,2048]{1,0:T(8,128)(2,1)}, u32[]{:S(2)}) copy-start(bf16[128,2048]{1,0:T(8,128)(2,1)} %refs_0_.1) | copy-start | bytes 1572868
  36.3 5.1 %copy-start.5 = (bf16[128,2048]{1,0:T(8,128)(2,1)S(1)}, bf16[128,2048]{1,0:T(8,128)(2,1)}, u32[]{:S(2)}) copy-start(bf16[128,2048]{1,0:T(8,128)(2,1)} %refs_1_.1) | copy-start | bytes 1572868
  36.3 25.3 %collective-permute-start.8 = (bf16[64,4096]{1,0:T(8,128)(2,1)S(1)}, bf16[64,4096]{1,0:T(8,128)(2,1)S(1)}, u32[]{:S(2)}, u32[]{:S(2)}) collective-permute-start(bf16[64,4096]{1,0:T(8,128)(2,1)S(1)} %slice.35), channel_id=1, source_target_pairs={{4,0},{8,4},{12,8},{14,12},{10,14},{6,10},{2,6},{0,2},{5,1},{9,5},... | collective-permute-start | bytes 1572872 | tf_op jit(solution)/shard_map/ppermute | solution.py:565
  41.3 8.3 %copy-start.1 = (bf16[128,4224]{1,0:T(8,128)(2,1)S(1)}, bf16[128,4224]{1,0:T(8,128)(2,1)}, u32[]{:S(2)}) copy-start(bf16[128,4224]{1,0:T(8,128)(2,1)} %copy-done) | copy-start | bytes 3244036
  41.3 8.3 %copy-start.3 = (bf16[128,4224]{1,0:T(8,128)(2,1)S(1)}, bf16[128,4224]{1,0:T(8,128)(2,1)}, u32[]{:S(2)}) copy-start(bf16[128,4224]{1,0:T(8,128)(2,1)} %copy-done.2) | copy-start | bytes 3244036
  47.5 24.5 %collective-permute-start.9 = (bf16[64,4224]{1,0:T(8,128)(2,1)S(1)}, bf16[64,4224]{1,0:T(8,128)(2,1)S(1)}, u32[]{:S(2)}, u32[]{:S(2)}) collective-permute-start(bf16[64,4224]{1,0:T(8,128)(2,1)S(1)} %collective-permute-done.5.refs_0_), channel_id=1, source_target_pairs={{0,4},{4,8},{8,12},{12,14},{14,10},{10,6},{6,2},{2,0},{1,5},{5,9},... | collective-permute-start | bytes 1622024 | tf_op jit(solution)/shard_map/ppermute | solution.py:565
  49.4 24.5 %collective-permute-start.10 = (bf16[64,4224]{1,0:T(8,128)(2,1)S(1)}, bf16[64,4224]{1,0:T(8,128)(2,1)S(1)}, u32[]{:S(2)}, u32[]{:S(2)}) collective-permute-start(bf16[64,4224]{1,0:T(8,128)(2,1)S(1)} %collective-permute-done.7.refs_2_), channel_id=1, source_target_pairs={{4,0},{8,4},{12,8},{14,12},{10,14},{6,10},{2,6},{0,2},{5,1},{9,5},... | collective-permute-start | bytes 1622024 | tf_op jit(solution)/shard_map/ppermute | solution.py:565
  59.7 20.6 %collective-permute-start.11 = (bf16[48,4096]{1,0:T(8,128)(2,1)S(1)}, bf16[48,4096]{1,0:T(8,128)(2,1)S(1)}, u32[]{:S(2)}, u32[]{:S(2)}) collective-permute-start(bf16[48,4096]{1,0:T(8,128)(2,1)S(1)} %slice.36), channel_id=1, source_target_pairs={{0,4},{4,8},{8,12},{12,14},{14,10},{10,6},{6,2},{2,0},{1,5},{5,9},... | collective-permute-start | bytes 1179656 | tf_op jit(solution)/shard_map/ppermute | solution.py:565
  61.6 18.9 %collective-permute-start.12 = (bf16[48,4096]{1,0:T(8,128)(2,1)S(1)}, bf16[48,4096]{1,0:T(8,128)(2,1)S(1)}, u32[]{:S(2)}, u32[]{:S(2)}) collective-permute-start(bf16[48,4096]{1,0:T(8,128)(2,1)S(1)} %slice.37), channel_id=1, source_target_pairs={{4,0},{8,4},{12,8},{14,12},{10,14},{6,10},{2,6},{0,2},{5,1},{9,5},... | collective-permute-start | bytes 1179656 | tf_op jit(solution)/shard_map/ppermute | solution.py:565
  72.0 16.3 %collective-permute-start.13 = (bf16[48,4224]{1,0:T(8,128)(2,1)S(1)}, bf16[48,4224]{1,0:T(8,128)(2,1)S(1)}, u32[]{:S(2)}, u32[]{:S(2)}) collective-permute-start(bf16[48,4224]{1,0:T(8,128)(2,1)S(1)} %slice.38), channel_id=1, source_target_pairs={{0,4},{4,8},{8,12},{12,14},{14,10},{10,6},{6,2},{2,0},{1,5},{5,9},... | collective-permute-start | bytes 1216520 | tf_op jit(solution)/shard_map/ppermute | solution.py:565
  73.9 15.3 %collective-permute-start.14 = (bf16[48,4224]{1,0:T(8,128)(2,1)S(1)}, bf16[48,4224]{1,0:T(8,128)(2,1)S(1)}, u32[]{:S(2)}, u32[]{:S(2)}) collective-permute-start(bf16[48,4224]{1,0:T(8,128)(2,1)S(1)} %slice.39), channel_id=1, source_target_pairs={{4,0},{8,4},{12,8},{14,12},{10,14},{6,10},{2,6},{0,2},{5,1},{9,5},... | collective-permute-start | bytes 1216520 | tf_op jit(solution)/shard_map/ppermute | solution.py:565
  85.9 9.0 %collective-permute-start.15 = (bf16[64,2048]{1,0:T(8,128)(2,1)S(1)}, bf16[64,2048]{1,0:T(8,128)(2,1)S(1)}, u32[]{:S(2)}, u32[]{:S(2)}) collective-permute-start(bf16[64,2048]{1,0:T(8,128)(2,1)S(1)} %shard_map.95), channel_id=1, source_target_pairs={{4,0},{8,4},{12,8},{14,12},{10,14},{6,10},{2,6},{0,2},{5,1},{9,5},... | collective-permute-start | bytes 786440 | tf_op jit(solution)/shard_map/ppermute | solution.py:568
  87.5 7.3 %collective-permute-start.16 = (bf16[64,2048]{1,0:T(8,128)(2,1)S(1)}, bf16[64,2048]{1,0:T(8,128)(2,1)S(1)}, u32[]{:S(2)}, u32[]{:S(2)}) collective-permute-start(bf16[64,2048]{1,0:T(8,128)(2,1)S(1)} %shard_map.96), channel_id=1, source_target_pairs={{0,4},{4,8},{8,12},{12,14},{14,10},{10,6},{6,2},{2,0},{1,5},{5,9},... | collective-permute-start | bytes 786440 | tf_op jit(solution)/shard_map/ppermute | solution.py:568
  94.9 8.1 %collective-permute-start.17 = (bf16[48,2176]{1,0:T(8,128)(2,1)S(1)}, bf16[48,2176]{1,0:T(8,128)(2,1)S(1)}, u32[]{:S(2)}, u32[]{:S(2)}) collective-permute-start(bf16[48,2176]{1,0:T(8,128)(2,1)S(1)} %get-tuple-element.94), channel_id=1, source_target_pairs={{4,0},{8,4},{12,8},{14,12},{10,14},{6,10},{2,6},{0,2},{5,1},{9,5},... | collective-permute-start | bytes 626696 | tf_op jit(solution)/shard_map/ppermute | solution.py:568
  95.8 8.2 %collective-permute-start.23 = (bf16[48,2176]{1,0:T(8,128)(2,1)S(1)}, bf16[48,2176]{1,0:T(8,128)(2,1)S(1)}, u32[]{:S(2)}, u32[]{:S(2)}) collective-permute-start(bf16[48,2176]{1,0:T(8,128)(2,1)S(1)} %get-tuple-element.102), channel_id=1, source_target_pairs={{0,4},{4,8},{8,12},{12,14},{14,10},{10,6},{6,2},{2,0},{1,5},{5,9},... | collective-permute-start | bytes 626696 | tf_op jit(solution)/shard_map/ppermute | solution.py:568
  97.0 16.9 %collective-permute-start.21 = (bf16[80,2048]{1,0:T(8,128)(2,1)S(1)}, bf16[80,2048]{1,0:T(8,128)(2,1)S(1)}, u32[]{:S(2)}, u32[]{:S(2)}) collective-permute-start(bf16[80,2048]{1,0:T(8,128)(2,1)S(1)} %shard_map.100), channel_id=1, source_target_pairs={{4,0},{8,4},{12,8},{14,12},{10,14},{6,10},{2,6},{0,2},{5,1},{9,5},... | collective-permute-start | bytes 983048 | tf_op jit(solution)/shard_map/ppermute | solution.py:568
  98.0 28.8 %copy-start.6 = (s32[128,8]{0,1:T(8,128)S(1)}, s32[128,8]{0,1:T(8,128)}, u32[]{:S(2)}) copy-start(s32[128,8]{0,1:T(8,128)} %param.9) | copy-start | bytes 12292
  98.0 16.9 %collective-permute-start.27 = (bf16[80,2048]{1,0:T(8,128)(2,1)S(1)}, bf16[80,2048]{1,0:T(8,128)(2,1)S(1)}, u32[]{:S(2)}, u32[]{:S(2)}) collective-permute-start(bf16[80,2048]{1,0:T(8,128)(2,1)S(1)} %shard_map.105), channel_id=1, source_target_pairs={{0,4},{4,8},{8,12},{12,14},{14,10},{10,6},{6,2},{2,0},{1,5},{5,9},... | collective-permute-start | bytes 983048 | tf_op jit(solution)/shard_map/ppermute | solution.py:568
  103.0 8.6 %collective-permute-start.18 = (bf16[48,2176]{1,0:T(8,128)(2,1)S(1)}, bf16[48,2176]{1,0:T(8,128)(2,1)S(1)}, u32[]{:S(2)}, u32[]{:S(2)}) collective-permute-start(bf16[48,2176]{1,0:T(8,128)(2,1)S(1)} %shard_map.97), channel_id=1, source_target_pairs={{4,0},{8,4},{12,8},{14,12},{10,14},{6,10},{2,6},{0,2},{5,1},{9,5},... | collective-permute-start | bytes 626696 | tf_op jit(solution)/shard_map/ppermute | solution.py:568
  104.1 8.6 %collective-permute-start.24 = (bf16[48,2176]{1,0:T(8,128)(2,1)S(1)}, bf16[48,2176]{1,0:T(8,128)(2,1)S(1)}, u32[]{:S(2)}, u32[]{:S(2)}) collective-permute-start(bf16[48,2176]{1,0:T(8,128)(2,1)S(1)} %shard_map.102), channel_id=1, source_target_pairs={{0,4},{4,8},{8,12},{12,14},{14,10},{10,6},{6,2},{2,0},{1,5},{5,9},... | collective-permute-start | bytes 626696 | tf_op jit(solution)/shard_map/ppermute | solution.py:568
  111.7 8.2 %collective-permute-start.19 = (bf16[48,2176]{1,0:T(8,128)(2,1)S(1)}, bf16[48,2176]{1,0:T(8,128)(2,1)S(1)}, u32[]{:S(2)}, u32[]{:S(2)}) collective-permute-start(bf16[48,2176]{1,0:T(8,128)(2,1)S(1)} %shard_map.98), channel_id=1, source_target_pairs={{4,0},{8,4},{12,8},{14,12},{10,14},{6,10},{2,6},{0,2},{5,1},{9,5},... | collective-permute-start | bytes 626696 | tf_op jit(solution)/shard_map/ppermute | solution.py:568
  112.7 8.2 %collective-permute-start.25 = (bf16[48,2176]{1,0:T(8,128)(2,1)S(1)}, bf16[48,2176]{1,0:T(8,128)(2,1)S(1)}, u32[]{:S(2)}, u32[]{:S(2)}) collective-permute-start(bf16[48,2176]{1,0:T(8,128)(2,1)S(1)} %shard_map.103), channel_id=1, source_target_pairs={{0,4},{4,8},{8,12},{12,14},{14,10},{10,6},{6,2},{2,0},{1,5},{5,9},... | collective-permute-start | bytes 626696 | tf_op jit(solution)/shard_map/ppermute | solution.py:568
  114.0 10.0 %collective-permute-start.22 = (bf16[80,2048]{1,0:T(8,128)(2,1)S(1)}, bf16[80,2048]{1,0:T(8,128)(2,1)S(1)}, u32[]{:S(2)}, u32[]{:S(2)}) collective-permute-start(bf16[80,2048]{1,0:T(8,128)(2,1)S(1)} %shard_map.101), channel_id=1, source_target_pairs={{4,0},{8,4},{12,8},{14,12},{10,14},{6,10},{2,6},{0,2},{5,1},{9,5},... | collective-permute-start | bytes 983048 | tf_op jit(solution)/shard_map/ppermute | solution.py:568
  115.0 9.3 %collective-permute-start.28 = (bf16[80,2048]{1,0:T(8,128)(2,1)S(1)}, bf16[80,2048]{1,0:T(8,128)(2,1)S(1)}, u32[]{:S(2)}, u32[]{:S(2)}) collective-permute-start(bf16[80,2048]{1,0:T(8,128)(2,1)S(1)} %shard_map.106), channel_id=1, source_target_pairs={{0,4},{4,8},{8,12},{12,14},{14,10},{10,6},{6,2},{2,0},{1,5},{5,9},... | collective-permute-start | bytes 983048 | tf_op jit(solution)/shard_map/ppermute | solution.py:568
  119.9 6.3 %collective-permute-start.20 = (bf16[48,2176]{1,0:T(8,128)(2,1)S(1)}, bf16[48,2176]{1,0:T(8,128)(2,1)S(1)}, u32[]{:S(2)}, u32[]{:S(2)}) collective-permute-start(bf16[48,2176]{1,0:T(8,128)(2,1)S(1)} %shard_map.99), channel_id=1, source_target_pairs={{4,0},{8,4},{12,8},{14,12},{10,14},{6,10},{2,6},{0,2},{5,1},{9,5},... | collective-permute-start | bytes 626696 | tf_op jit(solution)/shard_map/ppermute | solution.py:568
  120.9 5.9 %collective-permute-start.26 = (bf16[48,2176]{1,0:T(8,128)(2,1)S(1)}, bf16[48,2176]{1,0:T(8,128)(2,1)S(1)}, u32[]{:S(2)}, u32[]{:S(2)}) collective-permute-start(bf16[48,2176]{1,0:T(8,128)(2,1)S(1)} %shard_map.104), channel_id=1, source_target_pairs={{0,4},{4,8},{8,12},{12,14},{14,10},{10,6},{6,2},{2,0},{1,5},{5,9},... | collective-permute-start | bytes 626696 | tf_op jit(solution)/shard_map/ppermute | solution.py:568

commit v6 on v4

--- a/solution.py
+++ b/solution.py
@@ -591,7 +591,7 @@
     parts, last = call(last, ((cut, extra, 0),) * 2, *long)
     long_terms.append(parts[0::2])
     lower = parts[1::2]
-    parts, last = call(last, ((0, needed, extra),) * 2, *short, unrolled=True)
+    parts, last = call(last, ((0, needed, extra),) * 2, *short)
     short_back = send_back([joined(a, b) for a, b in zip(lower, parts[0::2])])
     carried = parts[1::2]
     parts, last = call(last, ((cut, 0, 0),) * 2, *long_last, unrolled=True)

time: 128 us -> 128 us (level)
    ppermute x7, starting transfers between devices: 12.7 us -> 8.97 us  [send_back(): lax.ppermute(pair[1], 'grp', ahead)]
    ppermute x7, starting transfers between devices: 2.37 us -> 5.84 us  [send_back(): lax.ppermute(pair[0], 'grp', behind)]
where the time goes in v6:
time: 128 us
  Pallas kernels  58.1 us (45%)
  waiting for transfers between devices  39.7 us (31%)
  starting transfers between devices  29.2 us (23%)
    pallas_call x6, Pallas kernels, experts_call(): pl.pallas_call(functools.partial(experts_kernel, len(given), plan, unroll...  43.9 us
    ppermute x6, waiting for transfers between devices, send(): lax.ppermute(pair[0], 'grp', ahead)  19.8 us
    ppermute x7, waiting for transfers between devices, send_back(): lax.ppermute(pair[0], 'grp', behind)  17.9 us
    ppermute x6, starting transfers between devices, send(): lax.ppermute(pair[0], 'grp', ahead)  11.9 us
    pallas_call x2, Pallas kernels, load(): pl.pallas_call(load_kernel, out_shape=(pltpu.VMEM((per_device, width, 2 *...  9.58 us
    ppermute x7, starting transfers between devices, send_back(): lax.ppermute(pair[1], 'grp', ahead)  8.97 us
    ppermute x7, starting transfers between devices, send_back(): lax.ppermute(pair[0], 'grp', behind)  5.84 us
    pallas_call x1, Pallas kernels, pack(): pl.pallas_call(functools.partial(pack_kernel, per_group), out_shape=(jax....  2.66 us
  transfers between devices with their start and end apart: 29, of which 11 were waited for; matrix products, arithmetic and copies ran while one was open for 0% of the time, Pallas kernels for 44%

profile of v6, /device:TPU:0, one launch (start us, length us, event | category | flops | bytes accessed | tf_op | source)
XLA Modules:
  0.0 128.2 jit_solution(18156570617029695998)
XLA Ops:
  0.6 0.5 collective-permute-start
  1.2 0.4 collective-permute-start.4
  1.7 2.7 %shard_map.86 = (bf16[128,4224]{1,0:T(8,128)(2,1)}, bf16[128,4224]{1,0:T(8,128)(2,1)S(1)}, bf16[128,128]{1,0:T(8,128)(2,1)S(1)}, bf16[128,128]{1,0:T(8,128)(2,1)S(1)}, bf16[128,128]{1,0:T(8,128)(2,1)S(1)}) custom-call(bf16[128,2048]{1,0:T(8,128)(2,1)} %refs_0_.1, bf16[128,2048]{1,0:T(8,128)(2,1)} %refs_1_.1, s32[8,128]{1,0:T(8,128)} %bitcast.5, ...), custom_call_target="tpu_custom_call" | custom-call | tf_op jit(solution)/shard_map/pallas_call | solution.py:287
  4.3 2.7 %collective-permute-start.1 = (bf16[128,4224]{1,0:T(8,128)(2,1)}, bf16[128,4224]{1,0:T(8,128)(2,1)S(1)}, u32[]{:S(2)}, u32[]{:S(2)}) collective-permute-start(bf16[128,4224]{1,0:T(8,128)(2,1)} %get-tuple-element.58), channel_id=1, source_target_pairs={{0,4},{4,8},{8,12},{12,14},{14,10},{10,6},{6,2},{2,0},{1,5},{5,9},... | collective-permute-start | bytes 3244040 | tf_op jit(solution)/shard_map/ppermute | solution.py:548
  7.1 4.7 %shard_map.87 = (bf16[2,2048,768]{2,1,0:T(8,128)(2,1)S(1)}, bf16[1536,2048]{1,0:T(8,128)(2,1)S(1)}, bf16[2048,768]{1,0:T(8,128)(2,1)S(1)}, f32[8,128]{1,0:T(8,128)S(1)}) custom-call(s32[2]{0:T(128)S(1)} %pad_add_fusion.after_this.place, bf16[2,2048,384]{2,1,0:T(8,128)(2,1)} %gate.1, bf16[2,2048,384]{2,1,0:T(8,128)(2,1)} %up.1, bf16[2,384,2048]{2,1,0:T(8,128)(2,1)} %down.1), custom_call_target="tpu_custom_call" | custom-call | flops 1 | bytes 25165824 | tf_op jit(solution)/shard_map/pallas_call | solution.py:342
  11.9 19.8 %collective-permute-done.1.refs_0_ = bf16[128,4224]{1,0:T(8,128)(2,1)S(1)} collective-permute-done((bf16[128,4224]{1,0:T(8,128)(2,1)}, bf16[128,4224]{1,0:T(8,128)(2,1)S(1)}, u32[]{:S(2)}, u32[]{:S(2)}) %collective-permute-start.1) | collective-permute-done | bytes 1081376 | tf_op jit(solution)/shard_map/ppermute | solution.py:548
  31.8 1.9 %collective-permute-start.5 = (bf16[64,4224]{1,0:T(8,128)(2,1)S(1)}, bf16[64,4224]{1,0:T(8,128)(2,1)S(1)}, u32[]{:S(2)}, u32[]{:S(2)}) collective-permute-start(bf16[64,4224]{1,0:T(8,128)(2,1)S(1)} %get-tuple-element.74), channel_id=1, source_target_pairs={{0,4},{4,8},{8,12},{12,14},{14,10},{10,6},{6,2},{2,0},{1,5},{5,9},... | collective-permute-start | bytes 1622024 | tf_op jit(solution)/shard_map/ppermute | solution.py:548
  33.7 0.3 collective-permute-start.7
  34.0 1.8 %collective-permute-start.6 = (bf16[64,4224]{1,0:T(8,128)(2,1)S(1)}, bf16[64,4224]{1,0:T(8,128)(2,1)S(1)}, u32[]{:S(2)}, u32[]{:S(2)}) collective-permute-start(bf16[64,4224]{1,0:T(8,128)(2,1)S(1)} %get-tuple-element.75), channel_id=1, source_target_pairs={{0,4},{4,8},{8,12},{12,14},{14,10},{10,6},{6,2},{2,0},{1,5},{5,9},... | collective-permute-start | bytes 1622024 | tf_op jit(solution)/shard_map/ppermute | solution.py:548
  35.8 0.2 collective-permute-start.8
  36.0 4.8 %shard_map.88 = (bf16[2,2048,768]{2,1,0:T(8,128)(2,1)S(1)}, bf16[1536,2048]{1,0:T(8,128)(2,1)S(1)}, bf16[2048,768]{1,0:T(8,128)(2,1)S(1)}, f32[8,128]{1,0:T(8,128)S(1)}) custom-call(f32[8,128]{1,0:T(8,128)S(1)} %get-tuple-element.57.after_this, bf16[2,2048,384]{2,1,0:T(8,128)(2,1)} %collective-permute-done.gate, ...), custom_call_target="tpu_custom_call" | custom-call | flops 1 | bytes 25165824 | tf_op jit(solution)/shard_map/pallas_call | solution.py:342
  40.9 6.2 %shard_map.89 = (bf16[128,2176]{1,0:T(8,128)(2,1)S(1)}, f32[8,128]{1,0:T(8,128)S(1)}) custom-call(s32[2]{0:T(128)S(1)} %pad_add_fusion.after_this.place, f32[8,128]{1,0:T(8,128)S(1)} %get-tuple-element.62.after_this, bf16[128,2048]{1,0:T(8,128)(2,1)S(1)} %copy-done.2, bf16[128,2048]{1,0:T(8,128)(2,1)S(1)} %copy-done.3, ...), custom_call_target="tpu_custom_call" | custom-call | flops 1 | bytes 1 | tf_op jit(solution)/shard_map/pallas_call | solution.py:449
  47.1 1.8 %collective-permute-start.9 = (bf16[64,4224]{1,0:T(8,128)(2,1)S(1)}, bf16[64,4224]{1,0:T(8,128)(2,1)S(1)}, u32[]{:S(2)}, u32[]{:S(2)}) collective-permute-start(bf16[64,4224]{1,0:T(8,128)(2,1)S(1)} %collective-permute-done.5.refs_0_), channel_id=1, source_target_pairs={{0,4},{4,8},{8,12},{12,14},{14,10},{10,6},{6,2},{2,0},{1,5},{5,9},... | collective-permute-start | bytes 1622024 | tf_op jit(solution)/shard_map/ppermute | solution.py:548
  48.8 0.1 collective-permute-done.7.refs_2_
  49.0 0.2 collective-permute-start.10
  49.2 10.1 %shard_map.90 = (bf16[48,2176]{1,0:T(8,128)(2,1)S(1)}, bf16[80,2048]{1,0:T(8,128)(2,1)S(1)}, bf16[48,2176]{1,0:T(8,128)(2,1)S(1)}, bf16[80,2048]{1,0:T(8,128)(2,1)S(1)}, f32[8,128]{1,0:T(8,128)S(1)}) custom-call(s32[2]{0:T(128)S(1)} %pad_add_fusion.after_this.place, f32[8,128]{1,0:T(8,128)S(1)} %get-tuple-element.71.after_this, ...), custom_call_target="tpu_custom_call" | custom-call | flops 1 | bytes 1 | tf_op jit(solution)/shard_map/pallas_call | solution.py:449
  59.3 1.9 %collective-permute-start.11 = (bf16[48,4224]{1,0:T(8,128)(2,1)S(1)}, bf16[48,4224]{1,0:T(8,128)(2,1)S(1)}, u32[]{:S(2)}, u32[]{:S(2)}) collective-permute-start(bf16[48,4224]{1,0:T(8,128)(2,1)S(1)} %slice.36), channel_id=1, source_target_pairs={{0,4},{4,8},{8,12},{12,14},{14,10},{10,6},{6,2},{2,0},{1,5},{5,9},... | collective-permute-start | bytes 1216520 | tf_op jit(solution)/shard_map/ppermute | solution.py:548
  61.2 0.3 collective-permute-start.12
  61.4 10.1 %shard_map.91 = (bf16[48,2176]{1,0:T(8,128)(2,1)S(1)}, bf16[80,2048]{1,0:T(8,128)(2,1)S(1)}, bf16[48,2176]{1,0:T(8,128)(2,1)S(1)}, bf16[80,2048]{1,0:T(8,128)(2,1)S(1)}, f32[8,128]{1,0:T(8,128)S(1)}) custom-call(s32[2]{0:T(128)S(1)} %pad_add_fusion.after_this.place, f32[8,128]{1,0:T(8,128)S(1)} %get-tuple-element.73.after_this, ...), custom_call_target="tpu_custom_call" | custom-call | flops 1 | bytes 1 | tf_op jit(solution)/shard_map/pallas_call | solution.py:449
  71.6 1.9 %collective-permute-start.13 = (bf16[48,4224]{1,0:T(8,128)(2,1)S(1)}, bf16[48,4224]{1,0:T(8,128)(2,1)S(1)}, u32[]{:S(2)}, u32[]{:S(2)}) collective-permute-start(bf16[48,4224]{1,0:T(8,128)(2,1)S(1)} %slice.38), channel_id=1, source_target_pairs={{0,4},{4,8},{8,12},{12,14},{14,10},{10,6},{6,2},{2,0},{1,5},{5,9},... | collective-permute-start | bytes 1216520 | tf_op jit(solution)/shard_map/ppermute | solution.py:548
  73.5 0.5 collective-permute-start.14
  74.0 5.9 %shard_map.92 = (bf16[48,2176]{1,0:T(8,128)(2,1)S(1)}, bf16[16,2048]{1,0:T(8,128)(2,1)S(1)}, bf16[48,2176]{1,0:T(8,128)(2,1)S(1)}, bf16[16,2048]{1,0:T(8,128)(2,1)S(1)}, f32[8,128]{1,0:T(8,128)S(1)}) custom-call(s32[2]{0:T(128)S(1)} %pad_add_fusion.after_this.place, f32[8,128]{1,0:T(8,128)S(1)} %get-tuple-element.79.after_this, ...), custom_call_target="tpu_custom_call" | custom-call | flops 1 | bytes 1 | tf_op jit(solution)/shard_map/pallas_call | solution.py:449
  79.9 1.0 collective-permute-done.12.refs_1_
  80.8 6.1 %shard_map.93 = (bf16[48,2048]{1,0:T(8,128)(2,1)S(1)}, bf16[48,128]{1,0:T(8,128)(2,1)S(1)}, bf16[48,2048]{1,0:T(8,128)(2,1)S(1)}, bf16[48,128]{1,0:T(8,128)(2,1)S(1)}, f32[8,128]{1,0:T(8,128)S(1)}) custom-call(s32[2]{0:T(128)S(1)} %pad_add_fusion.after_this.place, f32[8,128]{1,0:T(8,128)S(1)} %get-tuple-element.83.after_this, ...), custom_call_target="tpu_custom_call" | custom-call | flops 1 | bytes 1 | tf_op jit(solution)/shard_map/pallas_call | solution.py:449
  86.9 0.9 collective-permute-start.15
  87.8 1.3 collective-permute-start.16
  89.1 0.2 collective-permute-done.14.refs_1_
  89.3 5.7 %shard_map.94 = (bf16[48,2176]{1,0:T(8,128)(2,1)S(1)}, bf16[48,2176]{1,0:T(8,128)(2,1)S(1)}, f32[8,128]{1,0:T(8,128)}) custom-call(s32[2]{0:T(128)S(1)} %pad_add_fusion.after_this.place, f32[8,128]{1,0:T(8,128)S(1)} %get-tuple-element.86.after_this, bf16[48,4224]{1,0:T(8,128)(2,1)S(1)} %collective-permute-done.13.refs_0_, ...), custom_call_target="tpu_custom_call" | custom-call | flops 1 | bytes 1 | tf_op jit(solution)/shard_map/pallas_call | solution.py:449
  95.0 0.8 collective-permute-start.17
  95.8 1.2 collective-permute-start.23
  97.1 0.8 collective-permute-start.21
  98.0 1.3 %collective-permute-start.27 = (bf16[80,2048]{1,0:T(8,128)(2,1)S(1)}, bf16[80,2048]{1,0:T(8,128)(2,1)S(1)}, u32[]{:S(2)}, u32[]{:S(2)}) collective-permute-start(bf16[80,2048]{1,0:T(8,128)(2,1)S(1)} %shard_map.105), channel_id=1, source_target_pairs={{0,4},{4,8},{8,12},{12,14},{14,10},{10,6},{6,2},{2,0},{1,5},{5,9},... | collective-permute-start | bytes 983048 | tf_op jit(solution)/shard_map/ppermute | solution.py:551
  99.3 3.8 %collective-permute-done.17.b = bf16[48,2176]{1,0:T(8,128)(2,1)S(1)} collective-permute-done((bf16[48,2176]{1,0:T(8,128)(2,1)S(1)}, bf16[48,2176]{1,0:T(8,128)(2,1)S(1)}, u32[]{:S(2)}, u32[]{:S(2)}) %collective-permute-start.17) | collective-permute-done | bytes 208928 | tf_op jit(solution)/shard_map/ppermute | solution.py:551
  103.2 0.8 collective-permute-start.18
  104.1 1.3 %collective-permute-start.24 = (bf16[48,2176]{1,0:T(8,128)(2,1)S(1)}, bf16[48,2176]{1,0:T(8,128)(2,1)S(1)}, u32[]{:S(2)}, u32[]{:S(2)}) collective-permute-start(bf16[48,2176]{1,0:T(8,128)(2,1)S(1)} %shard_map.102), channel_id=1, source_target_pairs={{0,4},{4,8},{8,12},{12,14},{14,10},{10,6},{6,2},{2,0},{1,5},{5,9},... | collective-permute-start | bytes 626696 | tf_op jit(solution)/shard_map/ppermute | solution.py:551
  105.4 6.4 %collective-permute-done.18.b = bf16[48,2176]{1,0:T(8,128)(2,1)S(1)} collective-permute-done((bf16[48,2176]{1,0:T(8,128)(2,1)S(1)}, bf16[48,2176]{1,0:T(8,128)(2,1)S(1)}, u32[]{:S(2)}, u32[]{:S(2)}) %collective-permute-start.18) | collective-permute-done | bytes 208928 | tf_op jit(solution)/shard_map/ppermute | solution.py:551
  111.8 0.8 collective-permute-start.19
  112.7 1.3 %collective-permute-start.25 = (bf16[48,2176]{1,0:T(8,128)(2,1)S(1)}, bf16[48,2176]{1,0:T(8,128)(2,1)S(1)}, u32[]{:S(2)}, u32[]{:S(2)}) collective-permute-start(bf16[48,2176]{1,0:T(8,128)(2,1)S(1)} %shard_map.103), channel_id=1, source_target_pairs={{0,4},{4,8},{8,12},{12,14},{14,10},{10,6},{6,2},{2,0},{1,5},{5,9},... | collective-permute-start | bytes 626696 | tf_op jit(solution)/shard_map/ppermute | solution.py:551
  114.1 0.8 collective-permute-start.22
  115.0 1.3 %collective-permute-start.28 = (bf16[80,2048]{1,0:T(8,128)(2,1)S(1)}, bf16[80,2048]{1,0:T(8,128)(2,1)S(1)}, u32[]{:S(2)}, u32[]{:S(2)}) collective-permute-start(bf16[80,2048]{1,0:T(8,128)(2,1)S(1)} %shard_map.106), channel_id=1, source_target_pairs={{0,4},{4,8},{8,12},{12,14},{14,10},{10,6},{6,2},{2,0},{1,5},{5,9},... | collective-permute-start | bytes 983048 | tf_op jit(solution)/shard_map/ppermute | solution.py:551
  116.3 3.7 %collective-permute-done.19.b = bf16[48,2176]{1,0:T(8,128)(2,1)S(1)} collective-permute-done((bf16[48,2176]{1,0:T(8,128)(2,1)S(1)}, bf16[48,2176]{1,0:T(8,128)(2,1)S(1)}, u32[]{:S(2)}, u32[]{:S(2)}) %collective-permute-start.19) | collective-permute-done | bytes 208928 | tf_op jit(solution)/shard_map/ppermute | solution.py:551
  120.0 0.8 collective-permute-start.20
  120.9 1.3 %collective-permute-start.26 = (bf16[48,2176]{1,0:T(8,128)(2,1)S(1)}, bf16[48,2176]{1,0:T(8,128)(2,1)S(1)}, u32[]{:S(2)}, u32[]{:S(2)}) collective-permute-start(bf16[48,2176]{1,0:T(8,128)(2,1)S(1)} %shard_map.104), channel_id=1, source_target_pairs={{0,4},{4,8},{8,12},{12,14},{14,10},{10,6},{6,2},{2,0},{1,5},{5,9},... | collective-permute-start | bytes 626696 | tf_op jit(solution)/shard_map/ppermute | solution.py:551
  122.2 2.2 %collective-permute-done.22.short_up = bf16[80,2048]{1,0:T(8,128)(2,1)S(1)} collective-permute-done((bf16[80,2048]{1,0:T(8,128)(2,1)S(1)}, bf16[80,2048]{1,0:T(8,128)(2,1)S(1)}, u32[]{:S(2)}, u32[]{:S(2)}) %collective-permute-start.22) | collective-permute-done | bytes 327712 | tf_op jit(solution)/shard_map/ppermute | solution.py:551
  124.4 0.4 collective-permute-done.28.short_down
  124.7 1.9 %collective-permute-done.20.long_up = bf16[48,2176]{1,0:T(8,128)(2,1)S(1)} collective-permute-done((bf16[48,2176]{1,0:T(8,128)(2,1)S(1)}, bf16[48,2176]{1,0:T(8,128)(2,1)S(1)}, u32[]{:S(2)}, u32[]{:S(2)}) %collective-permute-start.20) | collective-permute-done | bytes 208928 | tf_op jit(solution)/shard_map/ppermute | solution.py:551
  126.6 0.4 collective-permute-done.26.long_down
  127.0 1.3 %shard_map.107 = (bf16[128,2048]{1,0:T(8,128)(2,1)}, bf16[8,128]{1,0:T(8,128)(2,1)}) custom-call(s32[8,128]{1,0:T(8,128)S(1)} %bitcast.6, bf16[128,128]{1,0:T(8,128)(2,1)S(1)} %get-tuple-element.55.order_up, bf16[128,128]{1,0:T(8,128)(2,1)S(1)} %get-tuple-element.56.order_down, bf16[128,2176]{1,0:T(8,128)(2,1)S(1)} %get-tuple-element.70.mine, ...), custom_call_target="tpu_custom_call" | custom-call | tf_op jit(solution)/shard_map/pallas_call | solution.py:484
  (49 shorter events, 1.2 us)
Async XLA Ops:
  0.6 31.1 %collective-permute-start = (bf16[2,2048,384]{2,1,0:T(8,128)(2,1)}, bf16[2,2048,384]{2,1,0:T(8,128)(2,1)}, u32[]{:S(2)}, u32[]{:S(2)}) collective-permute-start(bf16[2,2048,384]{2,1,0:T(8,128)(2,1)} %gate.1), channel_id=1, source_target_pairs={{0,1},{1,0},{2,3},{3,2},{4,5},{5,4},{6,7},{7,6},{8,9},{9,8},{10,11... | collective-permute-start | bytes 9437192 | tf_op jit(solution)/shard_map/ppermute | solution.py:557
  1.1 30.6 %collective-permute-start.3 = (bf16[2,2048,384]{2,1,0:T(8,128)(2,1)}, bf16[2,2048,384]{2,1,0:T(8,128)(2,1)}, u32[]{:S(2)}, u32[]{:S(2)}) collective-permute-start(bf16[2,2048,384]{2,1,0:T(8,128)(2,1)} %up.1), channel_id=1, source_target_pairs={{0,1},{1,0},{2,3},{3,2},{4,5},{5,4},{6,7},{7,6},{8,9},{9,8},{10,11... | collective-permute-start | bytes 9437192 | tf_op jit(solution)/shard_map/ppermute | solution.py:557
  1.2 30.5 %collective-permute-start.4 = (bf16[2,384,2048]{2,1,0:T(8,128)(2,1)}, bf16[2,384,2048]{2,1,0:T(8,128)(2,1)}, u32[]{:S(2)}, u32[]{:S(2)}) collective-permute-start(bf16[2,384,2048]{2,1,0:T(8,128)(2,1)} %down.1), channel_id=1, source_target_pairs={{0,1},{1,0},{2,3},{3,2},{4,5},{5,4},{6,7},{7,6},{8,9},{9,8},{10,11... | collective-permute-start | bytes 9437192 | tf_op jit(solution)/shard_map/ppermute | solution.py:557
  4.3 27.3 %collective-permute-start.1 = (bf16[128,4224]{1,0:T(8,128)(2,1)}, bf16[128,4224]{1,0:T(8,128)(2,1)S(1)}, u32[]{:S(2)}, u32[]{:S(2)}) collective-permute-start(bf16[128,4224]{1,0:T(8,128)(2,1)} %get-tuple-element.58), channel_id=1, source_target_pairs={{0,4},{4,8},{8,12},{12,14},{14,10},{10,6},{6,2},{2,0},{1,5},{5,9},... | collective-permute-start | bytes 3244040 | tf_op jit(solution)/shard_map/ppermute | solution.py:548
  7.1 26.5 %collective-permute-start.2 = (bf16[128,4224]{1,0:T(8,128)(2,1)S(1)}, bf16[128,4224]{1,0:T(8,128)(2,1)S(1)}, u32[]{:S(2)}, u32[]{:S(2)}) collective-permute-start(bf16[128,4224]{1,0:T(8,128)(2,1)S(1)} %get-tuple-element.59), channel_id=1, source_target_pairs={{4,0},{8,4},{12,8},{14,12},{10,14},{6,10},{2,6},{0,2},{5,1},{9,5},... | collective-permute-start | bytes 3244040 | tf_op jit(solution)/shard_map/ppermute | solution.py:548
  31.7 4.1 %copy-start = (bf16[128,4224]{1,0:T(8,128)(2,1)}, bf16[128,4224]{1,0:T(8,128)(2,1)S(1)}, u32[]{:S(2)}) copy-start(bf16[128,4224]{1,0:T(8,128)(2,1)S(1)} %collective-permute-done.1.refs_0_) | copy-start | bytes 3244036
  31.8 15.3 %collective-permute-start.5 = (bf16[64,4224]{1,0:T(8,128)(2,1)S(1)}, bf16[64,4224]{1,0:T(8,128)(2,1)S(1)}, u32[]{:S(2)}, u32[]{:S(2)}) collective-permute-start(bf16[64,4224]{1,0:T(8,128)(2,1)S(1)} %get-tuple-element.74), channel_id=1, source_target_pairs={{0,4},{4,8},{8,12},{12,14},{14,10},{10,6},{6,2},{2,0},{1,5},{5,9},... | collective-permute-start | bytes 1622024 | tf_op jit(solution)/shard_map/ppermute | solution.py:548
  33.7 15.3 %collective-permute-start.7 = (bf16[64,4224]{1,0:T(8,128)(2,1)S(1)}, bf16[64,4224]{1,0:T(8,128)(2,1)S(1)}, u32[]{:S(2)}, u32[]{:S(2)}) collective-permute-start(bf16[64,4224]{1,0:T(8,128)(2,1)S(1)} %get-tuple-element.76), channel_id=1, source_target_pairs={{4,0},{8,4},{12,8},{14,12},{10,14},{6,10},{2,6},{0,2},{5,1},{9,5},... | collective-permute-start | bytes 1622024 | tf_op jit(solution)/shard_map/ppermute | solution.py:548
  34.0 25.3 %collective-permute-start.6 = (bf16[64,4224]{1,0:T(8,128)(2,1)S(1)}, bf16[64,4224]{1,0:T(8,128)(2,1)S(1)}, u32[]{:S(2)}, u32[]{:S(2)}) collective-permute-start(bf16[64,4224]{1,0:T(8,128)(2,1)S(1)} %get-tuple-element.75), channel_id=1, source_target_pairs={{0,4},{4,8},{8,12},{12,14},{14,10},{10,6},{6,2},{2,0},{1,5},{5,9},... | collective-permute-start | bytes 1622024 | tf_op jit(solution)/shard_map/ppermute | solution.py:548
  35.8 5.1 %copy-start.2 = (bf16[128,2048]{1,0:T(8,128)(2,1)S(1)}, bf16[128,2048]{1,0:T(8,128)(2,1)}, u32[]{:S(2)}) copy-start(bf16[128,2048]{1,0:T(8,128)(2,1)} %refs_0_.1) | copy-start | bytes 1572868
  35.8 5.1 %copy-start.3 = (bf16[128,2048]{1,0:T(8,128)(2,1)S(1)}, bf16[128,2048]{1,0:T(8,128)(2,1)}, u32[]{:S(2)}) copy-start(bf16[128,2048]{1,0:T(8,128)(2,1)} %refs_1_.1) | copy-start | bytes 1572868
  35.8 25.4 %collective-permute-start.8 = (bf16[64,4224]{1,0:T(8,128)(2,1)S(1)}, bf16[64,4224]{1,0:T(8,128)(2,1)S(1)}, u32[]{:S(2)}, u32[]{:S(2)}) collective-permute-start(bf16[64,4224]{1,0:T(8,128)(2,1)S(1)} %get-tuple-element.77), channel_id=1, source_target_pairs={{4,0},{8,4},{12,8},{14,12},{10,14},{6,10},{2,6},{0,2},{5,1},{9,5},... | collective-permute-start | bytes 1622024 | tf_op jit(solution)/shard_map/ppermute | solution.py:548
  40.9 8.3 %copy-start.1 = (bf16[128,4224]{1,0:T(8,128)(2,1)S(1)}, bf16[128,4224]{1,0:T(8,128)(2,1)}, u32[]{:S(2)}) copy-start(bf16[128,4224]{1,0:T(8,128)(2,1)} %copy-done) | copy-start | bytes 3244036
  47.1 24.5 %collective-permute-start.9 = (bf16[64,4224]{1,0:T(8,128)(2,1)S(1)}, bf16[64,4224]{1,0:T(8,128)(2,1)S(1)}, u32[]{:S(2)}, u32[]{:S(2)}) collective-permute-start(bf16[64,4224]{1,0:T(8,128)(2,1)S(1)} %collective-permute-done.5.refs_0_), channel_id=1, source_target_pairs={{0,4},{4,8},{8,12},{12,14},{14,10},{10,6},{6,2},{2,0},{1,5},{5,9},... | collective-permute-start | bytes 1622024 | tf_op jit(solution)/shard_map/ppermute | solution.py:548
  49.0 24.5 %collective-permute-start.10 = (bf16[64,4224]{1,0:T(8,128)(2,1)S(1)}, bf16[64,4224]{1,0:T(8,128)(2,1)S(1)}, u32[]{:S(2)}, u32[]{:S(2)}) collective-permute-start(bf16[64,4224]{1,0:T(8,128)(2,1)S(1)} %collective-permute-done.7.refs_2_), channel_id=1, source_target_pairs={{4,0},{8,4},{12,8},{14,12},{10,14},{6,10},{2,6},{0,2},{5,1},{9,5},... | collective-permute-start | bytes 1622024 | tf_op jit(solution)/shard_map/ppermute | solution.py:548
  59.3 20.6 %collective-permute-start.11 = (bf16[48,4224]{1,0:T(8,128)(2,1)S(1)}, bf16[48,4224]{1,0:T(8,128)(2,1)S(1)}, u32[]{:S(2)}, u32[]{:S(2)}) collective-permute-start(bf16[48,4224]{1,0:T(8,128)(2,1)S(1)} %slice.36), channel_id=1, source_target_pairs={{0,4},{4,8},{8,12},{12,14},{14,10},{10,6},{6,2},{2,0},{1,5},{5,9},... | collective-permute-start | bytes 1216520 | tf_op jit(solution)/shard_map/ppermute | solution.py:548
  61.2 19.6 %collective-permute-start.12 = (bf16[48,4224]{1,0:T(8,128)(2,1)S(1)}, bf16[48,4224]{1,0:T(8,128)(2,1)S(1)}, u32[]{:S(2)}, u32[]{:S(2)}) collective-permute-start(bf16[48,4224]{1,0:T(8,128)(2,1)S(1)} %slice.37), channel_id=1, source_target_pairs={{4,0},{8,4},{12,8},{14,12},{10,14},{6,10},{2,6},{0,2},{5,1},{9,5},... | collective-permute-start | bytes 1216520 | tf_op jit(solution)/shard_map/ppermute | solution.py:548
  71.6 17.5 %collective-permute-start.13 = (bf16[48,4224]{1,0:T(8,128)(2,1)S(1)}, bf16[48,4224]{1,0:T(8,128)(2,1)S(1)}, u32[]{:S(2)}, u32[]{:S(2)}) collective-permute-start(bf16[48,4224]{1,0:T(8,128)(2,1)S(1)} %slice.38), channel_id=1, source_target_pairs={{0,4},{4,8},{8,12},{12,14},{14,10},{10,6},{6,2},{2,0},{1,5},{5,9},... | collective-permute-start | bytes 1216520 | tf_op jit(solution)/shard_map/ppermute | solution.py:548
  73.5 15.8 %collective-permute-start.14 = (bf16[48,4224]{1,0:T(8,128)(2,1)S(1)}, bf16[48,4224]{1,0:T(8,128)(2,1)S(1)}, u32[]{:S(2)}, u32[]{:S(2)}) collective-permute-start(bf16[48,4224]{1,0:T(8,128)(2,1)S(1)} %slice.39), channel_id=1, source_target_pairs={{4,0},{8,4},{12,8},{14,12},{10,14},{6,10},{2,6},{0,2},{5,1},{9,5},... | collective-permute-start | bytes 1216520 | tf_op jit(solution)/shard_map/ppermute | solution.py:548
  86.9 8.1 %collective-permute-start.15 = (bf16[64,2048]{1,0:T(8,128)(2,1)S(1)}, bf16[64,2048]{1,0:T(8,128)(2,1)S(1)}, u32[]{:S(2)}, u32[]{:S(2)}) collective-permute-start(bf16[64,2048]{1,0:T(8,128)(2,1)S(1)} %shard_map.95), channel_id=1, source_target_pairs={{4,0},{8,4},{12,8},{14,12},{10,14},{6,10},{2,6},{0,2},{5,1},{9,5},... | collective-permute-start | bytes 786440 | tf_op jit(solution)/shard_map/ppermute | solution.py:551
  87.8 7.2 %collective-permute-start.16 = (bf16[64,2048]{1,0:T(8,128)(2,1)S(1)}, bf16[64,2048]{1,0:T(8,128)(2,1)S(1)}, u32[]{:S(2)}, u32[]{:S(2)}) collective-permute-start(bf16[64,2048]{1,0:T(8,128)(2,1)S(1)} %shard_map.96), channel_id=1, source_target_pairs={{0,4},{4,8},{8,12},{12,14},{14,10},{10,6},{6,2},{2,0},{1,5},{5,9},... | collective-permute-start | bytes 786440 | tf_op jit(solution)/shard_map/ppermute | solution.py:551
  95.0 8.1 %collective-permute-start.17 = (bf16[48,2176]{1,0:T(8,128)(2,1)S(1)}, bf16[48,2176]{1,0:T(8,128)(2,1)S(1)}, u32[]{:S(2)}, u32[]{:S(2)}) collective-permute-start(bf16[48,2176]{1,0:T(8,128)(2,1)S(1)} %get-tuple-element.94), channel_id=1, source_target_pairs={{4,0},{8,4},{12,8},{14,12},{10,14},{6,10},{2,6},{0,2},{5,1},{9,5},... | collective-permute-start | bytes 626696 | tf_op jit(solution)/shard_map/ppermute | solution.py:551
  95.8 8.2 %collective-permute-start.23 = (bf16[48,2176]{1,0:T(8,128)(2,1)S(1)}, bf16[48,2176]{1,0:T(8,128)(2,1)S(1)}, u32[]{:S(2)}, u32[]{:S(2)}) collective-permute-start(bf16[48,2176]{1,0:T(8,128)(2,1)S(1)} %get-tuple-element.102), channel_id=1, source_target_pairs={{0,4},{4,8},{8,12},{12,14},{14,10},{10,6},{6,2},{2,0},{1,5},{5,9},... | collective-permute-start | bytes 626696 | tf_op jit(solution)/shard_map/ppermute | solution.py:551
  97.1 16.9 %collective-permute-start.21 = (bf16[80,2048]{1,0:T(8,128)(2,1)S(1)}, bf16[80,2048]{1,0:T(8,128)(2,1)S(1)}, u32[]{:S(2)}, u32[]{:S(2)}) collective-permute-start(bf16[80,2048]{1,0:T(8,128)(2,1)S(1)} %shard_map.100), channel_id=1, source_target_pairs={{4,0},{8,4},{12,8},{14,12},{10,14},{6,10},{2,6},{0,2},{5,1},{9,5},... | collective-permute-start | bytes 983048 | tf_op jit(solution)/shard_map/ppermute | solution.py:551
  97.9 29.0 %copy-start.4 = (s32[128,8]{0,1:T(8,128)S(1)}, s32[128,8]{0,1:T(8,128)}, u32[]{:S(2)}) copy-start(s32[128,8]{0,1:T(8,128)} %param.9) | copy-start | bytes 12292
  98.0 16.9 %collective-permute-start.27 = (bf16[80,2048]{1,0:T(8,128)(2,1)S(1)}, bf16[80,2048]{1,0:T(8,128)(2,1)S(1)}, u32[]{:S(2)}, u32[]{:S(2)}) collective-permute-start(bf16[80,2048]{1,0:T(8,128)(2,1)S(1)} %shard_map.105), channel_id=1, source_target_pairs={{0,4},{4,8},{8,12},{12,14},{14,10},{10,6},{6,2},{2,0},{1,5},{5,9},... | collective-permute-start | bytes 983048 | tf_op jit(solution)/shard_map/ppermute | solution.py:551
  103.2 8.6 %collective-permute-start.18 = (bf16[48,2176]{1,0:T(8,128)(2,1)S(1)}, bf16[48,2176]{1,0:T(8,128)(2,1)S(1)}, u32[]{:S(2)}, u32[]{:S(2)}) collective-permute-start(bf16[48,2176]{1,0:T(8,128)(2,1)S(1)} %shard_map.97), channel_id=1, source_target_pairs={{4,0},{8,4},{12,8},{14,12},{10,14},{6,10},{2,6},{0,2},{5,1},{9,5},... | collective-permute-start | bytes 626696 | tf_op jit(solution)/shard_map/ppermute | solution.py:551
  104.1 8.6 %collective-permute-start.24 = (bf16[48,2176]{1,0:T(8,128)(2,1)S(1)}, bf16[48,2176]{1,0:T(8,128)(2,1)S(1)}, u32[]{:S(2)}, u32[]{:S(2)}) collective-permute-start(bf16[48,2176]{1,0:T(8,128)(2,1)S(1)} %shard_map.102), channel_id=1, source_target_pairs={{0,4},{4,8},{8,12},{12,14},{14,10},{10,6},{6,2},{2,0},{1,5},{5,9},... | collective-permute-start | bytes 626696 | tf_op jit(solution)/shard_map/ppermute | solution.py:551
  111.8 8.2 %collective-permute-start.19 = (bf16[48,2176]{1,0:T(8,128)(2,1)S(1)}, bf16[48,2176]{1,0:T(8,128)(2,1)S(1)}, u32[]{:S(2)}, u32[]{:S(2)}) collective-permute-start(bf16[48,2176]{1,0:T(8,128)(2,1)S(1)} %shard_map.98), channel_id=1, source_target_pairs={{4,0},{8,4},{12,8},{14,12},{10,14},{6,10},{2,6},{0,2},{5,1},{9,5},... | collective-permute-start | bytes 626696 | tf_op jit(solution)/shard_map/ppermute | solution.py:551
  112.7 8.2 %collective-permute-start.25 = (bf16[48,2176]{1,0:T(8,128)(2,1)S(1)}, bf16[48,2176]{1,0:T(8,128)(2,1)S(1)}, u32[]{:S(2)}, u32[]{:S(2)}) collective-permute-start(bf16[48,2176]{1,0:T(8,128)(2,1)S(1)} %shard_map.103), channel_id=1, source_target_pairs={{0,4},{4,8},{8,12},{12,14},{14,10},{10,6},{6,2},{2,0},{1,5},{5,9},... | collective-permute-start | bytes 626696 | tf_op jit(solution)/shard_map/ppermute | solution.py:551
  114.1 10.3 %collective-permute-start.22 = (bf16[80,2048]{1,0:T(8,128)(2,1)S(1)}, bf16[80,2048]{1,0:T(8,128)(2,1)S(1)}, u32[]{:S(2)}, u32[]{:S(2)}) collective-permute-start(bf16[80,2048]{1,0:T(8,128)(2,1)S(1)} %shard_map.101), channel_id=1, source_target_pairs={{4,0},{8,4},{12,8},{14,12},{10,14},{6,10},{2,6},{0,2},{5,1},{9,5},... | collective-permute-start | bytes 983048 | tf_op jit(solution)/shard_map/ppermute | solution.py:551
  115.0 9.7 %collective-permute-start.28 = (bf16[80,2048]{1,0:T(8,128)(2,1)S(1)}, bf16[80,2048]{1,0:T(8,128)(2,1)S(1)}, u32[]{:S(2)}, u32[]{:S(2)}) collective-permute-start(bf16[80,2048]{1,0:T(8,128)(2,1)S(1)} %shard_map.106), channel_id=1, source_target_pairs={{0,4},{4,8},{8,12},{12,14},{14,10},{10,6},{6,2},{2,0},{1,5},{5,9},... | collective-permute-start | bytes 983048 | tf_op jit(solution)/shard_map/ppermute | solution.py:551
  120.0 6.6 %collective-permute-start.20 = (bf16[48,2176]{1,0:T(8,128)(2,1)S(1)}, bf16[48,2176]{1,0:T(8,128)(2,1)S(1)}, u32[]{:S(2)}, u32[]{:S(2)}) collective-permute-start(bf16[48,2176]{1,0:T(8,128)(2,1)S(1)} %shard_map.99), channel_id=1, source_target_pairs={{4,0},{8,4},{12,8},{14,12},{10,14},{6,10},{2,6},{0,2},{5,1},{9,5},... | collective-permute-start | bytes 626696 | tf_op jit(solution)/shard_map/ppermute | solution.py:551
  120.9 6.1 %collective-permute-start.26 = (bf16[48,2176]{1,0:T(8,128)(2,1)S(1)}, bf16[48,2176]{1,0:T(8,128)(2,1)S(1)}, u32[]{:S(2)}, u32[]{:S(2)}) collective-permute-start(bf16[48,2176]{1,0:T(8,128)(2,1)S(1)} %shard_map.104), channel_id=1, source_target_pairs={{0,4},{4,8},{8,12},{12,14},{14,10},{10,6},{6,2},{2,0},{1,5},{5,9},... | collective-permute-start | bytes 626696 | tf_op jit(solution)/shard_map/ppermute | solution.py:551
